TPU v7x, 32 devices: a whole 2x2x4 slice. The times are simulated.
32 devices in a mesh: fsdp: 4 (over y, core), ctx: 4 (over z), tp: 2 (over x).
Axes of the slice: x: 2, y: 2, z: 4, core: 2. Of those that a mesh axis runs over, the one named last changes fastest.
Arguments:
- tokens: bfloat16 [4, 2048, 1024], P('fsdp', 'ctx'), may hold values from -6 to 6
- lengths: int32 [4, 6], P('fsdp'), may hold values from 1 to 1536, as said below
- query_weight: bfloat16 [1024, 1024], P('fsdp', 'tp'), may hold values from -0.1875 to 0.1875
- key_weight: bfloat16 [1024, 512], P('fsdp', 'tp'), may hold values from -0.1875 to 0.1875
- value_weight: bfloat16 [1024, 512], P('fsdp', 'tp'), may hold values from -0.1875 to 0.1875
- out_weight: bfloat16 [1024, 1024], P('tp', 'fsdp'), may hold values from -0.75 to 0.75
- gate_weight: bfloat16 [1024, 4608], P('fsdp', 'tp'), may hold values from -0.1875 to 0.1875
- up_weight: bfloat16 [1024, 4608], P('fsdp', 'tp'), may hold values from -0.1875 to 0.1875
- down_weight: bfloat16 [4608, 1024], P('tp', 'fsdp'), may hold values from -0.09375 to 0.09375
- attn_gain: float32 [1024], replicated, may hold values from 0.5 to 1.5
- ffn_gain: float32 [1024], replicated, may hold values from 0.5 to 1.5
- query_gain: float32 [64], replicated, may hold values from 0.5 to 1.5
- key_gain: float32 [64], replicated, may hold values from 0.5 to 1.5
- out_grad: bfloat16 [4, 2048, 1024], P('fsdp', 'ctx'), may hold values from -6 to 6
Outputs:
- mixed: bfloat16 [4, 2048, 1024], P('fsdp', 'ctx')
- tokens_grad: float32 [4, 2048, 1024], P('fsdp', 'ctx')
- grad_query: float32 [1024, 1024], P('fsdp', 'tp')
- grad_key: float32 [1024, 512], P('fsdp', 'tp')
- grad_value: float32 [1024, 512], P('fsdp', 'tp')
- grad_out: float32 [1024, 1024], P('tp', 'fsdp')
- grad_gate: float32 [1024, 4608], P('fsdp', 'tp')
- grad_up: float32 [1024, 4608], P('fsdp', 'tp')
- grad_down: float32 [4608, 1024], P('tp', 'fsdp')
- grad_attn_gain: float32 [1024], replicated
- grad_ffn_gain: float32 [1024], replicated
- grad_query_gain: float32 [64], replicated
- grad_key_gain: float32 [64], replicated
Inputs may be any that keep to these rules, and one draw needn't show every extreme that they name: `lengths`: each row sums to 2048; in each row the longest sequence has exactly 1536 tokens.
All inputs are finite; a program needn't handle non-finite values.
Results may differ from a plain program's by a relative error of at most 0.019.
Values may be sent and summed in bfloat16 or wider, within the bound.
A program may use at most 192 MiB of HBM per device.

v0:
```python
import jax
import jax.numpy as jnp
from jax import lax
from jax.sharding import PartitionSpec as P

HD = 64


EPSILON = 1e-05
ROPE_BASE = 1000000.0


def rms_norm(values, gain_vec):
    return (
        values * lax.rsqrt(jnp.mean(values * values, axis=-1, keepdims=True) + EPSILON) * gain_vec
    )


def rotate(values, rope_pos):
    half_dim = HD // 2
    frequency = ROPE_BASE ** (-2.0 * jnp.arange(half_dim, dtype=jnp.float32) / HD)
    angles = rope_pos[..., None, None] * frequency
    cosine = jnp.cos(angles)
    sine_part = jnp.sin(angles)
    lower_half = values[..., :half_dim]
    upper_half = values[..., half_dim:]
    return jnp.concatenate(
        [
            lower_half * cosine - upper_half * sine_part,
            upper_half * cosine + lower_half * sine_part,
        ],
        axis=-1,
    )


def head_prep(projected, gain_vec, rope_pos):
    shaped = projected.reshape(projected.shape[:-1] + (-1, HD))
    return rotate(rms_norm(shaped, gain_vec), rope_pos)


def round_trip(values):
    return lax.optimization_barrier(values.astype(jnp.bfloat16)).astype(jnp.float32)


def to_items(stacked):
    moved = jnp.moveaxis(stacked, 2, 1)
    return moved.reshape((-1,) + moved.shape[2:])


def from_items(stacked, pack_count):
    shaped = stacked.reshape((pack_count, -1) + stacked.shape[1:])
    return jnp.moveaxis(shaped, 1, 2)


def masked_scores(query_item, key_item, start_item, place_item):
    scores = jnp.einsum(
        "sgd,td->gst", query_item, key_item, preferred_element_type=jnp.float32
    ) * HD ** (-0.5)
    key_place = jnp.arange(key_item.shape[0], dtype=jnp.int32)
    visible = (key_place[None, :] >= start_item[:, None]) & (
        key_place[None, :] <= place_item[:, None]
    )
    return jnp.where(visible[None], scores, -1e30)


def attend_item(packed):
    query_item, key_item, value_item, start_item, place_item = packed
    scores = masked_scores(query_item, key_item, start_item, place_item)
    row_max = jnp.max(scores, axis=-1, keepdims=True)
    exponent = jnp.exp(scores - row_max)
    row_total = jnp.sum(exponent, axis=-1, keepdims=True)
    weights_soft = (exponent / row_total).astype(jnp.bfloat16)
    attended = jnp.einsum(
        "gst,td->sgd", weights_soft, value_item, preferred_element_type=jnp.float32
    )
    return (attended, row_max[..., 0] + jnp.log(row_total[..., 0]))


def attend_back(packed):
    query_item, key_item, value_item, start_item, place_item, log_total, grad_item = packed
    scores = masked_scores(query_item, key_item, start_item, place_item)
    weights_soft = jnp.exp(scores - log_total[..., None])
    grad_soft = jnp.einsum("sgd,td->gst", grad_item, value_item, preferred_element_type=jnp.float32)
    grad_scores = (
        weights_soft * (grad_soft - jnp.sum(weights_soft * grad_soft, axis=-1, keepdims=True))
    ).astype(jnp.bfloat16)
    score_scale = HD ** (-0.5)
    grad_query = (
        jnp.einsum("gst,td->sgd", grad_scores, key_item, preferred_element_type=jnp.float32)
        * score_scale
    )
    grad_key = (
        jnp.einsum("gst,sgd->td", grad_scores, query_item, preferred_element_type=jnp.float32)
        * score_scale
    )
    grad_value = jnp.einsum(
        "gst,sgd->td",
        weights_soft.astype(jnp.bfloat16),
        grad_item,
        preferred_element_type=jnp.float32,
    )
    return (grad_query, grad_key, grad_value)


def shards(
    tokens,
    lengths,
    query_weight,
    key_weight,
    value_weight,
    out_weight,
    gate_weight,
    up_weight,
    down_weight,
    attn_gain,
    ffn_gain,
    query_gain,
    key_gain,
    out_grad,
):
    pack_count = tokens.shape[0]
    tok_rows = tokens.shape[1]
    pack_len = tok_rows * lax.axis_size("ctx")
    offset = lax.axis_index("ctx") * tok_rows
    group_count = key_weight.shape[1] // HD
    head_count = query_weight.shape[1] // HD
    per_group = head_count // group_count
    full_query, full_key, full_value, full_out, full_gate, full_up, full_down = (
        lax.all_gather(query_weight, "fsdp", axis=0, tiled=True),
        lax.all_gather(key_weight, "fsdp", axis=0, tiled=True),
        lax.all_gather(value_weight, "fsdp", axis=0, tiled=True),
        lax.all_gather(out_weight, "fsdp", axis=1, tiled=True),
        lax.all_gather(gate_weight, "fsdp", axis=0, tiled=True),
        lax.all_gather(up_weight, "fsdp", axis=0, tiled=True),
        lax.all_gather(down_weight, "fsdp", axis=1, tiled=True),
    )
    seq_ends = jnp.cumsum(lengths, axis=1)
    positions = jnp.arange(pack_len, dtype=jnp.int32)
    passed = (positions[None, :, None] >= seq_ends[:, None, :]).astype(jnp.int32)
    seq_start = jnp.sum(passed * lengths[:, None, :], axis=2)
    local_place = offset + jnp.arange(tok_rows, dtype=jnp.int32)
    local_start = lax.dynamic_slice_in_dim(seq_start, offset, tok_rows, 1)
    rope_pos = (local_place[None, :] - local_start).astype(jnp.float32)
    inputs = tokens.astype(jnp.float32)
    normed = rms_norm(inputs, attn_gain).astype(jnp.bfloat16)
    query_proj = jnp.dot(normed, full_query, preferred_element_type=jnp.float32)
    key_proj = jnp.dot(normed, full_key, preferred_element_type=jnp.float32)
    value_low = jnp.dot(normed, full_value, preferred_element_type=jnp.float32).astype(jnp.bfloat16)
    queries, query_pull = jax.vjp(
        lambda projected, gain_vec: head_prep(projected, gain_vec, rope_pos), query_proj, query_gain
    )
    keys_rot, key_pull = jax.vjp(
        lambda projected, gain_vec: head_prep(projected, gain_vec, rope_pos), key_proj, key_gain
    )
    queries = queries.astype(jnp.bfloat16)
    keys_rot = keys_rot.astype(jnp.bfloat16)
    value_heads = value_low.reshape(pack_count, tok_rows, group_count, HD)
    all_keys, all_values = (
        lax.all_gather(keys_rot, "ctx", axis=1, tiled=True),
        lax.all_gather(value_heads, "ctx", axis=1, tiled=True),
    )
    query_items = to_items(queries.reshape(pack_count, tok_rows, group_count, per_group, HD))
    key_items = to_items(all_keys)
    value_items = to_items(all_values)
    start_items = jnp.repeat(local_start, group_count, axis=0)
    place_items = jnp.broadcast_to(local_place, (pack_count * group_count, tok_rows))
    attended, log_total = lax.map(
        attend_item, (query_items, key_items, value_items, start_items, place_items)
    )
    attended = (
        from_items(attended, pack_count)
        .reshape(pack_count, tok_rows, head_count * HD)
        .astype(jnp.bfloat16)
    )
    attn_part = jnp.dot(attended, full_out, preferred_element_type=jnp.float32)
    after_attn = inputs + lax.psum(attn_part, "tp")
    normed_ffn = rms_norm(after_attn, ffn_gain).astype(jnp.bfloat16)
    gate_proj = jnp.dot(normed_ffn, full_gate, preferred_element_type=jnp.float32)
    up_proj = jnp.dot(normed_ffn, full_up, preferred_element_type=jnp.float32)
    hidden, swiglu_pull = jax.vjp(
        lambda gate_in, up_in: jax.nn.silu(gate_in) * up_in, gate_proj, up_proj
    )
    hidden = hidden.astype(jnp.bfloat16)
    ffn_out = lax.psum(
        jnp.dot(hidden, full_down, preferred_element_type=jnp.float32).astype(jnp.bfloat16), "tp"
    ).astype(jnp.float32)
    mixed = (after_attn + ffn_out).astype(jnp.bfloat16)
    grad_down = jnp.einsum("psf,psd->fd", hidden, out_grad, preferred_element_type=jnp.float32)
    grad_hidden = jnp.einsum("psd,fd->psf", out_grad, full_down, preferred_element_type=jnp.float32)
    grad_gate_proj, grad_up_proj = swiglu_pull(grad_hidden)
    grad_gate_proj = grad_gate_proj.astype(jnp.bfloat16)
    grad_up_proj = grad_up_proj.astype(jnp.bfloat16)
    grad_gate = jnp.einsum(
        "psd,psf->df", normed_ffn, grad_gate_proj, preferred_element_type=jnp.float32
    )
    grad_up = jnp.einsum(
        "psd,psf->df", normed_ffn, grad_up_proj, preferred_element_type=jnp.float32
    )
    grad_normed_ffn = jnp.einsum(
        "psf,df->psd", grad_gate_proj, full_gate, preferred_element_type=jnp.float32
    )
    grad_normed_ffn = grad_normed_ffn + jnp.einsum(
        "psf,df->psd", grad_up_proj, full_up, preferred_element_type=jnp.float32
    )
    unused_ffn, ffn_pull = jax.vjp(rms_norm, after_attn, ffn_gain)
    grad_after_part, grad_ffn_gain = ffn_pull(grad_normed_ffn)
    grad_after = out_grad.astype(jnp.float32) + lax.psum(grad_after_part, "tp")
    grad_after_low = grad_after.astype(jnp.bfloat16)
    grad_out = jnp.einsum(
        "psh,psd->hd", attended, grad_after_low, preferred_element_type=jnp.float32
    )
    grad_attended = jnp.einsum(
        "psd,hd->psh", grad_after_low, full_out, preferred_element_type=jnp.float32
    ).astype(jnp.bfloat16)
    grad_items = to_items(grad_attended.reshape(pack_count, tok_rows, group_count, per_group, HD))
    grad_q_items, grad_k_items, grad_v_items = lax.map(
        attend_back,
        (query_items, key_items, value_items, start_items, place_items, log_total, grad_items),
    )
    grad_keys_all = from_items(grad_k_items, pack_count)
    grad_values_all = from_items(grad_v_items, pack_count)
    grad_keys_rot, grad_value_heads = (
        lax.psum_scatter(
            grad_keys_all.astype(jnp.bfloat16), "ctx", scatter_dimension=1, tiled=True
        ).astype(jnp.float32),
        lax.psum_scatter(
            grad_values_all.astype(jnp.bfloat16), "ctx", scatter_dimension=1, tiled=True
        ).astype(jnp.float32),
    )
    grad_queries = from_items(grad_q_items, pack_count).reshape(
        pack_count, tok_rows, head_count, HD
    )
    grad_query_proj, grad_query_gain = query_pull(round_trip(grad_queries))
    grad_key_proj, grad_key_gain = key_pull(round_trip(grad_keys_rot))
    grad_query_low = grad_query_proj.astype(jnp.bfloat16)
    grad_key_low = grad_key_proj.astype(jnp.bfloat16)
    grad_value_low = grad_value_heads.reshape(pack_count, tok_rows, group_count * HD).astype(
        jnp.bfloat16
    )
    grad_query = jnp.einsum(
        "psd,psh->dh", normed, grad_query_low, preferred_element_type=jnp.float32
    )
    grad_key = jnp.einsum("psd,psh->dh", normed, grad_key_low, preferred_element_type=jnp.float32)
    grad_value = jnp.einsum(
        "psd,psh->dh", normed, grad_value_low, preferred_element_type=jnp.float32
    )
    grad_normed = jnp.einsum(
        "psh,dh->psd", grad_query_low, full_query, preferred_element_type=jnp.float32
    )
    grad_normed = grad_normed + jnp.einsum(
        "psh,dh->psd", grad_key_low, full_key, preferred_element_type=jnp.float32
    )
    grad_normed = grad_normed + jnp.einsum(
        "psh,dh->psd", grad_value_low, full_value, preferred_element_type=jnp.float32
    )
    unused_attn, attn_pull = jax.vjp(rms_norm, inputs, attn_gain)
    grad_input_part, grad_attn_gain = attn_pull(grad_normed)
    tokens_grad = grad_after + lax.psum(grad_input_part.astype(jnp.bfloat16), "tp").astype(
        jnp.float32
    )
    weight_grads = (grad_query, grad_key, grad_value, grad_out, grad_gate, grad_up, grad_down)
    shares = (
        lax.psum_scatter(
            weight_grads[0].astype(jnp.bfloat16), "fsdp", scatter_dimension=0, tiled=True
        ).astype(jnp.float32),
        lax.psum_scatter(
            weight_grads[1].astype(jnp.bfloat16), "fsdp", scatter_dimension=0, tiled=True
        ).astype(jnp.float32),
        lax.psum_scatter(
            weight_grads[2].astype(jnp.bfloat16), "fsdp", scatter_dimension=0, tiled=True
        ).astype(jnp.float32),
        lax.psum_scatter(
            weight_grads[3].astype(jnp.bfloat16), "fsdp", scatter_dimension=1, tiled=True
        ).astype(jnp.float32),
        lax.psum_scatter(
            weight_grads[4].astype(jnp.bfloat16), "fsdp", scatter_dimension=0, tiled=True
        ).astype(jnp.float32),
        lax.psum_scatter(
            weight_grads[5].astype(jnp.bfloat16), "fsdp", scatter_dimension=0, tiled=True
        ).astype(jnp.float32),
        lax.psum_scatter(
            weight_grads[6].astype(jnp.bfloat16), "fsdp", scatter_dimension=1, tiled=True
        ).astype(jnp.float32),
    )
    shares = (
        lax.psum(shares[0].astype(jnp.bfloat16), "ctx").astype(jnp.float32),
        lax.psum(shares[1].astype(jnp.bfloat16), "ctx").astype(jnp.float32),
        lax.psum(shares[2].astype(jnp.bfloat16), "ctx").astype(jnp.float32),
        lax.psum(shares[3].astype(jnp.bfloat16), "ctx").astype(jnp.float32),
        lax.psum(shares[4].astype(jnp.bfloat16), "ctx").astype(jnp.float32),
        lax.psum(shares[5].astype(jnp.bfloat16), "ctx").astype(jnp.float32),
        lax.psum(shares[6].astype(jnp.bfloat16), "ctx").astype(jnp.float32),
    )
    gain_sums = lax.psum(
        (grad_attn_gain, grad_ffn_gain, grad_query_gain, grad_key_gain), ("fsdp", "ctx", "tp")
    )
    return (
        mixed,
        tokens_grad,
        shares[0],
        shares[1],
        shares[2],
        shares[3],
        shares[4],
        shares[5],
        shares[6],
        gain_sums[0],
        gain_sums[1],
        gain_sums[2],
        gain_sums[3],
    )


def solution(mesh):
    in_specs = (
        P("fsdp", "ctx", None),
        P("fsdp", None),
        P("fsdp", "tp"),
        P("fsdp", "tp"),
        P("fsdp", "tp"),
        P("tp", "fsdp"),
        P("fsdp", "tp"),
        P("fsdp", "tp"),
        P("tp", "fsdp"),
        P(),
        P(),
        P(),
        P(),
        P("fsdp", "ctx", None),
    )
    out_specs = (
        P("fsdp", "ctx", None),
        P("fsdp", "ctx", None),
        P("fsdp", "tp"),
        P("fsdp", "tp"),
        P("fsdp", "tp"),
        P("tp", "fsdp"),
        P("fsdp", "tp"),
        P("fsdp", "tp"),
        P("tp", "fsdp"),
        P(),
        P(),
        P(),
        P(),
    )
    return jax.shard_map(shards, mesh=mesh, in_specs=in_specs, out_specs=out_specs, check_vma=False)
```

profile of v0, /device:TPU:0, one launch (start us, length us, event | category | flops | bytes accessed | tf_op | source)
XLA Modules:
  0.0 1032.4 jit_solution(6657470009052060460)
XLA Ops:
  9.5 9.0 all_gather.27
  22.2 9.0 all_gather.29
  39.0 21.6 %all-gather.8.cloned.1.call-done = bf16[1,2048,4,64]{1,3,2,0:T(8,128)(2,1)} async-done(((bf16[1,512,4,64]{1,3,2,0:T(8,128)(2,1)}), bf16[1,2048,4,64]{1,3,2,0:T(8,128)(2,1)}) %all-gather.8.cloned.1.call-update) | async-done | bytes 1048592 | tf_op jit(solution)/shard_map/all_gather | solution.py:160
  60.6 29.6 %all-gather.10.cloned.1.call-done = bf16[1,2048,4,64]{1,3,2,0:T(8,128)(2,1)} async-done(((bf16[1,512,4,64]{1,3,2,0:T(8,128)(2,1)}), bf16[1,2048,4,64]{1,3,2,0:T(8,128)(2,1)}) %all-gather.10.cloned.1.call-update) | async-done | bytes 1048592 | tf_op jit(solution)/shard_map/all_gather | solution.py:159
  90.3 37.3 %while.26 = (s32[]{:T(128)}, bf16[4,512,2,64]{1,3,2,0:T(8,128)(2,1)S(1)}, f32[4,2,512]{2,1,0:T(2,128)S(1)}, bf16[4,2048,64]{1,2,0:T(8,128)(2,1)}, s32[4,512]{1,0...) while((s32[]{:T(128)}, ...), condition=%wide.region_8.9_spmd, body=%wide.region_5.8_spmd.sunk | while | flops 565181440 | bytes 30324844 | solution.py:167
  91.4 2.8 fusion.164
  96.2 3.4 fusion.166
  100.8 2.8 fusion.164
  105.5 3.3 fusion.166
  110.1 2.8 fusion.164
  114.9 3.3 fusion.166
  119.4 2.8 fusion.164
  124.2 3.3 fusion.166
  127.6 3.6 convolution_bitcast_fusion.1
  133.9 59.9 %all-reduce.12.cloned.1.call-done = f32[1,512,1024]{2,1,0:T(8,128)} async-done(((f32[1,512,1024]{2,1,0:T(8,128)}), f32[1,512,1024]{2,1,0:T(8,128)}) %all-reduce.12.cloned.1.call-update) | async-done | bytes 2097168 | tf_op jit(solution)/shard_map/psum | solution.py:176
  197.0 35.8 %all-gather.18.cloned.1.call-done = bf16[1024,2304]{1,0:T(8,128)(2,1)} async-done(((bf16[256,2304]{1,0:T(8,128)(2,1)}), bf16[1024,2304]{1,0:T(8,128)(2,1)}) %all-gather.18.cloned.1.call-update) | async-done | bytes 4718608 | tf_op jit(solution)/shard_map/all_gather | solution.py:134
  232.8 7.4 fusion.104
  240.2 31.7 %all-gather.16.cloned.1.call-done = bf16[1024,2304]{1,0:T(8,128)(2,1)} async-done(((bf16[256,2304]{1,0:T(8,128)(2,1)}), bf16[1024,2304]{1,0:T(8,128)(2,1)}) %all-gather.16.cloned.1.call-update) | async-done | bytes 4718608 | tf_op jit(solution)/shard_map/all_gather | solution.py:133
  271.9 7.4 fusion.103
  279.3 32.3 %all-gather.20.cloned.1.call-done = bf16[2304,1024]{1,0:T(8,128)(2,1)} async-done(((bf16[2304,256]{1,0:T(8,128)(2,1)}), bf16[2304,1024]{1,0:T(8,128)(2,1)}) %all-gather.20.cloned.1.call-update) | async-done | bytes 4718608 | tf_op jit(solution)/shard_map/all_gather | solution.py:135
  311.7 11.2 %multiply_convert_fusion = (bf16[512,2304]{1,0:T(8,128)(2,1)S(1)}, bf16[512,2304]{1,0:T(8,128)(2,1)S(1)}, bf16[512,2304]{1,0:T(8,128)(2,1)}) fusion(f32[512,2304]{1,0:T(8,128)} %fusion.103, f32[512,2304]{1,0:T(8,128)} %fusion.104, bf16[2304,1024]{1,0:T(8,128)(2,1)} %all-gather.20.cloned.1.call-done, bf16[1,512,1024]{2,1,0:T(8,128)(2,1)} %param.31), kind=kOutput, calls=%fused_computation.81 | convolution fusion | flops 2434793472 | bytes 22282240 | tf_op jit(solution)/shard_map/psd,fd->psf/dot_general | solution.py:189
  325.6 5.5 fusion.72
  333.1 62.8 %all-reduce.14.cloned.1.call-done = f32[1,512,1024]{2,1,0:T(8,128)} async-done(((f32[1,512,1024]{2,1,0:T(8,128)}), f32[1,512,1024]{2,1,0:T(8,128)}) %all-reduce.14.cloned.1.call-update) | async-done | bytes 2097168 | tf_op jit(solution)/shard_map/psum | solution.py:207
  396.0 3.7 convolution_convert_fusion.8
  400.5 73.3 %while.27 = (s32[]{:T(128)}, bf16[4,512,2,64]{1,3,2,0:T(8,128)(2,1)}, bf16[4,2048,64]{1,2,0:T(8,128)(2,1)}, bf16[4,2048,64]{1,2,0:T(8,128)(2,1)}, bf16[4,2048,64...) while((s32[]{:T(128)}, ...), condition=%wide.region_16.17_spmd, body=%wide.region_14.16_spmd.sunk | while | flops 1376975872 | bytes 92845392 | solution.py:216
  406.6 4.1 fusion.177
  424.9 4.1 fusion.177
  429.1 2.7 fusion.178
  443.3 4.1 fusion.177
  461.6 4.1 fusion.177
  465.7 2.7 fusion.178
  474.6 3.7 convolution_convert_fusion.4
  483.8 17.3 %reduce-scatter.10.cloned.1.call-done = bf16[1,512,4,64]{1,3,2,0:T(8,128)(2,1)} async-done(((bf16[1,2048,4,64]{1,3,2,0:T(8,128)(2,1)}), bf16[1,512,4,64]{1,3,2,0:T(8,128)(2,1)}) %reduce-scatter.10.cloned.1.call-update) | async-done | bytes 262160 | tf_op jit(solution)/shard_map/reduce_scatter | solution.py:223
  505.4 24.0 %reduce-scatter.12.cloned.1.call-done = bf16[1,512,4,64]{1,3,2,0:T(8,128)(2,1)} async-done(((bf16[1,2048,4,64]{1,3,2,0:T(8,128)(2,1)}), bf16[1,512,4,64]{1,3,2,0:T(8,128)(2,1)}) %reduce-scatter.12.cloned.1.call-update) | async-done | bytes 262160 | tf_op jit(solution)/shard_map/reduce_scatter | solution.py:226
  531.9 6.8 convolution_convert_fusion
  538.7 6.9 convolution_convert_fusion.1
  545.7 6.9 convolution_convert_fusion.2
  553.0 6.8 fusion.75
  564.6 18.3 %reduce-scatter.14.cloned.1.call-done = bf16[256,512]{1,0:T(8,128)(2,1)} async-done(((bf16[1024,512]{1,0:T(8,128)(2,1)}), bf16[256,512]{1,0:T(8,128)(2,1)}) %reduce-scatter.14.cloned.1.call-update) | async-done | bytes 262160 | tf_op jit(solution)/shard_map/reduce_scatter | solution.py:263
  582.9 24.6 %reduce-scatter.16.cloned.1.call-done = bf16[256,256]{1,0:T(8,128)(2,1)} async-done(((bf16[1024,256]{1,0:T(8,128)(2,1)}), bf16[256,256]{1,0:T(8,128)(2,1)}) %reduce-scatter.16.cloned.1.call-update) | async-done | bytes 131088 | tf_op jit(solution)/shard_map/reduce_scatter | solution.py:266
  607.5 24.2 %reduce-scatter.18.cloned.1.call-done = bf16[256,256]{1,0:T(8,128)(2,1)} async-done(((bf16[1024,256]{1,0:T(8,128)(2,1)}), bf16[256,256]{1,0:T(8,128)(2,1)}) %reduce-scatter.18.cloned.1.call-update) | async-done | bytes 131088 | tf_op jit(solution)/shard_map/reduce_scatter | solution.py:269
  631.7 50.2 %reduce-scatter.26.cloned.1.call-done = bf16[2304,256]{1,0:T(8,128)(2,1)} async-done(((bf16[2304,1024]{1,0:T(8,128)(2,1)}), bf16[2304,256]{1,0:T(8,128)(2,1)}) %reduce-scatter.26.cloned.1.call-update) | async-done | bytes 1179664 | tf_op jit(solution)/shard_map/reduce_scatter | solution.py:281
  682.0 50.4 %reduce-scatter.24.cloned.1.call-done = bf16[256,2304]{1,0:T(8,128)(2,1)} async-done(((bf16[1024,2304]{1,0:T(8,128)(2,1)}), bf16[256,2304]{1,0:T(8,128)(2,1)}) %reduce-scatter.24.cloned.1.call-update) | async-done | bytes 1179664 | tf_op jit(solution)/shard_map/reduce_scatter | solution.py:278
  732.4 50.2 %reduce-scatter.22.cloned.1.call-done = bf16[256,2304]{1,0:T(8,128)(2,1)} async-done(((bf16[1024,2304]{1,0:T(8,128)(2,1)}), bf16[256,2304]{1,0:T(8,128)(2,1)}) %reduce-scatter.22.cloned.1.call-update) | async-done | bytes 1179664 | tf_op jit(solution)/shard_map/reduce_scatter | solution.py:275
  782.6 39.8 %all-reduce.4 = (f32[1024]{0:T(1024)}, f32[1024]{0:T(1024)}, f32[64]{0:T(128)}, f32[64]{0:T(128)}) all-reduce(f32[1024]{0:T(1024)S(1)} %get-tuple-element.160, f32[1024]{0:T(1024)S(1)} %copy-done.50, f32[64]{0:T(128)S(1)} %get-tuple-element.162, ...), channel_id=1, replica_groups=mesh['fsdp'=4,'ctx'=4,'tp'=2] {'fsdp','ctx','tp'}, use_global_device_ids=true, to_apply=%region_38.39 | all-reduce | flops 2176 | bytes 17408 | tf_op jit(solution)/shard_map/psum | solution.py:294
  822.4 26.7 %all-reduce.18.cloned.1.call-done = (bf16[1,512,1024]{2,1,0:T(8,128)(2,1)}, bf16[1,512,1024]{2,1,0:T(8,128)(2,1)}) async-done(((bf16[1,512,1024]{2,1,0:T(8,128)(2,1)}, bf16[1,512,1024]{2,1,0:T(8,128)(2,1)}), (bf16[1,512,1024]{2,1,0:T(8,128)(2,1)}, bf16[1,512,1024]{2,1,0:T(8,128)(2,1)})) %all-reduce.18.cloned.1.call-update) | async-done | bytes 2097168 | tf_op jit(solution)/shard_map/psum | solution.py:184
  849.1 4.7 convert_add_fusion.1
  853.8 159.5 %all-reduce.16.cloned.1.call-done = (bf16[256,512]{1,0:T(8,128)(2,1)}, bf16[256,256]{1,0:T(8,128)(2,1)}, bf16[256,256]{1,0:T(8,128)(2,1)}, bf16[512,256]{1,0:T(8...) async-done(((bf16[256,512]{1,0:T(8,128)(2,1)}, bf16[256,256]{1,0:T(8,128)(2,1)}, bf16[256,256]{1,0:T(8,128)(2,1)}, ...) | async-done | bytes 4325392 | tf_op jit(solution)/shard_map/psum | solution.py:286
  (303 shorter events, 117.9 us)
Async XLA Ops:
  7.2 27.7 %all-gather.12.cloned.1.call-start = ((), (), s32[]{:S(2)}) async-start(), calls=%async_computation.11 | async-start | bytes 1310720 | tf_op jit(solution)/shard_map/all_gather | solution.py:129
  7.9 14.1 %copy-start.51 = (s32[1,6]{1,0:T(1,128)S(1)}, s32[1,6]{1,0:T(1,128)}, u32[]{:S(2)}) copy-start(s32[1,6]{1,0:T(1,128)} %param.19) | copy-start | bytes 76
  7.9 14.3 %copy-start.36 = (bf16[256,256]{1,0:T(8,128)(2,1)S(1)}, bf16[256,256]{1,0:T(8,128)(2,1)}, u32[]{:S(2)}) copy-start(bf16[256,256]{1,0:T(8,128)(2,1)} %param.21) | copy-start | bytes 393220
  7.9 52.7 %all-gather.8.cloned.1.call-start = ((), (), s32[]{:S(2)}) async-start(), calls=%async_computation.9 | async-start | bytes 1310720 | tf_op jit(solution)/shard_map/all_gather | solution.py:160
  9.5 9.0 copy-start.41
  9.5 21.9 %copy-start = (bf16[1,512,1024]{2,1,0:T(8,128)(2,1)S(1)}, bf16[1,512,1024]{2,1,0:T(8,128)(2,1)}, u32[]{:S(2)}) copy-start(bf16[1,512,1024]{2,1,0:T(8,128)(2,1)} %param.18) | copy-start | bytes 3145732
  9.5 21.9 %copy-start.44 = (f32[1024]{0:T(1024)S(1)}, f32[1024]{0:T(1024)}, u32[]{:S(2)}) copy-start(f32[1024]{0:T(1024)} %param.27) | copy-start | bytes 12292
  19.3 15.5 %copy-start.39 = (f32[512]{0:T(512)}, f32[512]{0:T(512)S(1)}, u32[]{:S(2)}) copy-start(f32[512]{0:T(512)S(1)} %fusion.91) | copy-start | bytes 6148
  21.9 11.2 %copy-start.46 = (f32[64]{0:T(128)S(1)}, f32[64]{0:T(128)}, u32[]{:S(2)}) copy-start(f32[64]{0:T(128)} %param.30) | copy-start | bytes 772
  22.0 68.3 %all-gather.10.cloned.1.call-start = ((), (), s32[]{:S(2)}) async-start(), calls=%async_computation.10 | async-start | bytes 1310720 | tf_op jit(solution)/shard_map/all_gather | solution.py:159
  33.2 5.0 copy-start.17
  33.2 5.0 copy-start.19
  34.2 93.5 %all-gather.14.cloned.1.call-start = ((), (), s32[]{:S(2)}) async-start(), calls=%async_computation.12 | async-start | bytes 1310720 | tf_op jit(solution)/shard_map/all_gather | solution.py:132
  34.7 159.1 %all-reduce.12.cloned.1.call-start = ((), (), s32[]{:S(2)}) async-start(), calls=%async_computation.13 | async-start | bytes 4194304 | tf_op jit(solution)/shard_map/psum | solution.py:176
  34.8 3.0 copy-start.48
  127.6 3.7 copy-start.6
  127.6 3.7 copy-start.7
  131.3 101.5 %all-gather.18.cloned.1.call-start = ((), (), s32[]{:S(2)}) async-start(), calls=%async_computation.15 | async-start | bytes 5898240 | tf_op jit(solution)/shard_map/all_gather | solution.py:134
  131.9 140.1 %all-gather.16.cloned.1.call-start = ((), (), s32[]{:S(2)}) async-start(), calls=%async_computation.14 | async-start | bytes 5898240 | tf_op jit(solution)/shard_map/all_gather | solution.py:133
  132.6 179.0 %all-gather.20.cloned.1.call-start = ((), (), s32[]{:S(2)}) async-start(), calls=%async_computation.16 | async-start | bytes 5898240 | tf_op jit(solution)/shard_map/all_gather | solution.py:135
  133.4 62.4 %copy-start.43 = (f32[1024]{0:T(1024)S(1)}, f32[1024]{0:T(1024)}, u32[]{:S(2)}) copy-start(f32[1024]{0:T(1024)} %param.28) | copy-start | bytes 12292
  133.4 262.6 %all-reduce.14.cloned.1.call-start = ((), (), s32[]{:S(2)}) async-start(), calls=%async_computation.17 | async-start | bytes 4194304 | tf_op jit(solution)/shard_map/psum | solution.py:207
  311.7 11.3 %copy-start.52 = (bf16[1024,2304]{1,0:T(8,128)(2,1)S(1)}, bf16[1024,2304]{1,0:T(8,128)(2,1)}, u32[]{:S(2)}) copy-start(bf16[1024,2304]{1,0:T(8,128)(2,1)} %all-gather.16.cloned.1.call-done) | copy-start | bytes 14155780
  332.9 168.3 %reduce-scatter.10.cloned.1.call-start = ((), (), s32[]{:S(2)}) async-start(), calls=%async_computation.18 | async-start | bytes 1310720 | tf_op jit(solution)/shard_map/reduce_scatter | solution.py:223
  406.6 4.1 copy-start.26
  410.7 2.8 copy-start.11
  424.9 4.1 copy-start.26
  443.3 4.1 copy-start.26
  461.6 4.1 copy-start.26
  473.9 55.5 %reduce-scatter.12.cloned.1.call-start = ((), (), s32[]{:S(2)}) async-start(), calls=%async_computation.19 | async-start | bytes 1310720 | tf_op jit(solution)/shard_map/reduce_scatter | solution.py:226
  474.6 90.0 %reduce-scatter.20.cloned.1.call-start = ((), (), s32[]{:S(2)}) async-start(), calls=%async_computation.23 | async-start | bytes 1310720 | tf_op jit(solution)/shard_map/reduce_scatter | solution.py:272
  478.4 104.5 %reduce-scatter.14.cloned.1.call-start = ((), (), s32[]{:S(2)}) async-start(), calls=%async_computation.20 | async-start | bytes 1310720 | tf_op jit(solution)/shard_map/reduce_scatter | solution.py:263
  483.5 18.8 %copy-start.35 = (f32[512,4]{0,1:T(4,128)S(1)}, f32[512,4]{0,1:T(4,128)}, u32[]{:S(2)}) copy-start(f32[512,4]{0,1:T(4,128)} %copy-done.34) | copy-start | bytes 24580
  483.5 18.8 %copy-start.47 = (f32[64]{0:T(128)S(1)}, f32[64]{0:T(128)}, u32[]{:S(2)}) copy-start(f32[64]{0:T(128)} %param.30) | copy-start | bytes 772
  483.5 20.1 %copy-start.38 = (f32[512,4]{0,1:T(4,128)S(1)}, f32[512,4]{0,1:T(4,128)}, u32[]{:S(2)}) copy-start(f32[512,4]{0,1:T(4,128)} %copy-done.37) | copy-start | bytes 24580
  483.6 124.0 %reduce-scatter.16.cloned.1.call-start = ((), (), s32[]{:S(2)}) async-start(), calls=%async_computation.21 | async-start | bytes 655360 | tf_op jit(solution)/shard_map/reduce_scatter | solution.py:266
  505.3 126.4 %reduce-scatter.18.cloned.1.call-start = ((), (), s32[]{:S(2)}) async-start(), calls=%async_computation.22 | async-start | bytes 655360 | tf_op jit(solution)/shard_map/reduce_scatter | solution.py:269
  531.8 150.1 %reduce-scatter.26.cloned.1.call-start = ((), (), s32[]{:S(2)}) async-start(), calls=%async_computation.26 | async-start | bytes 5898240 | tf_op jit(solution)/shard_map/reduce_scatter | solution.py:281
  538.6 193.7 %reduce-scatter.24.cloned.1.call-start = ((), (), s32[]{:S(2)}) async-start(), calls=%async_computation.25 | async-start | bytes 5898240 | tf_op jit(solution)/shard_map/reduce_scatter | solution.py:278
  545.6 237.0 %reduce-scatter.22.cloned.1.call-start = ((), (), s32[]{:S(2)}) async-start(), calls=%async_computation.24 | async-start | bytes 5898240 | tf_op jit(solution)/shard_map/reduce_scatter | solution.py:275
  552.6 296.5 %all-reduce.18.cloned.1.call-start = ((), (), s32[]{:S(2)}) async-start(), calls=%async_computation.28 | async-start | bytes 4194304 | tf_op jit(solution)/shard_map/psum | solution.py:184
  552.9 6.8 copy-start.16
  553.0 6.8 copy-start.24
  564.5 218.1 %copy-start.50 = (f32[1024]{0:T(1024)S(1)}, f32[1024]{0:T(1024)}, u32[]{:S(2)}) copy-start(f32[1024]{0:T(1024)} %get-tuple-element.158) | copy-start | bytes 12292
  564.5 284.6 %copy-start.3 = (bf16[1,512,1024]{2,1,0:T(8,128)(2,1)S(1)}, bf16[1,512,1024]{2,1,0:T(8,128)(2,1)}, u32[]{:S(2)}) copy-start(bf16[1,512,1024]{2,1,0:T(8,128)(2,1)} %param.31) | copy-start | bytes 3145732
  564.6 448.7 %all-reduce.16.cloned.1.call-start = ((), (), s32[]{:S(2)}) async-start(), calls=%async_computation.27 | async-start | bytes 8650752 | tf_op jit(solution)/shard_map/psum | solution.py:286
  1013.3 7.0 copy-start.23
  1016.8 5.1 copy-start.22
  (48 other events, 83.5 us)
Sparse Core Ops, SparseCore 0:
  9.6 21.1 all-gather.11
  32.9 27.6 all-gather.7
  62.8 27.4 all-gather.9
  91.6 16.3 all-gather.13
  131.4 62.3 all-reduce.11
  195.3 37.4 all-gather.17
  234.4 37.4 all-gather.15
  273.5 38.0 all-gather.19
  333.0 62.9 all-reduce.13
  474.0 27.1 reduce-scatter.9
  503.6 25.7 reduce-scatter.11
  531.8 23.5 reduce-scatter.19
  558.0 24.8 reduce-scatter.13
  585.9 21.6 reduce-scatter.15
  610.0 21.6 reduce-scatter.17
  634.1 47.8 reduce-scatter.25
  684.5 47.8 reduce-scatter.23
  734.8 47.8 reduce-scatter.21
  785.7 63.4 all-reduce.17
  851.9 161.3 all-reduce.15
where the time goes:
time: 1040 us; the launch traced here: 1030 us
  waiting for transfers between devices  723 us (70%)
  matrix products  164 us (16%)
  other arithmetic  59.3 us (6%)
  blocking collectives  57.8 us (6%)
  between operations  15.5 us (1%)
    psum x1, waiting for transfers between devices, shards(): lax.psum(shares[0].astype(jnp.bfloat16), 'ctx').astype(jnp.float32)  159 us
    psum x1, waiting for transfers between devices, shards(): grad_after = out_grad.astype(jnp.float32) + lax.psum(grad_after_part, 'tp')  62.8 us
    psum x1, waiting for transfers between devices, shards(): after_attn = inputs + lax.psum(attn_part, 'tp')  59.9 us
    reduce_scatter x1, waiting for transfers between devices, shards(): lax.psum_scatter(weight_grads[5].astype(jnp.bfloat16), 'fsdp', scatter_di...  50.4 us
    reduce_scatter x1, waiting for transfers between devices, shards(): lax.psum_scatter(weight_grads[4].astype(jnp.bfloat16), 'fsdp', scatter_di...  50.2 us
    reduce_scatter x1, waiting for transfers between devices, shards(): lax.psum_scatter(weight_grads[6].astype(jnp.bfloat16), 'fsdp', scatter_di...  50.2 us
    psum x1, blocking collectives, shards(): lax.psum((grad_attn_gain, grad_ffn_gain, grad_query_gain, grad_key_gain),...  39.8 us
    all_gather x1, waiting for transfers between devices, shards(): lax.all_gather(up_weight, 'fsdp', axis=0, tiled=True)  35.8 us
  transfers between devices with their start and end apart: 20, of which 17 were waited for; matrix products, arithmetic and copies ran while one was open for 11% of the time, Pallas kernels for 0%

commit v1 on v0

v1 whole, which is shorter than its diff:
```python
import jax
import jax.numpy as jnp
from jax import lax
from jax.experimental import pallas as pl
from jax.experimental.pallas import tpu as pltpu
from jax.sharding import PartitionSpec as P

HD = 64


EPSILON = 1e-05
ROPE_BASE = 1000000.0


def rms_norm(values, gain_vec):
    return (
        values * lax.rsqrt(jnp.mean(values * values, axis=-1, keepdims=True) + EPSILON) * gain_vec
    )


def rotate(values, rope_pos):
    half_dim = HD // 2
    frequency = ROPE_BASE ** (-2.0 * jnp.arange(half_dim, dtype=jnp.float32) / HD)
    angles = rope_pos[..., None, None] * frequency
    cosine = jnp.cos(angles)
    sine_part = jnp.sin(angles)
    lower_half = values[..., :half_dim]
    upper_half = values[..., half_dim:]
    return jnp.concatenate(
        [
            lower_half * cosine - upper_half * sine_part,
            upper_half * cosine + lower_half * sine_part,
        ],
        axis=-1,
    )


def head_prep(projected, gain_vec, rope_pos):
    shaped = projected.reshape(projected.shape[:-1] + (-1, HD))
    return rotate(rms_norm(shaped, gain_vec), rope_pos)


def pairs(axis, step):
    return [(i, i ^ step) for i in range(lax.axis_size(axis))]


def keep_low(values):
    return lax.optimization_barrier(values.astype(jnp.bfloat16))


def both(values):
    total = keep_low(values)
    step = 1
    while step < lax.axis_size("tp"):
        other = lax.ppermute(total, "tp", pairs("tp", step))
        total = total.astype(jnp.float32) + other.astype(jnp.float32)
        step *= 2
        if step < lax.axis_size("tp"):
            total = keep_low(total)
    return total.astype(jnp.float32)


def gather(shard, axis):
    count = lax.axis_size("fsdp")
    mine = lax.axis_index("fsdp")
    pieces = {0: shard}
    step = count // 2
    while step >= 1:
        moved = {
            p ^ step: lax.ppermute(piece, "fsdp", pairs("fsdp", step))
            for p, piece in pieces.items()
        }
        pieces.update(moved)
        step //= 2
    extent = shard.shape[axis]
    reps = [1, 1]
    reps[axis] = count
    full = jnp.tile(shard, reps)
    for p, piece in pieces.items():
        if p:
            full = lax.dynamic_update_slice_in_dim(full, piece, (mine ^ p) * extent, axis)
    return full


def reduce_blocks(block_of):
    count = lax.axis_size("fsdp")
    mine = lax.axis_index("fsdp")
    held = {}
    for p in sorted(range(count), key=lambda p: -(p & 1)):
        held[p] = block_of(mine ^ p)
    step = 1
    while step < count:
        sent = {
            p: lax.ppermute(block.astype(jnp.bfloat16), "fsdp", pairs("fsdp", step))
            for p, block in held.items()
            if p & step
        }
        held = {
            p: block + sent[p ^ step].astype(jnp.float32)
            for p, block in held.items()
            if not p & step
        }
        step *= 2
    return held[0]


def over_ctx(block):
    count = lax.axis_size("ctx")
    place = lax.axis_index("ctx")
    rows = block.shape[0] // count
    ring = [(i, (i + 1) % count) for i in range(count)]

    def chunk(index):
        return lax.dynamic_slice_in_dim(block, (index % count) * rows, rows, 0)

    running = chunk(place + count)
    for step in range(1, count):
        arrived = lax.ppermute(running.astype(jnp.bfloat16), "ctx", ring)
        running = arrived.astype(jnp.float32) + chunk(place + count - step)
    held = keep_low(running)
    full = jnp.zeros(block.shape, jnp.float32)
    for step in range(count):
        if step:
            held = lax.ppermute(held, "ctx", ring)
        full = lax.dynamic_update_slice_in_dim(
            full, held.astype(jnp.float32), ((place + 1 + count - step) % count) * rows, 0
        )
    return full


def everywhere(values):
    for axis in ("tp", "fsdp", "ctx"):
        step = 1
        while step < lax.axis_size(axis):
            values = values + lax.ppermute(values, axis, pairs(axis, step))
            step *= 2
    return values


def visible_keys(start_ref, place_ref, key_count):
    key_place = lax.broadcasted_iota(jnp.int32, (key_count, start_ref.shape[-1]), 0)
    return (key_place >= start_ref[0]) & (key_place <= place_ref[0])


LAST = (((1,), (1,)), ((), ()))


def attend_kernel(start_ref, place_ref, query_ref, key_ref, value_t_ref, out_ref, log_ref):
    scores = lax.dot_general(key_ref[0], query_ref[0], LAST, preferred_element_type=jnp.float32)
    scores = jnp.where(visible_keys(start_ref, place_ref, key_ref.shape[1]), scores, -1e30)
    row_max = jnp.max(scores, axis=0, keepdims=True)
    exponent = jnp.exp(scores - row_max)
    row_total = jnp.sum(exponent, axis=0, keepdims=True)
    weights_soft = (exponent * (1.0 / row_total)).astype(jnp.bfloat16)
    attended = jnp.dot(value_t_ref[0], weights_soft, preferred_element_type=jnp.float32)
    out_ref[0] = attended.T.astype(jnp.bfloat16)
    log_ref[0] = row_max + jnp.log(row_total)


def back_kernel(
    start_ref,
    place_ref,
    query_ref,
    grad_ref,
    key_ref,
    key_t_ref,
    value_ref,
    log_ref,
    grad_query_ref,
    grad_key_ref,
    grad_value_ref,
    key_total,
    value_total,
):
    tile = pl.program_id(1)

    @pl.when(tile == 0)
    def _():
        key_total[...] = jnp.zeros_like(key_total)
        value_total[...] = jnp.zeros_like(value_total)

    query = query_ref[0]
    grad = grad_ref[0]
    scores = lax.dot_general(key_ref[0], query, LAST, preferred_element_type=jnp.float32)
    scores = jnp.where(visible_keys(start_ref, place_ref, key_ref.shape[1]), scores, -1e30)
    weights_soft = jnp.exp(scores - log_ref[0])
    grad_soft = lax.dot_general(value_ref[0], grad, LAST, preferred_element_type=jnp.float32)
    delta = jnp.sum(weights_soft * grad_soft, axis=0, keepdims=True)
    grad_scores = (weights_soft * (grad_soft - delta)).astype(jnp.bfloat16)
    grad_query = jnp.dot(key_t_ref[0], grad_scores, preferred_element_type=jnp.float32)
    grad_query_ref[0] = (grad_query * HD ** (-0.5)).T.astype(jnp.bfloat16)
    key_total[...] += jnp.dot(grad_scores, query, preferred_element_type=jnp.float32)
    value_total[...] += jnp.dot(
        weights_soft.astype(jnp.bfloat16), grad, preferred_element_type=jnp.float32
    )

    @pl.when(tile == pl.num_programs(1) - 1)
    def _():
        grad_key_ref[0] = key_total[...].astype(jnp.bfloat16)
        grad_value_ref[0] = value_total[...].astype(jnp.bfloat16)


def attention_specs(groups, tok_rows, key_count, tile):
    per_token = tok_rows // tile
    row = pl.BlockSpec((1, 1, tile), lambda i, j: (i // groups, 0, j % per_token))
    query = pl.BlockSpec((1, tile, HD), lambda i, j: (i, j, 0))
    key = pl.BlockSpec((1, key_count, HD), lambda i, j: (i, 0, 0))
    key_t = pl.BlockSpec((1, HD, key_count), lambda i, j: (i, 0, 0))
    log = pl.BlockSpec((1, 1, tile), lambda i, j: (i, 0, j))
    return row, query, key, key_t, log


def cost(items, rows, key_count, dots):
    return pl.CostEstimate(
        flops=2 * dots * items * rows * key_count * HD,
        bytes_accessed=4 * items * (rows + key_count) * HD,
        transcendentals=items * rows * key_count,
    )


PARAMS = pltpu.CompilerParams(vmem_limit_bytes=50 * 1024 * 1024)


def attend(start, place, queries, keys, values_t, groups):
    items, rows, _ = queries.shape
    key_count = keys.shape[1]
    tile = min(256, start.shape[-1])
    row, query, key, key_t, log = attention_specs(groups, start.shape[-1], key_count, tile)
    return pl.pallas_call(
        attend_kernel,
        grid=(items, rows // tile),
        in_specs=[row, row, query, key, key_t],
        out_specs=[query, log],
        out_shape=[
            jax.ShapeDtypeStruct((items, rows, HD), jnp.bfloat16),
            jax.ShapeDtypeStruct((items, 1, rows), jnp.float32),
        ],
        compiler_params=PARAMS,
        cost_estimate=cost(items, rows, key_count, 2),
    )(start, place, queries, keys, values_t)


def attend_back(start, place, queries, grads, keys, keys_t, values, log_total, groups):
    items, rows, _ = queries.shape
    key_count = keys.shape[1]
    tile = min(256, start.shape[-1])
    row, query, key, key_t, log = attention_specs(groups, start.shape[-1], key_count, tile)
    return pl.pallas_call(
        back_kernel,
        grid=(items, rows // tile),
        in_specs=[row, row, query, query, key, key_t, key, log],
        out_specs=[query, key, key],
        out_shape=[
            jax.ShapeDtypeStruct((items, rows, HD), jnp.bfloat16),
            jax.ShapeDtypeStruct((items, key_count, HD), jnp.bfloat16),
            jax.ShapeDtypeStruct((items, key_count, HD), jnp.bfloat16),
        ],
        scratch_shapes=[
            pltpu.VMEM((key_count, HD), jnp.float32),
            pltpu.VMEM((key_count, HD), jnp.float32),
        ],
        compiler_params=PARAMS,
        cost_estimate=cost(items, rows, key_count, 5),
    )(start, place, queries, grads, keys, keys_t, values, log_total)


def dot_nt(left, right):
    return lax.dot_general(left, right, LAST, preferred_element_type=jnp.float32)


def dot_tn(left, right):
    return lax.dot_general(
        left, right, (((0,), (0,)), ((), ())), preferred_element_type=jnp.float32
    )


def shards(
    tokens,
    lengths,
    query_weight,
    key_weight,
    value_weight,
    out_weight,
    gate_weight,
    up_weight,
    down_weight,
    attn_gain,
    ffn_gain,
    query_gain,
    key_gain,
    out_grad,
):
    pack_count, tok_rows, width = tokens.shape
    total_rows = pack_count * tok_rows
    pack_len = tok_rows * lax.axis_size("ctx")
    offset = lax.axis_index("ctx") * tok_rows
    q_width = query_weight.shape[1]
    k_width = key_weight.shape[1]
    units = gate_weight.shape[1]
    groups = k_width // HD
    heads = q_width // HD
    per_group = heads // groups
    qkv_shard = jnp.concatenate([query_weight, key_weight, value_weight], axis=1)
    full_qkv = gather(qkv_shard, 0)
    full_out = gather(out_weight, 1)
    full_gate = gather(gate_weight, 0)
    full_up = gather(up_weight, 0)
    full_down = gather(down_weight, 1)

    local_place = offset + jnp.arange(tok_rows, dtype=jnp.int32)
    seq_ends = jnp.cumsum(lengths, axis=1)
    passed = (local_place[None, :, None] >= seq_ends[:, None, :]).astype(jnp.int32)
    local_start = jnp.sum(passed * lengths[:, None, :], axis=2)
    rope_pos = (local_place[None, :] - local_start).astype(jnp.float32)
    start_rows = local_start[:, None, :]
    place_rows = jnp.broadcast_to(local_place, (pack_count, 1, tok_rows))

    inputs = tokens.reshape(total_rows, width).astype(jnp.float32)
    cotangent = out_grad.reshape(total_rows, width)
    normed = rms_norm(inputs, attn_gain).astype(jnp.bfloat16)
    projected = jnp.dot(normed, full_qkv, preferred_element_type=jnp.float32)
    shaped = projected.reshape(pack_count, tok_rows, -1)
    query_proj = shaped[..., :q_width]
    key_proj = shaped[..., q_width : q_width + k_width]
    value_low = shaped[..., q_width + k_width :].astype(jnp.bfloat16)
    queries, query_pull = jax.vjp(
        lambda values, gain_vec: head_prep(values, gain_vec, rope_pos), query_proj, query_gain
    )
    keys_rot, key_pull = jax.vjp(
        lambda values, gain_vec: head_prep(values, gain_vec, rope_pos), key_proj, key_gain
    )
    keys_low = keys_rot.astype(jnp.bfloat16).reshape(pack_count, tok_rows, k_width)
    all_kv = lax.all_gather(
        jnp.concatenate([keys_low, value_low], axis=-1), "ctx", axis=1, tiled=True
    )
    kv_items = all_kv.reshape(pack_count, pack_len, 2, groups, HD)
    kv_items = jnp.transpose(kv_items, (2, 0, 3, 1, 4)).reshape(
        2, pack_count * groups, pack_len, HD
    )
    key_items, value_items = kv_items[0], kv_items[1]
    key_t_items = jnp.swapaxes(key_items, 1, 2)
    value_t_items = jnp.swapaxes(value_items, 1, 2)

    def to_rows(values):
        split = values.reshape(pack_count, tok_rows, groups, per_group, HD)
        return jnp.transpose(split, (0, 2, 3, 1, 4)).reshape(
            pack_count * groups, per_group * tok_rows, HD
        )

    def from_rows(values):
        split = values.reshape(pack_count, groups, per_group, tok_rows, HD)
        return jnp.transpose(split, (0, 3, 1, 2, 4)).reshape(total_rows, heads * HD)

    query_items = to_rows((queries * HD ** (-0.5)).astype(jnp.bfloat16))
    attended_items, log_total = attend(
        start_rows, place_rows, query_items, key_items, value_t_items, groups
    )
    attended = from_rows(attended_items)
    attn_part = jnp.dot(attended, full_out, preferred_element_type=jnp.float32)
    after_attn = inputs + both(attn_part)
    normed_ffn = rms_norm(after_attn, ffn_gain).astype(jnp.bfloat16)
    gate_proj = jnp.dot(normed_ffn, full_gate, preferred_element_type=jnp.float32)
    up_proj = jnp.dot(normed_ffn, full_up, preferred_element_type=jnp.float32)
    hidden, swiglu_pull = jax.vjp(
        lambda gate_in, up_in: jax.nn.silu(gate_in) * up_in, gate_proj, up_proj
    )
    hidden = hidden.astype(jnp.bfloat16)

    def columns(values, index, extent):
        return lax.dynamic_slice_in_dim(values, index * extent, extent, 1)

    down_extent = down_weight.shape[1]
    row_extent = gate_weight.shape[0]
    share_down = over_ctx(
        reduce_blocks(lambda b: dot_tn(hidden, columns(cotangent, b, down_extent)))
    )
    grad_hidden = dot_nt(cotangent, full_down)
    grad_gate_proj, grad_up_proj = swiglu_pull(grad_hidden)
    grad_gate_proj = grad_gate_proj.astype(jnp.bfloat16)
    grad_up_proj = grad_up_proj.astype(jnp.bfloat16)
    grad_normed_ffn = dot_nt(grad_gate_proj, full_gate) + dot_nt(grad_up_proj, full_up)
    unused_ffn, ffn_pull = jax.vjp(rms_norm, after_attn, ffn_gain)
    grad_after_part, grad_ffn_gain = ffn_pull(grad_normed_ffn)
    grad_after = cotangent.astype(jnp.float32) + both(grad_after_part)
    ffn_out = both(jnp.dot(hidden, full_down, preferred_element_type=jnp.float32))
    mixed = (after_attn + ffn_out).astype(jnp.bfloat16)
    share_gate = over_ctx(
        reduce_blocks(lambda b: dot_tn(columns(normed_ffn, b, row_extent), grad_gate_proj))
    )
    share_up = over_ctx(
        reduce_blocks(lambda b: dot_tn(columns(normed_ffn, b, row_extent), grad_up_proj))
    )
    grad_after_low = grad_after.astype(jnp.bfloat16)
    grad_attended = dot_nt(grad_after_low, full_out).astype(jnp.bfloat16)
    share_out = over_ctx(
        reduce_blocks(lambda b: dot_tn(attended, columns(grad_after_low, b, down_extent)))
    )
    grad_q_items, grad_k_items, grad_v_items = attend_back(
        start_rows,
        place_rows,
        query_items,
        to_rows(grad_attended),
        key_items,
        key_t_items,
        value_items,
        log_total,
        groups,
    )
    grad_kv = jnp.stack([grad_k_items, grad_v_items]).reshape(
        2, pack_count, groups, pack_len, HD
    )
    grad_kv = jnp.transpose(grad_kv, (1, 3, 0, 2, 4)).reshape(pack_count, pack_len, 2 * k_width)
    own_kv = lax.psum_scatter(grad_kv, "ctx", scatter_dimension=1, tiled=True)
    own_kv = lax.optimization_barrier(own_kv.astype(jnp.bfloat16))
    grad_keys = own_kv[..., :k_width].reshape(pack_count, tok_rows, groups, HD)
    grad_value_low = own_kv[..., k_width:].reshape(total_rows, k_width)
    grad_queries = from_rows(grad_q_items).reshape(pack_count, tok_rows, heads, HD)
    grad_query_proj, grad_query_gain = query_pull(grad_queries.astype(jnp.float32))
    grad_key_proj, grad_key_gain = key_pull(grad_keys.astype(jnp.float32))
    grad_qkv = jnp.concatenate(
        [
            grad_query_proj.astype(jnp.bfloat16).reshape(total_rows, q_width),
            grad_key_proj.astype(jnp.bfloat16).reshape(total_rows, k_width),
            grad_value_low,
        ],
        axis=1,
    )
    share_qkv = over_ctx(
        reduce_blocks(lambda b: dot_tn(columns(normed, b, row_extent), grad_qkv))
    )
    grad_normed = dot_nt(grad_qkv, full_qkv)
    unused_attn, attn_pull = jax.vjp(rms_norm, inputs, attn_gain)
    grad_input_part, grad_attn_gain = attn_pull(grad_normed)
    tokens_grad = grad_after + both(grad_input_part)
    gain_parts = (grad_attn_gain, grad_ffn_gain, grad_query_gain, grad_key_gain)
    gain_sums = everywhere(jnp.concatenate(gain_parts))
    bounds = [0]
    for part in gain_parts:
        bounds.append(bounds[-1] + part.shape[0])
    return (
        mixed.reshape(tokens.shape),
        tokens_grad.reshape(tokens.shape),
        share_qkv[:, :q_width],
        share_qkv[:, q_width : q_width + k_width],
        share_qkv[:, q_width + k_width :],
        share_out,
        share_gate,
        share_up,
        share_down,
        gain_sums[bounds[0] : bounds[1]],
        gain_sums[bounds[1] : bounds[2]],
        gain_sums[bounds[2] : bounds[3]],
        gain_sums[bounds[3] : bounds[4]],
    )


def solution(mesh):
    in_specs = (
        P("fsdp", "ctx", None),
        P("fsdp", None),
        P("fsdp", "tp"),
        P("fsdp", "tp"),
        P("fsdp", "tp"),
        P("tp", "fsdp"),
        P("fsdp", "tp"),
        P("fsdp", "tp"),
        P("tp", "fsdp"),
        P(),
        P(),
        P(),
        P(),
        P("fsdp", "ctx", None),
    )
    out_specs = (
        P("fsdp", "ctx", None),
        P("fsdp", "ctx", None),
        P("fsdp", "tp"),
        P("fsdp", "tp"),
        P("fsdp", "tp"),
        P("tp", "fsdp"),
        P("fsdp", "tp"),
        P("fsdp", "tp"),
        P("tp", "fsdp"),
        P(),
        P(),
        P(),
        P(),
    )
    return jax.shard_map(shards, mesh=mesh, in_specs=in_specs, out_specs=out_specs, check_vma=False)
```

time: 1040 us -> 596 us (0.57)
  waiting for transfers between devices: 723 us -> 255 us
  matrix products: 164 us -> 70 us
  local copies, waits for them, and re-layouts: 9.98 us -> 83.3 us
  Pallas kernels: 0 us -> 66.9 us
  blocking collectives: 57.8 us -> 0 us
  starting transfers between devices: 1.91 us -> 48.4 us
  other arithmetic: 59.3 us -> 47.6 us
    psum x4 -> x0, waiting for transfers between devices: 309 us -> none  [the longest x1 159 us: shards(): lax.psum(shares[0].astype(jnp.bfloat16), 'ctx').astype(jnp.float32)]
    reduce_scatter x9 -> x1, waiting for transfers between devices: 259 us -> 0.01 us  [shards(): own_kv = lax.psum_scatter(grad_kv, 'ctx', scatter_dimension=1, tiled=True)]
    ppermute x0 -> x69, waiting for transfers between devices: none -> 255 us  [the longest x15 92.2 us: over_ctx(): held = lax.ppermute(held, 'ctx', ring)]
    all_gather x7 -> x1, waiting for transfers between devices: 151 us -> 0.01 us  [shards(): lax.all_gather(jnp.concatenate([keys_low, value_low], axis=-1), 'ctx', ax...]
    dot_general x45 -> x26, matrix products: 139 us -> 49.4 us  [the longest x20 28.7 us: dot_tn(): lax.dot_general(left, right, (((0,), (0,)), ((), ())), preferred_element_...]
    pallas_call x0 -> x2, Pallas kernels: none -> 66.9 us  [the longest x1 38.4 us: attend_back(): pl.pallas_call(back_kernel, grid=(items, rows // tile), in_specs=[row, ro...]
    ppermute x0 -> x69, starting transfers between devices: none -> 48.4 us  [the longest x15 19.7 us: over_ctx(): arrived = lax.ppermute(running.astype(jnp.bfloat16), 'ctx', ring)]
    psum x1 -> x0, blocking collectives: 39.8 us -> none  [shards(): lax.psum((grad_attn_gain, grad_ffn_gain, grad_query_gain, grad_key_gain),...]
  transfers between devices with their start and end apart: 20 -> 71, of which waited for: 17 -> 32; matrix products, arithmetic and copies ran while one was open for 11% -> 27% of each run, Pallas kernels for 0% -> 11%
where the time goes in v1:
time: 596 us; the launch traced here: 587 us
  waiting for transfers between devices  255 us (43%)
  local copies, waits for them, and re-layouts  83.3 us (14%)
  matrix products  70 us (12%)
  Pallas kernels  66.9 us (11%)
  starting transfers between devices  48.4 us (8%)
  other arithmetic  47.6 us (8%)
  between operations  15.9 us (3%)
    ppermute x15, waiting for transfers between devices, over_ctx(): held = lax.ppermute(held, 'ctx', ring)  92.2 us
    ppermute x15, waiting for transfers between devices, gather(): lax.ppermute(piece, 'fsdp', pairs('fsdp', step))  50.6 us
    ppermute x15, waiting for transfers between devices, over_ctx(): arrived = lax.ppermute(running.astype(jnp.bfloat16), 'ctx', ring)  49.9 us
    pallas_call x1, Pallas kernels, attend_back(): pl.pallas_call(back_kernel, grid=(items, rows // tile), in_specs=[row, ro...  38.4 us
    ppermute x4, waiting for transfers between devices, both(): other = lax.ppermute(total, 'tp', pairs('tp', step))  33.4 us
    dot_general x20, matrix products, dot_tn(): lax.dot_general(left, right, (((0,), (0,)), ((), ())), preferred_element_...  28.7 us
    pallas_call x1, Pallas kernels, attend(): pl.pallas_call(attend_kernel, grid=(items, rows // tile), in_specs=[row,...  28.5 us
    ppermute x15, waiting for transfers between devices, reduce_blocks(): lax.ppermute(block.astype(jnp.bfloat16), 'fsdp', pairs('fsdp', step))  22.3 us
  transfers between devices with their start and end apart: 71, of which 32 were waited for; matrix products, arithmetic and copies ran while one was open for 27% of the time, Pallas kernels for 11%

profile of v1, /device:TPU:0, one launch (start us, length us, event | category | flops | bytes accessed | tf_op | source)
XLA Modules:
  0.0 586.8 jit_solution(18088103318570818567)
XLA Ops:
  10.2 3.0 collective-permute-start
  19.7 12.0 %collective-permute-done.3 = bf16[512,256]{1,0:T(8,128)(2,1)} collective-permute-done((bf16[512,256]{1,0:T(8,128)(2,1)}, bf16[512,256]{1,0:T(8,128)(2,1)}, u32[]{:S(2)}, u32[]{:S(2)}) %collective-permute-start.3) | collective-permute-done | bytes 262176 | tf_op jit(solution)/shard_map/ppermute | solution.py:70
  32.3 2.9 tile.53
  35.3 3.7 copy.65
  59.5 3.9 tile.51
  65.7 16.5 %collective-permute-done.13 = bf16[2304,256]{1,0:T(8,128)(2,1)} collective-permute-done((bf16[2304,256]{1,0:T(8,128)(2,1)}, bf16[2304,256]{1,0:T(8,128)(2,1)}, u32[]{:S(2)}, u32[]{:S(2)}) %collective-permute-start.13) | collective-permute-done | bytes 1179680 | tf_op jit(solution)/shard_map/ppermute | solution.py:70
  84.7 22.0 %collective-permute-done.7 = bf16[256,2304]{1,0:T(8,128)(2,1)} collective-permute-done((bf16[256,2304]{1,0:T(8,128)(2,1)}, bf16[256,2304]{1,0:T(8,128)(2,1)}, u32[]{:S(2)}, u32[]{:S(2)}) %collective-permute-start.7) | collective-permute-done | bytes 1179680 | tf_op jit(solution)/shard_map/ppermute | solution.py:70
  106.7 3.7 tile.24
  120.4 3.1 copy.54
  123.5 3.2 copy.55
  126.7 6.1 %slice_bitcast_fusion.1 = (bf16[4,2048,64]{2,1,0:T(8,128)(2,1)}, bf16[4,64,2048]{1,2,0:T(8,128)(2,1)}, bf16[4,64,2048]{1,2,0:T(8,128)(2,1)}, bf16[4,2048,64]{2,1,0:T(8,128)(2,1)}) fusion(bf16[2,1,4,2048,64]{4,3,2,1,0:T(8,128)(2,1)} %bitcast.140), kind=kLoop, calls=%fused_computation.48 | loop fusion | bytes 6291456 | tf_op jit(solution)/shard_map/squeeze | solution.py:340
  134.7 28.5 %shard_map.237 = (bf16[4,1024,64]{2,1,0:T(8,128)(2,1)S(1)}, f32[4,1,1024]{2,1,0:T(1,128)S(1)}) custom-call(s32[1,1,512]{2,1,0:T(1,128)S(1)} %bitcast.135, s32[1,1,512]{2,1,0:T(1,128)S(1)} %iota_add_fusion.place_ref, bf16[4,1024,64]{2,1,0:T(8,128)(2,1)S(1)} %bitcast.130, bf16[4,2048,64]{2,1,0:T(8,128)(2,1)} %get-tuple-element.39.key_ref, ...), custom_call_target="tpu_custom_call" | custom-call | flops 2147483648 | bytes 3145728 | tf_op jit(solution)/shard_map/pallas_call | solution.py:229
  163.6 3.1 convolution_convert_fusion.7
  173.2 6.7 %convolution_bitcast_fusion = f32[512,2304]{1,0:T(8,128)} fusion(bf16[2304,1024]{1,0:T(8,128)(2,1)} %constant_dynamic-update-slice_fusion, bf16[1,512,1024]{2,1,0:T(8,128)(2,1)S(1)} %copy-done.13), kind=kOutput, calls=%fused_computation.1 | convolution fusion | flops 2415919104 | bytes 10485760 | tf_op jit(solution)/shard_map/dot_general | solution.py:268
  182.7 9.3 %collective-permute-done.6 = bf16[512,1024]{1,0:T(8,128)(2,1)} collective-permute-done((bf16[512,1024]{1,0:T(8,128)(2,1)}, bf16[512,1024]{1,0:T(8,128)(2,1)}, u32[]{:S(2)}, u32[]{:S(2)}) %collective-permute-start.6) | collective-permute-done | bytes 1048608 | tf_op jit(solution)/shard_map/ppermute | solution.py:55
  194.4 5.1 fusion.92
  199.5 7.3 %fusion.2 = (bf16[512,2304]{1,0:T(8,128)(2,1)S(1)}, bf16[512,2304]{1,0:T(8,128)(2,1)S(1)}, bf16[512,2304]{1,0:T(8,128)(2,1)S(1)}) fusion(f32[512,2304]{1,0:T(8,128)S(1)} %bitcast.174, f32[512,2304]{1,0:T(8,128)S(1)} %fusion.92, bf16[512,1024]{1,0:T(8,128)(2,1)S(1)} %multiply_convert_fusion.2, bf16[1024,2304]{1,0:T(8,128)(2,1)} %constant_dynamic-update-slice_fusion.6), kind=kOutput, calls=%fused_computation.4 | convolution fusion | flops 2434793472 | bytes 22282240 | tf_op jit(solution)/shard_map/dot_general | solution.py:362
  206.9 5.1 convolution_convert_fusion.6
  214.7 4.5 fusion.93
  226.8 5.1 multiply_reduce_fusion
  236.9 11.8 %collective-permute-done.16 = bf16[512,1024]{1,0:T(8,128)(2,1)S(1)} collective-permute-done((bf16[512,1024]{1,0:T(8,128)(2,1)S(1)}, bf16[512,1024]{1,0:T(8,128)(2,1)S(1)}, u32[]{:S(2)}, u32[]{:S(2)}) %collective-permute-start.16) | collective-permute-done | bytes 1048608 | tf_op jit(solution)/shard_map/ppermute | solution.py:55
  261.7 11.9 %collective-permute-done.17 = bf16[512,1024]{1,0:T(8,128)(2,1)S(1)} collective-permute-done((bf16[512,1024]{1,0:T(8,128)(2,1)S(1)}, bf16[512,1024]{1,0:T(8,128)(2,1)S(1)}, u32[]{:S(2)}, u32[]{:S(2)}) %collective-permute-start.17) | collective-permute-done | bytes 1048608 | tf_op jit(solution)/shard_map/ppermute | solution.py:55
  279.0 38.4 %shard_map.238 = (bf16[4,1024,64]{2,1,0:T(8,128)(2,1)S(1)}, bf16[4,2048,64]{2,1,0:T(8,128)(2,1)}, bf16[4,2048,64]{2,1,0:T(8,128)(2,1)}) custom-call(s32[1,1,512]{2,1,0:T(1,128)S(1)} %bitcast.136, s32[1,1,512]{2,1,0:T(1,128)S(1)} %iota_add_fusion.place_ref, bf16[4,1024,64]{2,1,0:T(8,128)(2,1)S(1)} %bitcast.131, bf16[4,1024,64]{2,1,0:T(8,128)(2,1)S(1)} %bitcast.133, ...), custom_call_target="tpu_custom_call" | custom-call | flops 5368709120 | bytes 3145728 | tf_op jit(solution)/shard_map/pallas_call | solution.py:248
  321.4 4.6 maximum_bitcast_fusion
  325.9 5.0 copy.62
  347.4 17.1 %collective-permute-done.39 = bf16[256,2304]{1,0:T(8,128)(2,1)S(1)} collective-permute-done((bf16[256,2304]{1,0:T(8,128)(2,1)S(1)}, bf16[256,2304]{1,0:T(8,128)(2,1)S(1)}, u32[]{:S(2)}, u32[]{:S(2)}) %collective-permute-start.39) | collective-permute-done | bytes 1179680 | tf_op jit(solution)/shard_map/ppermute | solution.py:94
  371.3 16.0 %collective-permute-done.31 = bf16[128,256]{1,0:T(8,128)(2,1)S(1)} collective-permute-done((bf16[128,256]{1,0:T(8,128)(2,1)S(1)}, bf16[128,256]{1,0:T(8,128)(2,1)S(1)}, u32[]{:S(2)}, u32[]{:S(2)}) %collective-permute-start.31) | collective-permute-done | bytes 65568 | tf_op jit(solution)/shard_map/ppermute | solution.py:118
  387.3 3.0 collective-permute-start.32
  392.9 9.8 %collective-permute-done.32 = bf16[128,256]{1,0:T(8,128)(2,1)S(1)} collective-permute-done((bf16[128,256]{1,0:T(8,128)(2,1)S(1)}, bf16[128,256]{1,0:T(8,128)(2,1)S(1)}, u32[]{:S(2)}, u32[]{:S(2)}) %collective-permute-start.32) | collective-permute-done | bytes 65568 | tf_op jit(solution)/shard_map/ppermute | solution.py:118
  403.4 7.9 %collective-permute-done.33 = bf16[128,256]{1,0:T(8,128)(2,1)S(1)} collective-permute-done((bf16[128,256]{1,0:T(8,128)(2,1)S(1)}, bf16[128,256]{1,0:T(8,128)(2,1)S(1)}, u32[]{:S(2)}, u32[]{:S(2)}) %collective-permute-start.33) | collective-permute-done | bytes 65568 | tf_op jit(solution)/shard_map/ppermute | solution.py:118
  411.5 7.0 %collective-permute-done.34 = bf16[128,256]{1,0:T(8,128)(2,1)S(1)} collective-permute-done((bf16[128,256]{1,0:T(8,128)(2,1)S(1)}, bf16[128,256]{1,0:T(8,128)(2,1)S(1)}, u32[]{:S(2)}, u32[]{:S(2)}) %collective-permute-start.34) | collective-permute-done | bytes 65568 | tf_op jit(solution)/shard_map/ppermute | solution.py:124
  420.4 3.4 collective-permute-start.42
  425.4 18.9 %collective-permute-done.36 = bf16[128,256]{1,0:T(8,128)(2,1)S(1)} collective-permute-done((bf16[128,256]{1,0:T(8,128)(2,1)S(1)}, bf16[128,256]{1,0:T(8,128)(2,1)S(1)}, u32[]{:S(2)}, u32[]{:S(2)}) %collective-permute-start.36) | collective-permute-done | bytes 65568 | tf_op jit(solution)/shard_map/ppermute | solution.py:124
  456.8 5.6 collective-permute-done.52
  463.3 5.5 collective-permute-done.43
  470.5 4.7 collective-permute-done.62
  475.2 6.2 %collective-permute-done.53 = bf16[64,2304]{1,0:T(8,128)(2,1)S(1)} collective-permute-done((bf16[64,2304]{1,0:T(8,128)(2,1)S(1)}, bf16[64,2304]{1,0:T(8,128)(2,1)S(1)}, u32[]{:S(2)}, u32[]{:S(2)}) %collective-permute-start.53) | collective-permute-done | bytes 294944 | tf_op jit(solution)/shard_map/ppermute | solution.py:124
  481.4 6.3 %collective-permute-done.44 = bf16[64,2304]{1,0:T(8,128)(2,1)S(1)} collective-permute-done((bf16[64,2304]{1,0:T(8,128)(2,1)S(1)}, bf16[64,2304]{1,0:T(8,128)(2,1)S(1)}, u32[]{:S(2)}, u32[]{:S(2)}) %collective-permute-start.44) | collective-permute-done | bytes 294944 | tf_op jit(solution)/shard_map/ppermute | solution.py:124
  491.5 8.9 %collective-permute-done.54 = bf16[64,2304]{1,0:T(8,128)(2,1)S(1)} collective-permute-done((bf16[64,2304]{1,0:T(8,128)(2,1)S(1)}, bf16[64,2304]{1,0:T(8,128)(2,1)S(1)}, u32[]{:S(2)}, u32[]{:S(2)}) %collective-permute-start.54) | collective-permute-done | bytes 294944 | tf_op jit(solution)/shard_map/ppermute | solution.py:124
  501.3 3.1 collective-permute-done.45
  521.8 3.2 collective-permute-done.67
  529.6 5.2 collective-permute-done.21
  535.8 6.2 %collective-permute-done.22 = bf16[64,1024]{1,0:T(8,128)(2,1)S(1)} collective-permute-done((bf16[64,1024]{1,0:T(8,128)(2,1)S(1)}, bf16[64,1024]{1,0:T(8,128)(2,1)S(1)}, u32[]{:S(2)}, u32[]{:S(2)}) %collective-permute-start.22) | collective-permute-done | bytes 131104 | tf_op jit(solution)/shard_map/ppermute | solution.py:118
  542.6 6.2 %collective-permute-done.23 = bf16[64,1024]{1,0:T(8,128)(2,1)S(1)} collective-permute-done((bf16[64,1024]{1,0:T(8,128)(2,1)S(1)}, bf16[64,1024]{1,0:T(8,128)(2,1)S(1)}, u32[]{:S(2)}, u32[]{:S(2)}) %collective-permute-start.23) | collective-permute-done | bytes 131104 | tf_op jit(solution)/shard_map/ppermute | solution.py:118
  551.8 3.8 collective-permute-done.24
  555.9 7.8 %collective-permute-done.25 = bf16[64,1024]{1,0:T(8,128)(2,1)S(1)} collective-permute-done((bf16[64,1024]{1,0:T(8,128)(2,1)S(1)}, bf16[64,1024]{1,0:T(8,128)(2,1)S(1)}, u32[]{:S(2)}, u32[]{:S(2)}) %collective-permute-start.25) | collective-permute-done | bytes 131104 | tf_op jit(solution)/shard_map/ppermute | solution.py:124
  563.8 7.3 %collective-permute-done.26 = bf16[64,1024]{1,0:T(8,128)(2,1)S(1)} collective-permute-done((bf16[64,1024]{1,0:T(8,128)(2,1)S(1)}, bf16[64,1024]{1,0:T(8,128)(2,1)S(1)}, u32[]{:S(2)}, u32[]{:S(2)}) %collective-permute-start.26) | collective-permute-done | bytes 131104 | tf_op jit(solution)/shard_map/ppermute | solution.py:124
  571.1 6.7 %collective-permute-done.27 = bf16[64,1024]{1,0:T(8,128)(2,1)S(1)} collective-permute-done((bf16[64,1024]{1,0:T(8,128)(2,1)S(1)}, bf16[64,1024]{1,0:T(8,128)(2,1)S(1)}, u32[]{:S(2)}, u32[]{:S(2)}) %collective-permute-start.27) | collective-permute-done | bytes 131104 | tf_op jit(solution)/shard_map/ppermute | solution.py:124
  (366 shorter events, 174.6 us)
Async XLA Ops:
  7.2 113.1 %all-gather.2.cloned.1.call-start = ((), (), s32[]{:S(2)}) async-start(), calls=%async_computation.1 | async-start | bytes 2621440 | tf_op jit(solution)/shard_map/all_gather | solution.py:333
  10.2 28.8 %collective-permute-start = (bf16[256,1024]{1,0:T(8,128)(2,1)S(1)}, bf16[256,1024]{1,0:T(8,128)(2,1)S(1)}, u32[]{:S(2)}, u32[]{:S(2)}) collective-permute-start(bf16[256,1024]{1,0:T(8,128)(2,1)S(1)} %constant_dynamic-update-slice_fusion.15), channel_id=1, source_target_pairs={{0,16},{8,24},{16,0},{24,8},{1,17},{9,25},{17,1},{25,9},{2,18},{10... | collective-permute-start | bytes 1572872 | tf_op jit(solution)/shard_map/ppermute | solution.py:70
  13.2 31.8 %collective-permute-start.1 = (bf16[256,1024]{1,0:T(8,128)(2,1)S(1)}, bf16[256,1024]{1,0:T(8,128)(2,1)S(1)}, u32[]{:S(2)}, u32[]{:S(2)}) collective-permute-start(bf16[256,1024]{1,0:T(8,128)(2,1)S(1)} %constant_dynamic-update-slice_fusion.15), channel_id=1, source_target_pairs={{0,8},{8,0},{16,24},{24,16},{1,9},{9,1},{17,25},{25,17},{2,10},{10... | collective-permute-start | bytes 1572872 | tf_op jit(solution)/shard_map/ppermute | solution.py:70
  13.2 18.5 %collective-permute-start.3 = (bf16[512,256]{1,0:T(8,128)(2,1)}, bf16[512,256]{1,0:T(8,128)(2,1)}, u32[]{:S(2)}, u32[]{:S(2)}) collective-permute-start(bf16[512,256]{1,0:T(8,128)(2,1)} %param.19), channel_id=1, source_target_pairs={{0,16},{8,24},{16,0},{24,8},{1,17},{9,25},{17,1},{25,9},{2,18},{10... | collective-permute-start | bytes 786440 | tf_op jit(solution)/shard_map/ppermute | solution.py:70
  13.4 27.0 %collective-permute-start.4 = (bf16[512,256]{1,0:T(8,128)(2,1)}, bf16[512,256]{1,0:T(8,128)(2,1)}, u32[]{:S(2)}, u32[]{:S(2)}) collective-permute-start(bf16[512,256]{1,0:T(8,128)(2,1)} %param.19), channel_id=1, source_target_pairs={{0,8},{8,0},{16,24},{24,16},{1,9},{9,1},{17,25},{25,17},{2,10},{10... | collective-permute-start | bytes 786440 | tf_op jit(solution)/shard_map/ppermute | solution.py:70
  13.7 45.6 %collective-permute-start.10 = (bf16[256,2304]{1,0:T(8,128)(2,1)}, bf16[256,2304]{1,0:T(8,128)(2,1)}, u32[]{:S(2)}, u32[]{:S(2)}) collective-permute-start(bf16[256,2304]{1,0:T(8,128)(2,1)} %param.21), channel_id=1, source_target_pairs={{0,16},{8,24},{16,0},{24,8},{1,17},{9,25},{17,1},{25,9},{2,18},{10... | collective-permute-start | bytes 3538952 | tf_op jit(solution)/shard_map/ppermute | solution.py:70
  40.3 72.4 %collective-permute-start.11 = (bf16[256,2304]{1,0:T(8,128)(2,1)}, bf16[256,2304]{1,0:T(8,128)(2,1)}, u32[]{:S(2)}, u32[]{:S(2)}) collective-permute-start(bf16[256,2304]{1,0:T(8,128)(2,1)} %param.21), channel_id=1, source_target_pairs={{0,8},{8,0},{16,24},{24,16},{1,9},{9,1},{17,25},{25,17},{2,10},{10... | collective-permute-start | bytes 3538952 | tf_op jit(solution)/shard_map/ppermute | solution.py:70
  41.5 40.7 %collective-permute-start.13 = (bf16[2304,256]{1,0:T(8,128)(2,1)}, bf16[2304,256]{1,0:T(8,128)(2,1)}, u32[]{:S(2)}, u32[]{:S(2)}) collective-permute-start(bf16[2304,256]{1,0:T(8,128)(2,1)} %param.22), channel_id=1, source_target_pairs={{0,16},{8,24},{16,0},{24,8},{1,17},{9,25},{17,1},{25,9},{2,18},{10... | collective-permute-start | bytes 3538952 | tf_op jit(solution)/shard_map/ppermute | solution.py:70
  45.0 70.7 %collective-permute-start.14 = (bf16[2304,256]{1,0:T(8,128)(2,1)}, bf16[2304,256]{1,0:T(8,128)(2,1)}, u32[]{:S(2)}, u32[]{:S(2)}) collective-permute-start(bf16[2304,256]{1,0:T(8,128)(2,1)} %param.22), channel_id=1, source_target_pairs={{0,8},{8,0},{16,24},{24,16},{1,9},{9,1},{17,25},{25,17},{2,10},{10... | collective-permute-start | bytes 3538952 | tf_op jit(solution)/shard_map/ppermute | solution.py:70
  45.6 61.0 %collective-permute-start.7 = (bf16[256,2304]{1,0:T(8,128)(2,1)}, bf16[256,2304]{1,0:T(8,128)(2,1)}, u32[]{:S(2)}, u32[]{:S(2)}) collective-permute-start(bf16[256,2304]{1,0:T(8,128)(2,1)} %param.20), channel_id=1, source_target_pairs={{0,16},{8,24},{16,0},{24,8},{1,17},{9,25},{17,1},{25,9},{2,18},{10... | collective-permute-start | bytes 3538952 | tf_op jit(solution)/shard_map/ppermute | solution.py:70
  51.4 453.8 %reduce-scatter.2.cloned.1.call-start = ((), (), s32[]{:S(2)}) async-start(), calls=%async_computation.2 | async-start | bytes 2621440 | tf_op jit(solution)/shard_map/reduce_scatter | solution.py:413
  59.4 58.8 %collective-permute-start.8 = (bf16[256,2304]{1,0:T(8,128)(2,1)}, bf16[256,2304]{1,0:T(8,128)(2,1)S(1)}, u32[]{:S(2)}, u32[]{:S(2)}) collective-permute-start(bf16[256,2304]{1,0:T(8,128)(2,1)} %param.20), channel_id=1, source_target_pairs={{0,8},{8,0},{16,24},{24,16},{1,9},{9,1},{17,25},{25,17},{2,10},{10... | collective-permute-start | bytes 3538952 | tf_op jit(solution)/shard_map/ppermute | solution.py:70
  82.2 37.0 %collective-permute-start.12 = (bf16[256,2304]{1,0:T(8,128)(2,1)}, bf16[256,2304]{1,0:T(8,128)(2,1)S(1)}, u32[]{:S(2)}, u32[]{:S(2)}) collective-permute-start(bf16[256,2304]{1,0:T(8,128)(2,1)} %collective-permute-done.10), channel_id=1, source_target_pairs={{0,8},{8,0},{16,24},{24,16},{1,9},{9,1},{17,25},{25,17},{2,10},{10... | collective-permute-start | bytes 3538952 | tf_op jit(solution)/shard_map/ppermute | solution.py:70
  106.7 61.7 %collective-permute-start.15 = (bf16[2304,256]{1,0:T(8,128)(2,1)}, bf16[2304,256]{1,0:T(8,128)(2,1)}, u32[]{:S(2)}, u32[]{:S(2)}) collective-permute-start(bf16[2304,256]{1,0:T(8,128)(2,1)} %collective-permute-done.13), channel_id=1, source_target_pairs={{0,8},{8,0},{16,24},{24,16},{1,9},{9,1},{17,25},{25,17},{2,10},{10... | collective-permute-start | bytes 3538952 | tf_op jit(solution)/shard_map/ppermute | solution.py:70
  112.7 58.1 %collective-permute-start.9 = (bf16[256,2304]{1,0:T(8,128)(2,1)}, bf16[256,2304]{1,0:T(8,128)(2,1)}, u32[]{:S(2)}, u32[]{:S(2)}) collective-permute-start(bf16[256,2304]{1,0:T(8,128)(2,1)} %collective-permute-done.7), channel_id=1, source_target_pairs={{0,8},{8,0},{16,24},{24,16},{1,9},{9,1},{17,25},{25,17},{2,10},{10... | collective-permute-start | bytes 3538952 | tf_op jit(solution)/shard_map/ppermute | solution.py:70
  166.7 25.3 %collective-permute-start.6 = (bf16[512,1024]{1,0:T(8,128)(2,1)}, bf16[512,1024]{1,0:T(8,128)(2,1)}, u32[]{:S(2)}, u32[]{:S(2)}) collective-permute-start(bf16[512,1024]{1,0:T(8,128)(2,1)} %convolution_convert_fusion.7), channel_id=1, source_target_pairs={{0,1},{1,0},{2,3},{3,2},{4,5},{5,4},{6,7},{7,6},{8,9},{9,8},{10,11... | collective-permute-start | bytes 3145736 | tf_op jit(solution)/shard_map/ppermute | solution.py:55
  224.5 24.2 %collective-permute-start.16 = (bf16[512,1024]{1,0:T(8,128)(2,1)S(1)}, bf16[512,1024]{1,0:T(8,128)(2,1)S(1)}, u32[]{:S(2)}, u32[]{:S(2)}) collective-permute-start(bf16[512,1024]{1,0:T(8,128)(2,1)S(1)} %convolution_convert_fusion.6), channel_id=1, source_target_pairs={{0,1},{1,0},{2,3},{3,2},{4,5},{5,4},{6,7},{7,6},{8,9},{9,8},{10,11... | collective-permute-start | bytes 3145736 | tf_op jit(solution)/shard_map/ppermute | solution.py:55
  226.3 30.1 %collective-permute-start.56 = (bf16[2304,256]{1,0:T(8,128)(2,1)S(1)}, bf16[2304,256]{1,0:T(8,128)(2,1)S(1)}, u32[]{:S(2)}, u32[]{:S(2)}) collective-permute-start(bf16[2304,256]{1,0:T(8,128)(2,1)S(1)} %convolution_convert_fusion), channel_id=1, source_target_pairs={{0,8},{8,0},{16,24},{24,16},{1,9},{9,1},{17,25},{25,17},{2,10},{10... | collective-permute-start | bytes 3538952 | tf_op jit(solution)/shard_map/ppermute | solution.py:94
  226.3 27.7 %collective-permute-start.47 = (bf16[256,2304]{1,0:T(8,128)(2,1)S(1)}, bf16[256,2304]{1,0:T(8,128)(2,1)S(1)}, u32[]{:S(2)}, u32[]{:S(2)}) collective-permute-start(bf16[256,2304]{1,0:T(8,128)(2,1)S(1)} %convolution_convert_fusion.2), channel_id=1, source_target_pairs={{0,8},{8,0},{16,24},{24,16},{1,9},{9,1},{17,25},{25,17},{2,10},{10... | collective-permute-start | bytes 3538952 | tf_op jit(solution)/shard_map/ppermute | solution.py:94
  236.8 21.5 %collective-permute-start.38 = (bf16[256,2304]{1,0:T(8,128)(2,1)S(1)}, bf16[256,2304]{1,0:T(8,128)(2,1)S(1)}, u32[]{:S(2)}, u32[]{:S(2)}) collective-permute-start(bf16[256,2304]{1,0:T(8,128)(2,1)S(1)} %convolution_convert_fusion.4), channel_id=1, source_target_pairs={{0,8},{8,0},{16,24},{24,16},{1,9},{9,1},{17,25},{25,17},{2,10},{10... | collective-permute-start | bytes 3538952 | tf_op jit(solution)/shard_map/ppermute | solution.py:94
  250.4 23.2 %collective-permute-start.17 = (bf16[512,1024]{1,0:T(8,128)(2,1)S(1)}, bf16[512,1024]{1,0:T(8,128)(2,1)S(1)}, u32[]{:S(2)}, u32[]{:S(2)}) collective-permute-start(bf16[512,1024]{1,0:T(8,128)(2,1)S(1)} %get-tuple-element.40), channel_id=1, source_target_pairs={{0,1},{1,0},{2,3},{3,2},{4,5},{5,4},{6,7},{7,6},{8,9},{9,8},{10,11... | collective-permute-start | bytes 3145736 | tf_op jit(solution)/shard_map/ppermute | solution.py:55
  254.0 82.7 %collective-permute-start.55 = (bf16[2304,256]{1,0:T(8,128)(2,1)}, bf16[2304,256]{1,0:T(8,128)(2,1)}, u32[]{:S(2)}, u32[]{:S(2)}) collective-permute-start(bf16[2304,256]{1,0:T(8,128)(2,1)} %convolution_convert_fusion.1), channel_id=1, source_target_pairs={{0,8},{8,0},{16,24},{24,16},{1,9},{9,1},{17,25},{25,17},{2,10},{10... | collective-permute-start | bytes 3538952 | tf_op jit(solution)/shard_map/ppermute | solution.py:94
  254.0 85.8 %collective-permute-start.46 = (bf16[256,2304]{1,0:T(8,128)(2,1)}, bf16[256,2304]{1,0:T(8,128)(2,1)}, u32[]{:S(2)}, u32[]{:S(2)}) collective-permute-start(bf16[256,2304]{1,0:T(8,128)(2,1)} %convolution_convert_fusion.3), channel_id=1, source_target_pairs={{0,8},{8,0},{16,24},{24,16},{1,9},{9,1},{17,25},{25,17},{2,10},{10... | collective-permute-start | bytes 3538952 | tf_op jit(solution)/shard_map/ppermute | solution.py:94
  256.4 89.5 %collective-permute-start.37 = (bf16[256,2304]{1,0:T(8,128)(2,1)}, bf16[256,2304]{1,0:T(8,128)(2,1)}, u32[]{:S(2)}, u32[]{:S(2)}) collective-permute-start(bf16[256,2304]{1,0:T(8,128)(2,1)} %convolution_convert_fusion.5), channel_id=1, source_target_pairs={{0,8},{8,0},{16,24},{24,16},{1,9},{9,1},{17,25},{25,17},{2,10},{10... | collective-permute-start | bytes 3538952 | tf_op jit(solution)/shard_map/ppermute | solution.py:94
  258.3 78.8 %collective-permute-start.57 = (bf16[2304,256]{1,0:T(8,128)(2,1)}, bf16[2304,256]{1,0:T(8,128)(2,1)}, u32[]{:S(2)}, u32[]{:S(2)}) collective-permute-start(bf16[2304,256]{1,0:T(8,128)(2,1)} %add_convert_fusion), channel_id=1, source_target_pairs={{0,16},{8,24},{16,0},{24,8},{1,17},{9,25},{17,1},{25,9},{2,18},{10... | collective-permute-start | bytes 3538952 | tf_op jit(solution)/shard_map/ppermute | solution.py:94
  273.5 66.4 %collective-permute-start.48 = (bf16[256,2304]{1,0:T(8,128)(2,1)}, bf16[256,2304]{1,0:T(8,128)(2,1)}, u32[]{:S(2)}, u32[]{:S(2)}) collective-permute-start(bf16[256,2304]{1,0:T(8,128)(2,1)} %add_convert_fusion.1), channel_id=1, source_target_pairs={{0,16},{8,24},{16,0},{24,8},{1,17},{9,25},{17,1},{25,9},{2,18},{10... | collective-permute-start | bytes 3538952 | tf_op jit(solution)/shard_map/ppermute | solution.py:94
  336.7 27.8 %collective-permute-start.39 = (bf16[256,2304]{1,0:T(8,128)(2,1)S(1)}, bf16[256,2304]{1,0:T(8,128)(2,1)S(1)}, u32[]{:S(2)}, u32[]{:S(2)}) collective-permute-start(bf16[256,2304]{1,0:T(8,128)(2,1)S(1)} %copy-done.26), channel_id=1, source_target_pairs={{0,16},{8,24},{16,0},{24,8},{1,17},{9,25},{17,1},{25,9},{2,18},{10... | collective-permute-start | bytes 3538952 | tf_op jit(solution)/shard_map/ppermute | solution.py:94
  337.1 30.7 %collective-permute-start.28 = (bf16[512,256]{1,0:T(8,128)(2,1)S(1)}, bf16[512,256]{1,0:T(8,128)(2,1)S(1)}, u32[]{:S(2)}, u32[]{:S(2)}) collective-permute-start(bf16[512,256]{1,0:T(8,128)(2,1)S(1)} %convolution_convert_fusion.12), channel_id=1, source_target_pairs={{0,8},{8,0},{16,24},{24,16},{1,9},{9,1},{17,25},{25,17},{2,10},{10... | collective-permute-start | bytes 786440 | tf_op jit(solution)/shard_map/ppermute | solution.py:94
  339.9 29.7 %collective-permute-start.58 = (bf16[576,256]{1,0:T(8,128)(2,1)S(1)}, bf16[576,256]{1,0:T(8,128)(2,1)S(1)}, u32[]{:S(2)}, u32[]{:S(2)}) collective-permute-start(bf16[576,256]{1,0:T(8,128)(2,1)S(1)} %dynamic-slice_convert_fusion), channel_id=1, source_target_pairs={{0,2},{2,4},{4,6},{6,0},{1,3},{3,5},{5,7},{7,1},{8,10},{10,12},{12... | collective-permute-start | bytes 884744 | tf_op jit(solution)/shard_map/ppermute | solution.py:118
  343.9 46.3 %collective-permute-start.49 = (bf16[64,2304]{1,0:T(8,128)(2,1)S(1)}, bf16[64,2304]{1,0:T(8,128)(2,1)S(1)}, u32[]{:S(2)}, u32[]{:S(2)}) collective-permute-start(bf16[64,2304]{1,0:T(8,128)(2,1)S(1)} %dynamic-slice_convert_fusion.1), channel_id=1, source_target_pairs={{0,2},{2,4},{4,6},{6,0},{1,3},{3,5},{5,7},{7,1},{8,10},{10,12},{12... | collective-permute-start | bytes 884744 | tf_op jit(solution)/shard_map/ppermute | solution.py:118
  345.9 22.0 %collective-permute-start.30 = (bf16[512,256]{1,0:T(8,128)(2,1)S(1)}, bf16[512,256]{1,0:T(8,128)(2,1)S(1)}, u32[]{:S(2)}, u32[]{:S(2)}) collective-permute-start(bf16[512,256]{1,0:T(8,128)(2,1)S(1)} %add_convert_fusion.14), channel_id=1, source_target_pairs={{0,16},{8,24},{16,0},{24,8},{1,17},{9,25},{17,1},{25,9},{2,18},{10... | collective-permute-start | bytes 786440 | tf_op jit(solution)/shard_map/ppermute | solution.py:94
  366.2 36.6 %collective-permute-start.40 = (bf16[64,2304]{1,0:T(8,128)(2,1)S(1)}, bf16[64,2304]{1,0:T(8,128)(2,1)S(1)}, u32[]{:S(2)}, u32[]{:S(2)}) collective-permute-start(bf16[64,2304]{1,0:T(8,128)(2,1)S(1)} %dynamic-slice_convert_fusion.2), channel_id=1, source_target_pairs={{0,2},{2,4},{4,6},{6,0},{1,3},{3,5},{5,7},{7,1},{8,10},{10,12},{12... | collective-permute-start | bytes 884744 | tf_op jit(solution)/shard_map/ppermute | solution.py:118
  367.9 19.3 %collective-permute-start.31 = (bf16[128,256]{1,0:T(8,128)(2,1)S(1)}, bf16[128,256]{1,0:T(8,128)(2,1)S(1)}, u32[]{:S(2)}, u32[]{:S(2)}) collective-permute-start(bf16[128,256]{1,0:T(8,128)(2,1)S(1)} %dynamic-slice_convert_fusion.4), channel_id=1, source_target_pairs={{0,2},{2,4},{4,6},{6,0},{1,3},{3,5},{5,7},{7,1},{8,10},{10,12},{12... | collective-permute-start | bytes 196616 | tf_op jit(solution)/shard_map/ppermute | solution.py:118
  369.7 48.9 %collective-permute-start.59 = (bf16[576,256]{1,0:T(8,128)(2,1)S(1)}, bf16[576,256]{1,0:T(8,128)(2,1)S(1)}, u32[]{:S(2)}, u32[]{:S(2)}) collective-permute-start(bf16[576,256]{1,0:T(8,128)(2,1)S(1)} %add_convert_fusion.7), channel_id=1, source_target_pairs={{0,2},{2,4},{4,6},{6,0},{1,3},{3,5},{5,7},{7,1},{8,10},{10,12},{12... | collective-permute-start | bytes 884744 | tf_op jit(solution)/shard_map/ppermute | solution.py:118
  390.3 28.4 %collective-permute-start.50 = (bf16[64,2304]{1,0:T(8,128)(2,1)S(1)}, bf16[64,2304]{1,0:T(8,128)(2,1)S(1)}, u32[]{:S(2)}, u32[]{:S(2)}) collective-permute-start(bf16[64,2304]{1,0:T(8,128)(2,1)S(1)} %add_convert_fusion.10), channel_id=1, source_target_pairs={{0,2},{2,4},{4,6},{6,0},{1,3},{3,5},{5,7},{7,1},{8,10},{10,12},{12... | collective-permute-start | bytes 884744 | tf_op jit(solution)/shard_map/ppermute | solution.py:118
  402.9 17.5 %collective-permute-start.41 = (bf16[64,2304]{1,0:T(8,128)(2,1)S(1)}, bf16[64,2304]{1,0:T(8,128)(2,1)S(1)}, u32[]{:S(2)}, u32[]{:S(2)}) collective-permute-start(bf16[64,2304]{1,0:T(8,128)(2,1)S(1)} %add_convert_fusion.13), channel_id=1, source_target_pairs={{0,2},{2,4},{4,6},{6,0},{1,3},{3,5},{5,7},{7,1},{8,10},{10,12},{12... | collective-permute-start | bytes 884744 | tf_op jit(solution)/shard_map/ppermute | solution.py:118
  418.6 25.7 %collective-permute-start.60 = (bf16[576,256]{1,0:T(8,128)(2,1)S(1)}, bf16[576,256]{1,0:T(8,128)(2,1)S(1)}, u32[]{:S(2)}, u32[]{:S(2)}) collective-permute-start(bf16[576,256]{1,0:T(8,128)(2,1)S(1)} %add_convert_fusion.6), channel_id=1, source_target_pairs={{0,2},{2,4},{4,6},{6,0},{1,3},{3,5},{5,7},{7,1},{8,10},{10,12},{12... | collective-permute-start | bytes 884744 | tf_op jit(solution)/shard_map/ppermute | solution.py:118
  418.8 25.6 %collective-permute-start.51 = (bf16[64,2304]{1,0:T(8,128)(2,1)S(1)}, bf16[64,2304]{1,0:T(8,128)(2,1)S(1)}, u32[]{:S(2)}, u32[]{:S(2)}) collective-permute-start(bf16[64,2304]{1,0:T(8,128)(2,1)S(1)} %add_convert_fusion.9), channel_id=1, source_target_pairs={{0,2},{2,4},{4,6},{6,0},{1,3},{3,5},{5,7},{7,1},{8,10},{10,12},{12... | collective-permute-start | bytes 884744 | tf_op jit(solution)/shard_map/ppermute | solution.py:118
  420.4 24.2 %collective-permute-start.42 = (bf16[64,2304]{1,0:T(8,128)(2,1)S(1)}, bf16[64,2304]{1,0:T(8,128)(2,1)S(1)}, u32[]{:S(2)}, u32[]{:S(2)}) collective-permute-start(bf16[64,2304]{1,0:T(8,128)(2,1)S(1)} %add_convert_fusion.12), channel_id=1, source_target_pairs={{0,2},{2,4},{4,6},{6,0},{1,3},{3,5},{5,7},{7,1},{8,10},{10,12},{12... | collective-permute-start | bytes 884744 | tf_op jit(solution)/shard_map/ppermute | solution.py:118
  425.3 18.9 %collective-permute-start.36 = (bf16[128,256]{1,0:T(8,128)(2,1)S(1)}, bf16[128,256]{1,0:T(8,128)(2,1)S(1)}, u32[]{:S(2)}, u32[]{:S(2)}) collective-permute-start(bf16[128,256]{1,0:T(8,128)(2,1)S(1)} %collective-permute-done.35), channel_id=1, source_target_pairs={{0,2},{2,4},{4,6},{6,0},{1,3},{3,5},{5,7},{7,1},{8,10},{10,12},{12... | collective-permute-start | bytes 196616 | tf_op jit(solution)/shard_map/ppermute | solution.py:124
  444.5 18.0 %collective-permute-start.52 = (bf16[64,2304]{1,0:T(8,128)(2,1)S(1)}, bf16[64,2304]{1,0:T(8,128)(2,1)S(1)}, u32[]{:S(2)}, u32[]{:S(2)}) collective-permute-start(bf16[64,2304]{1,0:T(8,128)(2,1)S(1)} %add_convert_fusion.8), channel_id=1, source_target_pairs={{0,2},{2,4},{4,6},{6,0},{1,3},{3,5},{5,7},{7,1},{8,10},{10,12},{12... | collective-permute-start | bytes 884744 | tf_op jit(solution)/shard_map/ppermute | solution.py:124
  445.1 23.7 %collective-permute-start.43 = (bf16[64,2304]{1,0:T(8,128)(2,1)S(1)}, bf16[64,2304]{1,0:T(8,128)(2,1)S(1)}, u32[]{:S(2)}, u32[]{:S(2)}) collective-permute-start(bf16[64,2304]{1,0:T(8,128)(2,1)S(1)} %add_convert_fusion.11), channel_id=1, source_target_pairs={{0,2},{2,4},{4,6},{6,0},{1,3},{3,5},{5,7},{7,1},{8,10},{10,12},{12... | collective-permute-start | bytes 884744 | tf_op jit(solution)/shard_map/ppermute | solution.py:124
  456.2 19.1 %collective-permute-start.62 = (bf16[576,256]{1,0:T(8,128)(2,1)S(1)}, bf16[576,256]{1,0:T(8,128)(2,1)}, u32[]{:S(2)}, u32[]{:S(2)}) collective-permute-start(bf16[576,256]{1,0:T(8,128)(2,1)S(1)} %collective-permute-done.61), channel_id=1, source_target_pairs={{0,2},{2,4},{4,6},{6,0},{1,3},{3,5},{5,7},{7,1},{8,10},{10,12},{12... | collective-permute-start | bytes 884744 | tf_op jit(solution)/shard_map/ppermute | solution.py:124
  462.5 19.0 %collective-permute-start.53 = (bf16[64,2304]{1,0:T(8,128)(2,1)S(1)}, bf16[64,2304]{1,0:T(8,128)(2,1)S(1)}, u32[]{:S(2)}, u32[]{:S(2)}) collective-permute-start(bf16[64,2304]{1,0:T(8,128)(2,1)S(1)} %collective-permute-done.52), channel_id=1, source_target_pairs={{0,2},{2,4},{4,6},{6,0},{1,3},{3,5},{5,7},{7,1},{8,10},{10,12},{12... | collective-permute-start | bytes 884744 | tf_op jit(solution)/shard_map/ppermute | solution.py:124
  468.8 19.0 %collective-permute-start.44 = (bf16[64,2304]{1,0:T(8,128)(2,1)S(1)}, bf16[64,2304]{1,0:T(8,128)(2,1)S(1)}, u32[]{:S(2)}, u32[]{:S(2)}) collective-permute-start(bf16[64,2304]{1,0:T(8,128)(2,1)S(1)} %collective-permute-done.43), channel_id=1, source_target_pairs={{0,2},{2,4},{4,6},{6,0},{1,3},{3,5},{5,7},{7,1},{8,10},{10,12},{12... | collective-permute-start | bytes 884744 | tf_op jit(solution)/shard_map/ppermute | solution.py:124
  475.2 37.8 %collective-permute-start.63 = (bf16[576,256]{1,0:T(8,128)(2,1)}, bf16[576,256]{1,0:T(8,128)(2,1)}, u32[]{:S(2)}, u32[]{:S(2)}) collective-permute-start(bf16[576,256]{1,0:T(8,128)(2,1)} %collective-permute-done.62), channel_id=1, source_target_pairs={{0,2},{2,4},{4,6},{6,0},{1,3},{3,5},{5,7},{7,1},{8,10},{10,12},{12... | collective-permute-start | bytes 884744 | tf_op jit(solution)/shard_map/ppermute | solution.py:124
  481.4 19.0 %collective-permute-start.54 = (bf16[64,2304]{1,0:T(8,128)(2,1)S(1)}, bf16[64,2304]{1,0:T(8,128)(2,1)S(1)}, u32[]{:S(2)}, u32[]{:S(2)}) collective-permute-start(bf16[64,2304]{1,0:T(8,128)(2,1)S(1)} %collective-permute-done.53), channel_id=1, source_target_pairs={{0,2},{2,4},{4,6},{6,0},{1,3},{3,5},{5,7},{7,1},{8,10},{10,12},{12... | collective-permute-start | bytes 884744 | tf_op jit(solution)/shard_map/ppermute | solution.py:124
  525.6 23.8 %collective-permute-start.18 = (bf16[512,1024]{1,0:T(8,128)(2,1)S(1)}, bf16[512,1024]{1,0:T(8,128)(2,1)S(1)}, u32[]{:S(2)}, u32[]{:S(2)}) collective-permute-start(bf16[512,1024]{1,0:T(8,128)(2,1)S(1)} %fusion.9), channel_id=1, source_target_pairs={{0,1},{1,0},{2,3},{3,2},{4,5},{5,4},{6,7},{7,6},{8,9},{9,8},{10,11... | collective-permute-start | bytes 3145736 | tf_op jit(solution)/shard_map/ppermute | solution.py:55
  (70 other events, 520.2 us)
Sparse Core Ops, SparseCore 0:
  51.5 47.1 all-gather.1
  331.0 72.1 reduce-scatter.1

commit v2 on v1

--- a/solution.py
+++ b/solution.py
@@ -104,26 +104,31 @@
     return held[0]
 
 
+def summed(block):
+    return lax.psum(block.astype(jnp.bfloat16), "ctx").astype(jnp.float32)
+
+
 def over_ctx(block):
     count = lax.axis_size("ctx")
     place = lax.axis_index("ctx")
     rows = block.shape[0] // count
-    ring = [(i, (i + 1) % count) for i in range(count)]
+
+    def away(shift):
+        return [(i, (i + shift) % count) for i in range(count)]
 
     def chunk(index):
         return lax.dynamic_slice_in_dim(block, (index % count) * rows, rows, 0)
 
-    running = chunk(place + count)
-    for step in range(1, count):
-        arrived = lax.ppermute(running.astype(jnp.bfloat16), "ctx", ring)
-        running = arrived.astype(jnp.float32) + chunk(place + count - step)
+    running = chunk(place)
+    for shift in range(1, count):
+        sent = chunk(place + shift).astype(jnp.bfloat16)
+        running = running + lax.ppermute(sent, "ctx", away(shift)).astype(jnp.float32)
     held = keep_low(running)
     full = jnp.zeros(block.shape, jnp.float32)
-    for step in range(count):
-        if step:
-            held = lax.ppermute(held, "ctx", ring)
+    for shift in range(count):
+        piece = lax.ppermute(held, "ctx", away(shift)) if shift else held
         full = lax.dynamic_update_slice_in_dim(
-            full, held.astype(jnp.float32), ((place + 1 + count - step) % count) * rows, 0
+            full, piece.astype(jnp.float32), ((place + count - shift) % count) * rows, 0
         )
     return full
 
@@ -145,16 +150,29 @@
 LAST = (((1,), (1,)), ((), ()))
 
 
-def attend_kernel(start_ref, place_ref, query_ref, key_ref, value_t_ref, out_ref, log_ref):
-    scores = lax.dot_general(key_ref[0], query_ref[0], LAST, preferred_element_type=jnp.float32)
-    scores = jnp.where(visible_keys(start_ref, place_ref, key_ref.shape[1]), scores, -1e30)
-    row_max = jnp.max(scores, axis=0, keepdims=True)
-    exponent = jnp.exp(scores - row_max)
-    row_total = jnp.sum(exponent, axis=0, keepdims=True)
-    weights_soft = (exponent * (1.0 / row_total)).astype(jnp.bfloat16)
-    attended = jnp.dot(value_t_ref[0], weights_soft, preferred_element_type=jnp.float32)
-    out_ref[0] = attended.T.astype(jnp.bfloat16)
-    log_ref[0] = row_max + jnp.log(row_total)
+def hidden_bias(start_ref, place_ref, key_count):
+    return jnp.where(visible_keys(start_ref, place_ref, key_count), 0.0, -1e30)
+
+
+def head(ref, at):
+    return ref[0, :, at * HD : (at + 1) * HD]
+
+
+def attend_kernel(start_ref, place_ref, query_ref, key_ref, value_ref, out_ref, log_ref):
+    bias = hidden_bias(start_ref, place_ref, key_ref.shape[1])
+    per_group = log_ref.shape[1] // 2
+    results = []
+    for group in range(2):
+        key, value = head(key_ref, group), head(value_ref, group)
+        for at in range(group * per_group, (group + 1) * per_group):
+            scores = dot_nt(key, head(query_ref, at)) + bias
+            row_max = jnp.max(scores, axis=0, keepdims=True)
+            exponent = jnp.exp(scores - row_max)
+            row_total = jnp.sum(exponent, axis=0, keepdims=True)
+            attended = dot_tn(value, exponent.astype(jnp.bfloat16))
+            results.append(attended * (1.0 / row_total))
+            log_ref[0, at : at + 1, :] = row_max + jnp.log(row_total)
+    out_ref[0] = jnp.concatenate(results, axis=0).T.astype(jnp.bfloat16)
 
 
 def back_kernel(
@@ -163,7 +181,6 @@
     query_ref,
     grad_ref,
     key_ref,
-    key_t_ref,
     value_ref,
     log_ref,
     grad_query_ref,
@@ -179,20 +196,28 @@
         key_total[...] = jnp.zeros_like(key_total)
         value_total[...] = jnp.zeros_like(value_total)
 
-    query = query_ref[0]
-    grad = grad_ref[0]
-    scores = lax.dot_general(key_ref[0], query, LAST, preferred_element_type=jnp.float32)
-    scores = jnp.where(visible_keys(start_ref, place_ref, key_ref.shape[1]), scores, -1e30)
-    weights_soft = jnp.exp(scores - log_ref[0])
-    grad_soft = lax.dot_general(value_ref[0], grad, LAST, preferred_element_type=jnp.float32)
-    delta = jnp.sum(weights_soft * grad_soft, axis=0, keepdims=True)
-    grad_scores = (weights_soft * (grad_soft - delta)).astype(jnp.bfloat16)
-    grad_query = jnp.dot(key_t_ref[0], grad_scores, preferred_element_type=jnp.float32)
-    grad_query_ref[0] = (grad_query * HD ** (-0.5)).T.astype(jnp.bfloat16)
-    key_total[...] += jnp.dot(grad_scores, query, preferred_element_type=jnp.float32)
-    value_total[...] += jnp.dot(
-        weights_soft.astype(jnp.bfloat16), grad, preferred_element_type=jnp.float32
-    )
+    bias = hidden_bias(start_ref, place_ref, key_ref.shape[1])
+    per_group = log_ref.shape[1] // 2
+    results = []
+    for group in range(2):
+        key, value = head(key_ref, group), head(value_ref, group)
+        key_part, value_part = 0.0, 0.0
+        for at in range(group * per_group, (group + 1) * per_group):
+            query, grad = head(query_ref, at), head(grad_ref, at)
+            scores = dot_nt(key, query) + bias
+            weights_soft = jnp.exp(scores - log_ref[0, at : at + 1, :])
+            grad_soft = dot_nt(value, grad)
+            delta = jnp.sum(weights_soft * grad_soft, axis=0, keepdims=True)
+            grad_scores = (weights_soft * (grad_soft - delta)).astype(jnp.bfloat16)
+            results.append(dot_tn(key, grad_scores) * HD ** (-0.5))
+            key_part += jnp.dot(grad_scores, query, preferred_element_type=jnp.float32)
+            value_part += jnp.dot(
+                weights_soft.astype(jnp.bfloat16), grad, preferred_element_type=jnp.float32
+            )
+        lanes = slice(group * HD, (group + 1) * HD)
+        key_total[:, lanes] += key_part
+        value_total[:, lanes] += value_part
+    grad_query_ref[0] = jnp.concatenate(results, axis=0).T.astype(jnp.bfloat16)
 
     @pl.when(tile == pl.num_programs(1) - 1)
     def _():
@@ -200,68 +225,69 @@
         grad_value_ref[0] = value_total[...].astype(jnp.bfloat16)
 
 
-def attention_specs(groups, tok_rows, key_count, tile):
-    per_token = tok_rows // tile
-    row = pl.BlockSpec((1, 1, tile), lambda i, j: (i // groups, 0, j % per_token))
-    query = pl.BlockSpec((1, tile, HD), lambda i, j: (i, j, 0))
-    key = pl.BlockSpec((1, key_count, HD), lambda i, j: (i, 0, 0))
-    key_t = pl.BlockSpec((1, HD, key_count), lambda i, j: (i, 0, 0))
-    log = pl.BlockSpec((1, 1, tile), lambda i, j: (i, 0, j))
-    return row, query, key, key_t, log
-
-
-def cost(items, rows, key_count, dots):
+def attention_specs(halves, per_pair, key_count, tile):
+    row = pl.BlockSpec((1, 1, tile), lambda i, j: (i // halves, 0, j))
+    query = pl.BlockSpec((1, tile, per_pair * HD), lambda i, j: (i // halves, j, i % halves))
+    key = pl.BlockSpec((1, key_count, 2 * HD), lambda i, j: (i // halves, 0, i % halves))
+    value = pl.BlockSpec((1, key_count, 2 * HD), lambda i, j: (i // halves, 0, halves + i % halves))
+    log = pl.BlockSpec((1, per_pair, tile), lambda i, j: (i, 0, j))
+    return row, query, key, value, log
+
+
+def cost(queries, key_count, weight):
     return pl.CostEstimate(
-        flops=2 * dots * items * rows * key_count * HD,
-        bytes_accessed=4 * items * (rows + key_count) * HD,
-        transcendentals=items * rows * key_count,
+        flops=weight * queries.size * key_count, bytes_accessed=queries.size * 8, transcendentals=0
     )
 
 
 PARAMS = pltpu.CompilerParams(vmem_limit_bytes=50 * 1024 * 1024)
 
 
-def attend(start, place, queries, keys, values_t, groups):
-    items, rows, _ = queries.shape
-    key_count = keys.shape[1]
-    tile = min(256, start.shape[-1])
-    row, query, key, key_t, log = attention_specs(groups, start.shape[-1], key_count, tile)
+def attend(start, place, queries, all_kv, groups):
+    packs, rows, q_width = queries.shape
+    key_count = all_kv.shape[1]
+    tile = min(256, rows)
+    halves = groups // 2
+    per_pair = q_width // HD // halves
+    row, query, key, value, log = attention_specs(halves, per_pair, key_count, tile)
     return pl.pallas_call(
         attend_kernel,
-        grid=(items, rows // tile),
-        in_specs=[row, row, query, key, key_t],
+        grid=(packs * halves, rows // tile),
+        in_specs=[row, row, query, key, value],
         out_specs=[query, log],
         out_shape=[
-            jax.ShapeDtypeStruct((items, rows, HD), jnp.bfloat16),
-            jax.ShapeDtypeStruct((items, 1, rows), jnp.float32),
+            jax.ShapeDtypeStruct(queries.shape, jnp.bfloat16),
+            jax.ShapeDtypeStruct((packs * halves, per_pair, rows), jnp.float32),
         ],
         compiler_params=PARAMS,
-        cost_estimate=cost(items, rows, key_count, 2),
-    )(start, place, queries, keys, values_t)
-
-
-def attend_back(start, place, queries, grads, keys, keys_t, values, log_total, groups):
-    items, rows, _ = queries.shape
-    key_count = keys.shape[1]
-    tile = min(256, start.shape[-1])
-    row, query, key, key_t, log = attention_specs(groups, start.shape[-1], key_count, tile)
+        cost_estimate=cost(queries, key_count, 50),
+    )(start, place, queries, all_kv, all_kv)
+
+
+def attend_back(start, place, queries, grads, all_kv, log_total, groups):
+    packs, rows, q_width = queries.shape
+    key_count = all_kv.shape[1]
+    tile = min(256, rows)
+    halves = groups // 2
+    per_pair = q_width // HD // halves
+    row, query, key, value, log = attention_specs(halves, per_pair, key_count, tile)
     return pl.pallas_call(
         back_kernel,
-        grid=(items, rows // tile),
-        in_specs=[row, row, query, query, key, key_t, key, log],
+        grid=(packs * halves, rows // tile),
+        in_specs=[row, row, query, query, key, value, log],
         out_specs=[query, key, key],
         out_shape=[
-            jax.ShapeDtypeStruct((items, rows, HD), jnp.bfloat16),
-            jax.ShapeDtypeStruct((items, key_count, HD), jnp.bfloat16),
-            jax.ShapeDtypeStruct((items, key_count, HD), jnp.bfloat16),
+            jax.ShapeDtypeStruct(queries.shape, jnp.bfloat16),
+            jax.ShapeDtypeStruct((packs, key_count, groups * HD), jnp.bfloat16),
+            jax.ShapeDtypeStruct((packs, key_count, groups * HD), jnp.bfloat16),
         ],
         scratch_shapes=[
-            pltpu.VMEM((key_count, HD), jnp.float32),
-            pltpu.VMEM((key_count, HD), jnp.float32),
+            pltpu.VMEM((key_count, 2 * HD), jnp.float32),
+            pltpu.VMEM((key_count, 2 * HD), jnp.float32),
         ],
         compiler_params=PARAMS,
-        cost_estimate=cost(items, rows, key_count, 5),
-    )(start, place, queries, grads, keys, keys_t, values, log_total)
+        cost_estimate=cost(queries, key_count, 80),
+    )(start, place, queries, grads, all_kv, all_kv, log_total)
 
 
 def dot_nt(left, right):
@@ -299,7 +325,6 @@
     units = gate_weight.shape[1]
     groups = k_width // HD
     heads = q_width // HD
-    per_group = heads // groups
     qkv_shard = jnp.concatenate([query_weight, key_weight, value_weight], axis=1)
     full_qkv = gather(qkv_shard, 0)
     full_out = gather(out_weight, 1)
@@ -333,29 +358,9 @@
     all_kv = lax.all_gather(
         jnp.concatenate([keys_low, value_low], axis=-1), "ctx", axis=1, tiled=True
     )
-    kv_items = all_kv.reshape(pack_count, pack_len, 2, groups, HD)
-    kv_items = jnp.transpose(kv_items, (2, 0, 3, 1, 4)).reshape(
-        2, pack_count * groups, pack_len, HD
-    )
-    key_items, value_items = kv_items[0], kv_items[1]
-    key_t_items = jnp.swapaxes(key_items, 1, 2)
-    value_t_items = jnp.swapaxes(value_items, 1, 2)
-
-    def to_rows(values):
-        split = values.reshape(pack_count, tok_rows, groups, per_group, HD)
-        return jnp.transpose(split, (0, 2, 3, 1, 4)).reshape(
-            pack_count * groups, per_group * tok_rows, HD
-        )
-
-    def from_rows(values):
-        split = values.reshape(pack_count, groups, per_group, tok_rows, HD)
-        return jnp.transpose(split, (0, 3, 1, 2, 4)).reshape(total_rows, heads * HD)
-
-    query_items = to_rows((queries * HD ** (-0.5)).astype(jnp.bfloat16))
-    attended_items, log_total = attend(
-        start_rows, place_rows, query_items, key_items, value_t_items, groups
-    )
-    attended = from_rows(attended_items)
+    query_rows = (queries * HD ** (-0.5)).astype(jnp.bfloat16).reshape(pack_count, tok_rows, q_width)
+    attended_rows, log_total = attend(start_rows, place_rows, query_rows, all_kv, groups)
+    attended = attended_rows.reshape(total_rows, q_width)
     attn_part = jnp.dot(attended, full_out, preferred_element_type=jnp.float32)
     after_attn = inputs + both(attn_part)
     normed_ffn = rms_norm(after_attn, ffn_gain).astype(jnp.bfloat16)
@@ -371,9 +376,8 @@
 
     down_extent = down_weight.shape[1]
     row_extent = gate_weight.shape[0]
-    share_down = over_ctx(
-        reduce_blocks(lambda b: dot_tn(hidden, columns(cotangent, b, down_extent)))
-    )
+    held_down = reduce_blocks(lambda b: dot_tn(hidden, columns(cotangent, b, down_extent)))
+    held_down = held_down.astype(jnp.bfloat16)
     grad_hidden = dot_nt(cotangent, full_down)
     grad_gate_proj, grad_up_proj = swiglu_pull(grad_hidden)
     grad_gate_proj = grad_gate_proj.astype(jnp.bfloat16)
@@ -381,40 +385,43 @@
     grad_normed_ffn = dot_nt(grad_gate_proj, full_gate) + dot_nt(grad_up_proj, full_up)
     unused_ffn, ffn_pull = jax.vjp(rms_norm, after_attn, ffn_gain)
     grad_after_part, grad_ffn_gain = ffn_pull(grad_normed_ffn)
-    grad_after = cotangent.astype(jnp.float32) + both(grad_after_part)
-    ffn_out = both(jnp.dot(hidden, full_down, preferred_element_type=jnp.float32))
-    mixed = (after_attn + ffn_out).astype(jnp.bfloat16)
-    share_gate = over_ctx(
-        reduce_blocks(lambda b: dot_tn(columns(normed_ffn, b, row_extent), grad_gate_proj))
-    )
-    share_up = over_ctx(
-        reduce_blocks(lambda b: dot_tn(columns(normed_ffn, b, row_extent), grad_up_proj))
-    )
+    grad_after_sum, held_down = lax.optimization_barrier((both(grad_after_part), held_down))
+    share_down = summed(held_down)
+    grad_after = cotangent.astype(jnp.float32) + grad_after_sum
     grad_after_low = grad_after.astype(jnp.bfloat16)
+    ffn_part = jnp.dot(hidden, full_down, preferred_element_type=jnp.float32)
+    ffn_part, grad_after_low = lax.optimization_barrier(
+        (ffn_part.astype(jnp.bfloat16), grad_after_low)
+    )
+    mixed = (after_attn + both(ffn_part)).astype(jnp.bfloat16)
+    held_gate = reduce_blocks(lambda b: dot_tn(columns(normed_ffn, b, row_extent), grad_gate_proj))
+    held_gate = held_gate.astype(jnp.bfloat16)
+    held_up = reduce_blocks(lambda b: dot_tn(columns(normed_ffn, b, row_extent), grad_up_proj))
+    held_up = held_up.astype(jnp.bfloat16)
     grad_attended = dot_nt(grad_after_low, full_out).astype(jnp.bfloat16)
+    grad_attended, held_gate = lax.optimization_barrier((grad_attended, held_gate))
+    held_gate, share_down = lax.optimization_barrier((held_gate, share_down))
+    share_gate = summed(held_gate)
     share_out = over_ctx(
         reduce_blocks(lambda b: dot_tn(attended, columns(grad_after_low, b, down_extent)))
     )
-    grad_q_items, grad_k_items, grad_v_items = attend_back(
+    grad_q_rows, grad_k_rows, grad_v_rows = attend_back(
         start_rows,
         place_rows,
-        query_items,
-        to_rows(grad_attended),
-        key_items,
-        key_t_items,
-        value_items,
+        query_rows,
+        grad_attended.reshape(pack_count, tok_rows, q_width),
+        all_kv,
         log_total,
         groups,
     )
-    grad_kv = jnp.stack([grad_k_items, grad_v_items]).reshape(
-        2, pack_count, groups, pack_len, HD
-    )
-    grad_kv = jnp.transpose(grad_kv, (1, 3, 0, 2, 4)).reshape(pack_count, pack_len, 2 * k_width)
+    grad_kv = jnp.concatenate([grad_k_rows, grad_v_rows], axis=-1)
+    grad_kv, share_gate = lax.optimization_barrier((grad_kv, share_gate))
     own_kv = lax.psum_scatter(grad_kv, "ctx", scatter_dimension=1, tiled=True)
-    own_kv = lax.optimization_barrier(own_kv.astype(jnp.bfloat16))
+    own_kv, held_up = lax.optimization_barrier((own_kv.astype(jnp.bfloat16), held_up))
+    share_up = summed(held_up)
     grad_keys = own_kv[..., :k_width].reshape(pack_count, tok_rows, groups, HD)
     grad_value_low = own_kv[..., k_width:].reshape(total_rows, k_width)
-    grad_queries = from_rows(grad_q_items).reshape(pack_count, tok_rows, heads, HD)
+    grad_queries = grad_q_rows.reshape(pack_count, tok_rows, heads, HD)
     grad_query_proj, grad_query_gain = query_pull(grad_queries.astype(jnp.float32))
     grad_key_proj, grad_key_gain = key_pull(grad_keys.astype(jnp.float32))
     grad_qkv = jnp.concatenate(

time: 596 us -> 530 us (0.89)
  waiting for transfers between devices: 255 us -> 228 us
  local copies, waits for them, and re-layouts: 83.3 us -> 58.3 us
  Pallas kernels: 66.9 us -> 54.2 us
  starting transfers between devices: 48.4 us -> 60.8 us
  other arithmetic: 47.6 us -> 39 us
    ppermute x30 -> x12, waiting for transfers between devices: 142 us -> 24.3 us  [the longest x6 15.9 us: over_ctx(): lax.ppermute(sent, 'ctx', away(shift)).astype(jnp.float32)]
    psum x0 -> x3, waiting for transfers between devices: none -> 74.1 us  [summed(): return lax.psum(block.astype(jnp.bfloat16), 'ctx').astype(jnp.float32)]
    ppermute x15, waiting for transfers between devices: 22.3 us -> 41.5 us  [reduce_blocks(): lax.ppermute(block.astype(jnp.bfloat16), 'fsdp', pairs('fsdp', step))]
    convert_element_type x12 -> x7, other arithmetic: 2.88 us -> 16.4 us  [the longest x3 8.51 us: summed(): return lax.psum(block.astype(jnp.bfloat16), 'ctx').astype(jnp.float32)]
    pallas_call x2, Pallas kernels: 66.9 us -> 54.2 us  [the longest x1 32.2 us: attend_back(): pl.pallas_call(back_kernel, grid=(packs * halves, rows // tile), in_specs...]
    dynamic_update_slice x20 -> x8, other arithmetic: 12.3 us -> 0.16 us  [over_ctx(): lax.dynamic_update_slice_in_dim(full, piece.astype(jnp.float32), (place +...]
    transpose x3 -> x0, local copies, waits for them, and re-layouts: 9.63 us -> none  [the longest x1 4.95 us: shards(): jnp.transpose(grad_kv, (1, 3, 0, 2, 4))]
    ppermute x4, waiting for transfers between devices: 33.4 us -> 24.9 us  [both(): other = lax.ppermute(total, 'tp', pairs('tp', step))]
  transfers between devices with their start and end apart: 71 -> 56, of which waited for: 32 -> 21; matrix products, arithmetic and copies ran while one was open for 27% -> 22% of each run, Pallas kernels for 11% -> 10%
where the time goes in v2:
time: 530 us; the launch traced here: 521 us
  waiting for transfers between devices  228 us (43%)
  matrix products  65.4 us (12%)
  starting transfers between devices  60.8 us (11%)
  local copies, waits for them, and re-layouts  58.3 us (11%)
  Pallas kernels  54.2 us (10%)
  other arithmetic  39 us (7%)
  between operations  15.6 us (3%)
    psum x3, waiting for transfers between devices, summed(): return lax.psum(block.astype(jnp.bfloat16), 'ctx').astype(jnp.float32)  74.1 us
    ppermute x15, waiting for transfers between devices, gather(): lax.ppermute(piece, 'fsdp', pairs('fsdp', step))  53.6 us
    ppermute x15, waiting for transfers between devices, reduce_blocks(): lax.ppermute(block.astype(jnp.bfloat16), 'fsdp', pairs('fsdp', step))  41.5 us
    pallas_call x1, Pallas kernels, attend_back(): pl.pallas_call(back_kernel, grid=(packs * halves, rows // tile), in_specs...  32.2 us
    ppermute x4, waiting for transfers between devices, both(): other = lax.ppermute(total, 'tp', pairs('tp', step))  24.9 us
    dot_general x20, matrix products, dot_tn(): lax.dot_general(left, right, (((0,), (0,)), ((), ())), preferred_element_...  23.8 us
    dynamic_update_slice x15, local copies, waits for them, and re-layouts, gather(): lax.dynamic_update_slice_in_dim(full, piece, (mine ^ p) * extent, axis)  23.3 us
    pallas_call x1, Pallas kernels, attend(): pl.pallas_call(attend_kernel, grid=(packs * halves, rows // tile), in_spe...  22 us
  transfers between devices with their start and end apart: 56, of which 21 were waited for; matrix products, arithmetic and copies ran while one was open for 22% of the time, Pallas kernels for 10%

profile of v2, /device:TPU:0, one launch (start us, length us, event | category | flops | bytes accessed | tf_op | source)
XLA Modules:
  0.0 521.2 jit_solution(7849108060229438663)
XLA Ops:
  10.2 3.0 collective-permute-start
  19.0 12.7 %collective-permute-done.3 = bf16[512,256]{1,0:T(8,128)(2,1)} collective-permute-done((bf16[512,256]{1,0:T(8,128)(2,1)}, bf16[512,256]{1,0:T(8,128)(2,1)}, u32[]{:S(2)}, u32[]{:S(2)}) %collective-permute-start.3) | collective-permute-done | bytes 262176 | tf_op jit(solution)/shard_map/ppermute | solution.py:70
  33.3 2.9 tile.53
  36.3 3.7 copy.48
  57.3 3.8 tile.51
  61.1 2.4 constant_dynamic-update-slice_fusion.5
  63.5 18.8 %collective-permute-done.13 = bf16[2304,256]{1,0:T(8,128)(2,1)} collective-permute-done((bf16[2304,256]{1,0:T(8,128)(2,1)}, bf16[2304,256]{1,0:T(8,128)(2,1)}, u32[]{:S(2)}, u32[]{:S(2)}) %collective-permute-start.13) | collective-permute-done | bytes 1179680 | tf_op jit(solution)/shard_map/ppermute | solution.py:70
  82.3 2.4 constant_dynamic-update-slice_fusion.2
  84.7 22.1 %collective-permute-done.7 = bf16[256,2304]{1,0:T(8,128)(2,1)} collective-permute-done((bf16[256,2304]{1,0:T(8,128)(2,1)}, bf16[256,2304]{1,0:T(8,128)(2,1)}, u32[]{:S(2)}, u32[]{:S(2)}) %collective-permute-start.7) | collective-permute-done | bytes 1179680 | tf_op jit(solution)/shard_map/ppermute | solution.py:70
  106.7 3.8 tile.24
  113.4 2.4 constant_dynamic-update-slice_fusion.4
  115.8 2.4 constant_dynamic-update-slice_fusion.1
  122.1 22.0 %shard_map.237 = (bf16[1,512,512]{2,1,0:T(8,128)(2,1)S(1)}, f32[2,4,512]{2,1,0:T(4,128)S(1)}) custom-call(s32[1,1,512]{2,1,0:T(1,128)S(1)} %bitcast.103, s32[1,1,512]{2,1,0:T(1,128)S(1)} %iota_add_fusion.place_ref, bf16[1,512,512]{2,1,0:T(8,128)(2,1)S(1)} %copy.40.query_ref, bf16[1,2048,512]{2,1,0:T(8,128)(2,1)S(1)} %copy-done.2, ...), custom_call_target="tpu_custom_call" | custom-call | flops 26843545600 | bytes 2097152 | tf_op jit(solution)/shard_map/pallas_call | solution.py:253
  146.7 2.4 constant_dynamic-update-slice_fusion
  149.1 2.4 constant_dynamic-update-slice_fusion.6
  151.5 5.0 convolution_bitcast_fusion
  156.5 13.5 %collective-permute-done.6 = bf16[512,1024]{1,0:T(8,128)(2,1)S(1)} collective-permute-done((bf16[512,1024]{1,0:T(8,128)(2,1)S(1)}, bf16[512,1024]{1,0:T(8,128)(2,1)S(1)}, u32[]{:S(2)}, u32[]{:S(2)}) %collective-permute-start.6) | collective-permute-done | bytes 1048608 | tf_op jit(solution)/shard_map/ppermute | solution.py:55
  170.8 5.4 %fusion.98 = f32[512,2304]{1,0:T(8,128)S(1)} fusion(bf16[512,1024]{1,0:T(8,128)(2,1)S(1)} %multiply_convert_fusion.2, bf16[1024,2304]{1,0:T(8,128)(2,1)} %constant_dynamic-update-slice_fusion.3), kind=kOutput, calls=%fused_computation.208 | convolution fusion | flops 2415919104 | bytes 10485760 | tf_op jit(solution)/shard_map/dot_general | solution.py:368
  176.3 7.3 %fusion.2 = (bf16[512,2304]{1,0:T(8,128)(2,1)S(1)}, bf16[512,2304]{1,0:T(8,128)(2,1)S(1)}, bf16[512,2304]{1,0:T(8,128)(2,1)S(1)}) fusion(f32[512,2304]{1,0:T(8,128)S(1)} %convolution_bitcast_fusion, f32[512,2304]{1,0:T(8,128)S(1)} %fusion.98, bf16[512,1024]{1,0:T(8,128)(2,1)S(1)} %multiply_convert_fusion.2, ...), kind=kOutput, calls=%fused_computation.4 | convolution fusion | flops 2434793472 | bytes 22282240 | tf_op jit(solution)/shard_map/dot_general | solution.py:367
  189.1 4.5 fusion.99
  195.9 5.1 multiply_reduce_fusion
  203.2 6.0 %convolution_convert_fusion.6 = bf16[512,1024]{1,0:T(8,128)(2,1)} fusion(bf16[512,2304]{1,0:T(8,128)(2,1)S(1)} %get-tuple-element.59, bf16[2304,1024]{1,0:T(8,128)(2,1)} %constant_dynamic-update-slice_fusion), kind=kOutput, calls=%fused_computation.48 | convolution fusion | flops 2416443392 | bytes 8126464 | tf_op jit(solution)/shard_map/dot_general | solution.py:392
  217.0 10.1 %collective-permute-done.16 = bf16[512,1024]{1,0:T(8,128)(2,1)S(1)} collective-permute-done((bf16[512,1024]{1,0:T(8,128)(2,1)S(1)}, bf16[512,1024]{1,0:T(8,128)(2,1)S(1)}, u32[]{:S(2)}, u32[]{:S(2)}) %collective-permute-start.16) | collective-permute-done | bytes 1048608 | tf_op jit(solution)/shard_map/ppermute | solution.py:55
  233.8 8.6 %collective-permute-done.19 = bf16[2304,256]{1,0:T(8,128)(2,1)S(1)} collective-permute-done((bf16[2304,256]{1,0:T(8,128)(2,1)S(1)}, bf16[2304,256]{1,0:T(8,128)(2,1)S(1)}, u32[]{:S(2)}, u32[]{:S(2)}) %collective-permute-start.19) | collective-permute-done | bytes 1179680 | tf_op jit(solution)/shard_map/ppermute | solution.py:94
  248.1 19.6 %collective-permute-done.23 = bf16[256,2304]{1,0:T(8,128)(2,1)} collective-permute-done((bf16[256,2304]{1,0:T(8,128)(2,1)}, bf16[256,2304]{1,0:T(8,128)(2,1)}, u32[]{:S(2)}, u32[]{:S(2)}) %collective-permute-start.23) | collective-permute-done | bytes 1179680 | tf_op jit(solution)/shard_map/ppermute | solution.py:94
  267.7 3.1 add_convert_fusion.2
  270.8 29.5 %all-reduce.8.cloned.1.call-done = bf16[2304,256]{1,0:T(8,128)(2,1)} async-done(((bf16[2304,256]{1,0:T(8,128)(2,1)}), bf16[2304,256]{1,0:T(8,128)(2,1)}) %all-reduce.8.cloned.1.call-update) | async-done | bytes 1179664 | tf_op jit(solution)/shard_map/psum | solution.py:108
  300.3 2.9 convert_element_type.370
  305.3 32.2 %shard_map.238 = (bf16[1,512,512]{2,1,0:T(8,128)(2,1)S(1)}, bf16[1,2048,256]{2,1,0:T(8,128)(2,1)S(1)}, bf16[1,2048,256]{2,1,0:T(8,128)(2,1)S(1)}) custom-call(s32[1,1,512]{2,1,0:T(1,128)S(1)} %bitcast.104, s32[1,1,512]{2,1,0:T(1,128)S(1)} %iota_add_fusion.place_ref, bf16[1,512,512]{2,1,0:T(8,128)(2,1)S(1)} %copy-done.1, bf16[1,512,512]{2,1,0:T(8,128)(2,1)S(1)} %bitcast.105, ...), custom_call_target="tpu_custom_call" | custom-call | flops 42949672960 | bytes 2097152 | tf_op jit(solution)/shard_map/pallas_call | solution.py:274
  342.4 16.3 %all-reduce.10.cloned.1.call-done = bf16[256,2304]{1,0:T(8,128)(2,1)} async-done(((bf16[256,2304]{1,0:T(8,128)(2,1)}), bf16[256,2304]{1,0:T(8,128)(2,1)}) %all-reduce.10.cloned.1.call-update) | async-done | bytes 1179664 | tf_op jit(solution)/shard_map/psum | solution.py:108
  358.8 2.8 convert_element_type.371
  369.4 5.5 %collective-permute-done.39 = bf16[512,256]{1,0:T(8,128)(2,1)S(1)} collective-permute-done((bf16[512,256]{1,0:T(8,128)(2,1)S(1)}, bf16[512,256]{1,0:T(8,128)(2,1)S(1)}, u32[]{:S(2)}, u32[]{:S(2)}) %collective-permute-start.39) | collective-permute-done | bytes 262176 | tf_op jit(solution)/shard_map/ppermute | solution.py:94
  377.5 2.4 collective-permute-start.42
  379.9 3.2 add_convert_fusion
  383.1 4.8 collective-permute-done.41
  387.9 4.7 collective-permute-start.43
  395.3 2.9 collective-permute-done.43
  398.2 5.5 %collective-permute-done.44 = bf16[128,256]{1,0:T(8,128)(2,1)S(1)} collective-permute-done((bf16[128,256]{1,0:T(8,128)(2,1)S(1)}, bf16[128,256]{1,0:T(8,128)(2,1)S(1)}, u32[]{:S(2)}, u32[]{:S(2)}) %collective-permute-start.44) | collective-permute-done | bytes 65568 | tf_op jit(solution)/shard_map/ppermute | solution.py:129
  403.8 3.2 fusion.14
  407.0 6.4 %reduce-scatter.2.cloned.1.call-done = bf16[1,512,512]{2,1,0:T(8,128)(2,1)} async-done(((bf16[1,2048,512]{2,1,0:T(8,128)(2,1)}), bf16[1,512,512]{2,1,0:T(8,128)(2,1)}) %reduce-scatter.2.cloned.1.call-update) | async-done | bytes 524304 | tf_op jit(solution)/shard_map/reduce_scatter | solution.py:419
  416.0 4.8 fusion.7
  429.5 3.3 collective-permute-start.49
  442.0 7.8 %collective-permute-done.30 = bf16[256,1024]{1,0:T(8,128)(2,1)} collective-permute-done((bf16[256,1024]{1,0:T(8,128)(2,1)}, bf16[256,1024]{1,0:T(8,128)(2,1)}, u32[]{:S(2)}, u32[]{:S(2)}) %collective-permute-start.30) | collective-permute-done | bytes 524320 | tf_op jit(solution)/shard_map/ppermute | solution.py:94
  459.5 2.8 collective-permute-done.31
  462.3 8.4 %collective-permute-done.32 = bf16[64,1024]{1,0:T(8,128)(2,1)S(1)} collective-permute-done((bf16[64,1024]{1,0:T(8,128)(2,1)S(1)}, bf16[64,1024]{1,0:T(8,128)(2,1)S(1)}, u32[]{:S(2)}, u32[]{:S(2)}) %collective-permute-start.32) | collective-permute-done | bytes 131104 | tf_op jit(solution)/shard_map/ppermute | solution.py:125
  470.7 8.1 %collective-permute-start.34 = (bf16[64,1024]{1,0:T(8,128)(2,1)S(1)}, bf16[64,1024]{1,0:T(8,128)(2,1)S(1)}, u32[]{:S(2)}, u32[]{:S(2)}) collective-permute-start(bf16[64,1024]{1,0:T(8,128)(2,1)S(1)} %add_convert_fusion.9), channel_id=1, source_target_pairs={{0,2},{2,4},{4,6},{6,0},{1,3},{3,5},{5,7},{7,1},{8,10},{10,12},{12... | collective-permute-start | bytes 393224 | tf_op jit(solution)/shard_map/ppermute | solution.py:129
  481.3 28.2 %all-reduce.12.cloned.1.call-done = bf16[256,2304]{1,0:T(8,128)(2,1)} async-done(((bf16[256,2304]{1,0:T(8,128)(2,1)}), bf16[256,2304]{1,0:T(8,128)(2,1)}) %all-reduce.12.cloned.1.call-update) | async-done | bytes 1179664 | tf_op jit(solution)/shard_map/psum | solution.py:108
  509.5 2.8 convert_element_type.420
  (333 shorter events, 121.8 us)
Async XLA Ops:
  7.2 113.3 %all-gather.2.cloned.1.call-start = ((), (), s32[]{:S(2)}) async-start(), calls=%async_computation.1 | async-start | bytes 2621440 | tf_op jit(solution)/shard_map/all_gather | solution.py:358
  10.2 29.8 %collective-permute-start = (bf16[256,1024]{1,0:T(8,128)(2,1)S(1)}, bf16[256,1024]{1,0:T(8,128)(2,1)S(1)}, u32[]{:S(2)}, u32[]{:S(2)}) collective-permute-start(bf16[256,1024]{1,0:T(8,128)(2,1)S(1)} %constant_dynamic-update-slice_fusion.15), channel_id=1, source_target_pairs={{0,16},{8,24},{16,0},{24,8},{1,17},{9,25},{17,1},{25,9},{2,18},{10... | collective-permute-start | bytes 1572872 | tf_op jit(solution)/shard_map/ppermute | solution.py:70
  13.2 33.8 %collective-permute-start.1 = (bf16[256,1024]{1,0:T(8,128)(2,1)S(1)}, bf16[256,1024]{1,0:T(8,128)(2,1)}, u32[]{:S(2)}, u32[]{:S(2)}) collective-permute-start(bf16[256,1024]{1,0:T(8,128)(2,1)S(1)} %constant_dynamic-update-slice_fusion.15), channel_id=1, source_target_pairs={{0,8},{8,0},{16,24},{24,16},{1,9},{9,1},{17,25},{25,17},{2,10},{10... | collective-permute-start | bytes 1572872 | tf_op jit(solution)/shard_map/ppermute | solution.py:70
  13.2 18.5 %collective-permute-start.3 = (bf16[512,256]{1,0:T(8,128)(2,1)}, bf16[512,256]{1,0:T(8,128)(2,1)}, u32[]{:S(2)}, u32[]{:S(2)}) collective-permute-start(bf16[512,256]{1,0:T(8,128)(2,1)} %param.19), channel_id=1, source_target_pairs={{0,16},{8,24},{16,0},{24,8},{1,17},{9,25},{17,1},{25,9},{2,18},{10... | collective-permute-start | bytes 786440 | tf_op jit(solution)/shard_map/ppermute | solution.py:70
  13.4 28.0 %collective-permute-start.4 = (bf16[512,256]{1,0:T(8,128)(2,1)}, bf16[512,256]{1,0:T(8,128)(2,1)}, u32[]{:S(2)}, u32[]{:S(2)}) collective-permute-start(bf16[512,256]{1,0:T(8,128)(2,1)} %param.19), channel_id=1, source_target_pairs={{0,8},{8,0},{16,24},{24,16},{1,9},{9,1},{17,25},{25,17},{2,10},{10... | collective-permute-start | bytes 786440 | tf_op jit(solution)/shard_map/ppermute | solution.py:70
  13.8 43.3 %collective-permute-start.10 = (bf16[256,2304]{1,0:T(8,128)(2,1)}, bf16[256,2304]{1,0:T(8,128)(2,1)}, u32[]{:S(2)}, u32[]{:S(2)}) collective-permute-start(bf16[256,2304]{1,0:T(8,128)(2,1)} %param.21), channel_id=1, source_target_pairs={{0,16},{8,24},{16,0},{24,8},{1,17},{9,25},{17,1},{25,9},{2,18},{10... | collective-permute-start | bytes 3538952 | tf_op jit(solution)/shard_map/ppermute | solution.py:70
  31.7 10.8 %collective-permute-start.5 = (bf16[512,256]{1,0:T(8,128)(2,1)}, bf16[512,256]{1,0:T(8,128)(2,1)}, u32[]{:S(2)}, u32[]{:S(2)}) collective-permute-start(bf16[512,256]{1,0:T(8,128)(2,1)} %collective-permute-done.3), channel_id=1, source_target_pairs={{0,8},{8,0},{16,24},{24,16},{1,9},{9,1},{17,25},{25,17},{2,10},{10... | collective-permute-start | bytes 786440 | tf_op jit(solution)/shard_map/ppermute | solution.py:70
  40.0 8.4 %collective-permute-start.2 = (bf16[256,1024]{1,0:T(8,128)(2,1)S(1)}, bf16[256,1024]{1,0:T(8,128)(2,1)S(1)}, u32[]{:S(2)}, u32[]{:S(2)}) collective-permute-start(bf16[256,1024]{1,0:T(8,128)(2,1)S(1)} %collective-permute-done), channel_id=1, source_target_pairs={{0,8},{8,0},{16,24},{24,16},{1,9},{9,1},{17,25},{25,17},{2,10},{10... | collective-permute-start | bytes 1572872 | tf_op jit(solution)/shard_map/ppermute | solution.py:70
  41.4 71.5 %collective-permute-start.11 = (bf16[256,2304]{1,0:T(8,128)(2,1)}, bf16[256,2304]{1,0:T(8,128)(2,1)}, u32[]{:S(2)}, u32[]{:S(2)}) collective-permute-start(bf16[256,2304]{1,0:T(8,128)(2,1)} %param.21), channel_id=1, source_target_pairs={{0,8},{8,0},{16,24},{24,16},{1,9},{9,1},{17,25},{25,17},{2,10},{10... | collective-permute-start | bytes 3538952 | tf_op jit(solution)/shard_map/ppermute | solution.py:70
  42.6 39.7 %collective-permute-start.13 = (bf16[2304,256]{1,0:T(8,128)(2,1)}, bf16[2304,256]{1,0:T(8,128)(2,1)}, u32[]{:S(2)}, u32[]{:S(2)}) collective-permute-start(bf16[2304,256]{1,0:T(8,128)(2,1)} %param.22), channel_id=1, source_target_pairs={{0,16},{8,24},{16,0},{24,8},{1,17},{9,25},{17,1},{25,9},{2,18},{10... | collective-permute-start | bytes 3538952 | tf_op jit(solution)/shard_map/ppermute | solution.py:70
  47.0 68.8 %collective-permute-start.14 = (bf16[2304,256]{1,0:T(8,128)(2,1)}, bf16[2304,256]{1,0:T(8,128)(2,1)}, u32[]{:S(2)}, u32[]{:S(2)}) collective-permute-start(bf16[2304,256]{1,0:T(8,128)(2,1)} %param.22), channel_id=1, source_target_pairs={{0,8},{8,0},{16,24},{24,16},{1,9},{9,1},{17,25},{25,17},{2,10},{10... | collective-permute-start | bytes 3538952 | tf_op jit(solution)/shard_map/ppermute | solution.py:70
  48.4 58.4 %collective-permute-start.7 = (bf16[256,2304]{1,0:T(8,128)(2,1)}, bf16[256,2304]{1,0:T(8,128)(2,1)}, u32[]{:S(2)}, u32[]{:S(2)}) collective-permute-start(bf16[256,2304]{1,0:T(8,128)(2,1)} %param.20), channel_id=1, source_target_pairs={{0,16},{8,24},{16,0},{24,8},{1,17},{9,25},{17,1},{25,9},{2,18},{10... | collective-permute-start | bytes 3538952 | tf_op jit(solution)/shard_map/ppermute | solution.py:70
  54.4 245.8 %all-reduce.8.cloned.1.call-start = ((), (), s32[]{:S(2)}) async-start(), calls=%async_computation.2 | async-start | bytes 2359296 | tf_op jit(solution)/shard_map/psum | solution.py:108
  57.1 61.2 %collective-permute-start.8 = (bf16[256,2304]{1,0:T(8,128)(2,1)}, bf16[256,2304]{1,0:T(8,128)(2,1)S(1)}, u32[]{:S(2)}, u32[]{:S(2)}) collective-permute-start(bf16[256,2304]{1,0:T(8,128)(2,1)} %param.20), channel_id=1, source_target_pairs={{0,8},{8,0},{16,24},{24,16},{1,9},{9,1},{17,25},{25,17},{2,10},{10... | collective-permute-start | bytes 3538952 | tf_op jit(solution)/shard_map/ppermute | solution.py:70
  82.3 37.1 %collective-permute-start.12 = (bf16[256,2304]{1,0:T(8,128)(2,1)}, bf16[256,2304]{1,0:T(8,128)(2,1)S(1)}, u32[]{:S(2)}, u32[]{:S(2)}) collective-permute-start(bf16[256,2304]{1,0:T(8,128)(2,1)} %collective-permute-done.10), channel_id=1, source_target_pairs={{0,8},{8,0},{16,24},{24,16},{1,9},{9,1},{17,25},{25,17},{2,10},{10... | collective-permute-start | bytes 3538952 | tf_op jit(solution)/shard_map/ppermute | solution.py:70
  106.7 40.0 %collective-permute-start.15 = (bf16[2304,256]{1,0:T(8,128)(2,1)}, bf16[2304,256]{1,0:T(8,128)(2,1)}, u32[]{:S(2)}, u32[]{:S(2)}) collective-permute-start(bf16[2304,256]{1,0:T(8,128)(2,1)} %collective-permute-done.13), channel_id=1, source_target_pairs={{0,8},{8,0},{16,24},{24,16},{1,9},{9,1},{17,25},{25,17},{2,10},{10... | collective-permute-start | bytes 3538952 | tf_op jit(solution)/shard_map/ppermute | solution.py:70
  112.9 36.2 %collective-permute-start.9 = (bf16[256,2304]{1,0:T(8,128)(2,1)}, bf16[256,2304]{1,0:T(8,128)(2,1)}, u32[]{:S(2)}, u32[]{:S(2)}) collective-permute-start(bf16[256,2304]{1,0:T(8,128)(2,1)} %collective-permute-done.7), channel_id=1, source_target_pairs={{0,8},{8,0},{16,24},{24,16},{1,9},{9,1},{17,25},{25,17},{2,10},{10... | collective-permute-start | bytes 3538952 | tf_op jit(solution)/shard_map/ppermute | solution.py:70
  144.9 25.1 %collective-permute-start.6 = (bf16[512,1024]{1,0:T(8,128)(2,1)S(1)}, bf16[512,1024]{1,0:T(8,128)(2,1)S(1)}, u32[]{:S(2)}, u32[]{:S(2)}) collective-permute-start(bf16[512,1024]{1,0:T(8,128)(2,1)S(1)} %convolution_convert_fusion.7), channel_id=1, source_target_pairs={{0,1},{1,0},{2,3},{3,2},{4,5},{5,4},{6,7},{7,6},{8,9},{9,8},{10,11... | collective-permute-start | bytes 3145736 | tf_op jit(solution)/shard_map/ppermute | solution.py:55
  195.9 16.8 %collective-permute-start.18 = (bf16[2304,256]{1,0:T(8,128)(2,1)S(1)}, bf16[2304,256]{1,0:T(8,128)(2,1)S(1)}, u32[]{:S(2)}, u32[]{:S(2)}) collective-permute-start(bf16[2304,256]{1,0:T(8,128)(2,1)S(1)} %convolution_convert_fusion.4), channel_id=1, source_target_pairs={{0,8},{8,0},{16,24},{24,16},{1,9},{9,1},{17,25},{25,17},{2,10},{10... | collective-permute-start | bytes 3538952 | tf_op jit(solution)/shard_map/ppermute | solution.py:94
  201.4 25.6 %collective-permute-start.16 = (bf16[512,1024]{1,0:T(8,128)(2,1)S(1)}, bf16[512,1024]{1,0:T(8,128)(2,1)S(1)}, u32[]{:S(2)}, u32[]{:S(2)}) collective-permute-start(bf16[512,1024]{1,0:T(8,128)(2,1)S(1)} %fusion.8), channel_id=1, source_target_pairs={{0,1},{1,0},{2,3},{3,2},{4,5},{5,4},{6,7},{7,6},{8,9},{9,8},{10,11... | collective-permute-start | bytes 3145736 | tf_op jit(solution)/shard_map/ppermute | solution.py:55
  210.0 17.5 %collective-permute-start.22 = (bf16[256,2304]{1,0:T(8,128)(2,1)S(1)}, bf16[256,2304]{1,0:T(8,128)(2,1)S(1)}, u32[]{:S(2)}, u32[]{:S(2)}) collective-permute-start(bf16[256,2304]{1,0:T(8,128)(2,1)S(1)} %convolution_convert_fusion.2), channel_id=1, source_target_pairs={{0,8},{8,0},{16,24},{24,16},{1,9},{9,1},{17,25},{25,17},{2,10},{10... | collective-permute-start | bytes 3538952 | tf_op jit(solution)/shard_map/ppermute | solution.py:94
  210.3 23.3 %collective-permute-start.17 = (bf16[2304,256]{1,0:T(8,128)(2,1)S(1)}, bf16[2304,256]{1,0:T(8,128)(2,1)S(1)}, u32[]{:S(2)}, u32[]{:S(2)}) collective-permute-start(bf16[2304,256]{1,0:T(8,128)(2,1)S(1)} %convolution_convert_fusion.5), channel_id=1, source_target_pairs={{0,8},{8,0},{16,24},{24,16},{1,9},{9,1},{17,25},{25,17},{2,10},{10... | collective-permute-start | bytes 3538952 | tf_op jit(solution)/shard_map/ppermute | solution.py:94
  210.6 19.3 %collective-permute-start.25 = (bf16[256,2304]{1,0:T(8,128)(2,1)S(1)}, bf16[256,2304]{1,0:T(8,128)(2,1)S(1)}, u32[]{:S(2)}, u32[]{:S(2)}) collective-permute-start(bf16[256,2304]{1,0:T(8,128)(2,1)S(1)} %convolution_convert_fusion), channel_id=1, source_target_pairs={{0,8},{8,0},{16,24},{24,16},{1,9},{9,1},{17,25},{25,17},{2,10},{10... | collective-permute-start | bytes 3538952 | tf_op jit(solution)/shard_map/ppermute | solution.py:94
  213.5 28.9 %collective-permute-start.19 = (bf16[2304,256]{1,0:T(8,128)(2,1)S(1)}, bf16[2304,256]{1,0:T(8,128)(2,1)S(1)}, u32[]{:S(2)}, u32[]{:S(2)}) collective-permute-start(bf16[2304,256]{1,0:T(8,128)(2,1)S(1)} %add_convert_fusion.5), channel_id=1, source_target_pairs={{0,16},{8,24},{16,0},{24,8},{1,17},{9,25},{17,1},{25,9},{2,18},{10... | collective-permute-start | bytes 3538952 | tf_op jit(solution)/shard_map/ppermute | solution.py:94
  227.1 21.0 %collective-permute-start.21 = (bf16[256,2304]{1,0:T(8,128)(2,1)}, bf16[256,2304]{1,0:T(8,128)(2,1)}, u32[]{:S(2)}, u32[]{:S(2)}) collective-permute-start(bf16[256,2304]{1,0:T(8,128)(2,1)} %convolution_convert_fusion.3), channel_id=1, source_target_pairs={{0,8},{8,0},{16,24},{24,16},{1,9},{9,1},{17,25},{25,17},{2,10},{10... | collective-permute-start | bytes 3538952 | tf_op jit(solution)/shard_map/ppermute | solution.py:94
  227.5 150.0 %collective-permute-start.24 = (bf16[256,2304]{1,0:T(8,128)(2,1)}, bf16[256,2304]{1,0:T(8,128)(2,1)}, u32[]{:S(2)}, u32[]{:S(2)}) collective-permute-start(bf16[256,2304]{1,0:T(8,128)(2,1)} %convolution_convert_fusion.1), channel_id=1, source_target_pairs={{0,8},{8,0},{16,24},{24,16},{1,9},{9,1},{17,25},{25,17},{2,10},{10... | collective-permute-start | bytes 3538952 | tf_op jit(solution)/shard_map/ppermute | solution.py:94
  229.9 37.8 %collective-permute-start.23 = (bf16[256,2304]{1,0:T(8,128)(2,1)}, bf16[256,2304]{1,0:T(8,128)(2,1)}, u32[]{:S(2)}, u32[]{:S(2)}) collective-permute-start(bf16[256,2304]{1,0:T(8,128)(2,1)} %add_convert_fusion.3), channel_id=1, source_target_pairs={{0,16},{8,24},{16,0},{24,8},{1,17},{9,25},{17,1},{25,9},{2,18},{10... | collective-permute-start | bytes 3538952 | tf_op jit(solution)/shard_map/ppermute | solution.py:94
  233.5 146.3 %collective-permute-start.26 = (bf16[256,2304]{1,0:T(8,128)(2,1)}, bf16[256,2304]{1,0:T(8,128)(2,1)}, u32[]{:S(2)}, u32[]{:S(2)}) collective-permute-start(bf16[256,2304]{1,0:T(8,128)(2,1)} %add_convert_fusion.1), channel_id=1, source_target_pairs={{0,16},{8,24},{16,0},{24,8},{1,17},{9,25},{17,1},{25,9},{2,18},{10... | collective-permute-start | bytes 3538952 | tf_op jit(solution)/shard_map/ppermute | solution.py:94
  243.8 114.9 %all-reduce.10.cloned.1.call-start = ((), (), s32[]{:S(2)}) async-start(), calls=%async_computation.3 | async-start | bytes 2359296 | tf_op jit(solution)/shard_map/psum | solution.py:108
  303.2 110.3 %reduce-scatter.2.cloned.1.call-start = ((), (), s32[]{:S(2)}) async-start(), calls=%async_computation.4 | async-start | bytes 2621440 | tf_op jit(solution)/shard_map/reduce_scatter | solution.py:419
  361.6 147.9 %all-reduce.12.cloned.1.call-start = ((), (), s32[]{:S(2)}) async-start(), calls=%async_computation.5 | async-start | bytes 2359296 | tf_op jit(solution)/shard_map/psum | solution.py:108
  364.5 39.2 %collective-permute-start.20 = (bf16[512,1024]{1,0:T(8,128)(2,1)}, bf16[512,1024]{1,0:T(8,128)(2,1)}, u32[]{:S(2)}, u32[]{:S(2)}) collective-permute-start(bf16[512,1024]{1,0:T(8,128)(2,1)} %convolution_convert_fusion.6), channel_id=1, source_target_pairs={{0,1},{1,0},{2,3},{3,2},{4,5},{5,4},{6,7},{7,6},{8,9},{9,8},{10,11... | collective-permute-start | bytes 3145736 | tf_op jit(solution)/shard_map/ppermute | solution.py:55
  374.9 8.2 %collective-permute-start.40 = (bf16[128,256]{1,0:T(8,128)(2,1)S(1)}, bf16[128,256]{1,0:T(8,128)(2,1)S(1)}, u32[]{:S(2)}, u32[]{:S(2)}) collective-permute-start(bf16[128,256]{1,0:T(8,128)(2,1)S(1)} %get-tuple-element.73), channel_id=1, source_target_pairs={{0,2},{2,4},{4,6},{6,0},{1,3},{3,5},{5,7},{7,1},{8,10},{10,12},{12... | collective-permute-start | bytes 196616 | tf_op jit(solution)/shard_map/ppermute | solution.py:125
  376.4 11.5 %collective-permute-start.41 = (bf16[128,256]{1,0:T(8,128)(2,1)S(1)}, bf16[128,256]{1,0:T(8,128)(2,1)S(1)}, u32[]{:S(2)}, u32[]{:S(2)}) collective-permute-start(bf16[128,256]{1,0:T(8,128)(2,1)S(1)} %get-tuple-element.75), channel_id=1, source_target_pairs={{0,4},{2,6},{4,0},{6,2},{1,5},{3,7},{5,1},{7,3},{8,12},{10,14},{12... | collective-permute-start | bytes 196616 | tf_op jit(solution)/shard_map/ppermute | solution.py:125
  377.5 10.4 %collective-permute-start.42 = (bf16[128,256]{1,0:T(8,128)(2,1)S(1)}, bf16[128,256]{1,0:T(8,128)(2,1)S(1)}, u32[]{:S(2)}, u32[]{:S(2)}) collective-permute-start(bf16[128,256]{1,0:T(8,128)(2,1)S(1)} %get-tuple-element.74), channel_id=1, source_target_pairs={{0,6},{2,0},{4,2},{6,4},{1,7},{3,1},{5,3},{7,5},{8,14},{10,8},{12,... | collective-permute-start | bytes 196616 | tf_op jit(solution)/shard_map/ppermute | solution.py:125
  387.9 10.3 %collective-permute-start.43 = (bf16[128,256]{1,0:T(8,128)(2,1)S(1)}, bf16[128,256]{1,0:T(8,128)(2,1)S(1)}, u32[]{:S(2)}, u32[]{:S(2)}) collective-permute-start(bf16[128,256]{1,0:T(8,128)(2,1)S(1)} %add_convert_fusion.11), channel_id=1, source_target_pairs={{0,2},{2,4},{4,6},{6,0},{1,3},{3,5},{5,7},{7,1},{8,10},{10,12},{12... | collective-permute-start | bytes 196616 | tf_op jit(solution)/shard_map/ppermute | solution.py:129
  392.6 11.1 %collective-permute-start.44 = (bf16[128,256]{1,0:T(8,128)(2,1)S(1)}, bf16[128,256]{1,0:T(8,128)(2,1)S(1)}, u32[]{:S(2)}, u32[]{:S(2)}) collective-permute-start(bf16[128,256]{1,0:T(8,128)(2,1)S(1)} %add_convert_fusion.11), channel_id=1, source_target_pairs={{0,4},{2,6},{4,0},{6,2},{1,5},{3,7},{5,1},{7,3},{8,12},{10,14},{12... | collective-permute-start | bytes 196616 | tf_op jit(solution)/shard_map/ppermute | solution.py:129
  394.2 9.5 %collective-permute-start.45 = (bf16[128,256]{1,0:T(8,128)(2,1)S(1)}, bf16[128,256]{1,0:T(8,128)(2,1)S(1)}, u32[]{:S(2)}, u32[]{:S(2)}) collective-permute-start(bf16[128,256]{1,0:T(8,128)(2,1)S(1)} %add_convert_fusion.11), channel_id=1, source_target_pairs={{0,6},{2,0},{4,2},{6,4},{1,7},{3,1},{5,3},{7,5},{8,14},{10,8},{12,... | collective-permute-start | bytes 196616 | tf_op jit(solution)/shard_map/ppermute | solution.py:129
  425.1 16.9 %collective-permute-start.28 = (bf16[256,1024]{1,0:T(8,128)(2,1)}, bf16[256,1024]{1,0:T(8,128)(2,1)}, u32[]{:S(2)}, u32[]{:S(2)}) collective-permute-start(bf16[256,1024]{1,0:T(8,128)(2,1)} %convolution_convert_fusion.9), channel_id=1, source_target_pairs={{0,8},{8,0},{16,24},{24,16},{1,9},{9,1},{17,25},{25,17},{2,10},{10... | collective-permute-start | bytes 1572872 | tf_op jit(solution)/shard_map/ppermute | solution.py:94
  425.6 10.9 %collective-permute-start.29 = (bf16[256,1024]{1,0:T(8,128)(2,1)S(1)}, bf16[256,1024]{1,0:T(8,128)(2,1)S(1)}, u32[]{:S(2)}, u32[]{:S(2)}) collective-permute-start(bf16[256,1024]{1,0:T(8,128)(2,1)S(1)} %convolution_convert_fusion.8), channel_id=1, source_target_pairs={{0,8},{8,0},{16,24},{24,16},{1,9},{9,1},{17,25},{25,17},{2,10},{10... | collective-permute-start | bytes 1572872 | tf_op jit(solution)/shard_map/ppermute | solution.py:94
  433.3 24.1 %collective-permute-start.27 = (bf16[512,1024]{1,0:T(8,128)(2,1)S(1)}, bf16[512,1024]{1,0:T(8,128)(2,1)S(1)}, u32[]{:S(2)}, u32[]{:S(2)}) collective-permute-start(bf16[512,1024]{1,0:T(8,128)(2,1)S(1)} %fusion.9), channel_id=1, source_target_pairs={{0,1},{1,0},{2,3},{3,2},{4,5},{5,4},{6,7},{7,6},{8,9},{9,8},{10,11... | collective-permute-start | bytes 3145736 | tf_op jit(solution)/shard_map/ppermute | solution.py:55
  437.8 12.0 %collective-permute-start.30 = (bf16[256,1024]{1,0:T(8,128)(2,1)}, bf16[256,1024]{1,0:T(8,128)(2,1)}, u32[]{:S(2)}, u32[]{:S(2)}) collective-permute-start(bf16[256,1024]{1,0:T(8,128)(2,1)} %add_convert_fusion.7), channel_id=1, source_target_pairs={{0,16},{8,24},{16,0},{24,8},{1,17},{9,25},{17,1},{25,9},{2,18},{10... | collective-permute-start | bytes 1572872 | tf_op jit(solution)/shard_map/ppermute | solution.py:94
  451.3 11.0 %collective-permute-start.31 = (bf16[64,1024]{1,0:T(8,128)(2,1)S(1)}, bf16[64,1024]{1,0:T(8,128)(2,1)S(1)}, u32[]{:S(2)}, u32[]{:S(2)}) collective-permute-start(bf16[64,1024]{1,0:T(8,128)(2,1)S(1)} %get-tuple-element.66), channel_id=1, source_target_pairs={{0,2},{2,4},{4,6},{6,0},{1,3},{3,5},{5,7},{7,1},{8,10},{10,12},{12... | collective-permute-start | bytes 393224 | tf_op jit(solution)/shard_map/ppermute | solution.py:125
  452.3 18.3 %collective-permute-start.32 = (bf16[64,1024]{1,0:T(8,128)(2,1)S(1)}, bf16[64,1024]{1,0:T(8,128)(2,1)S(1)}, u32[]{:S(2)}, u32[]{:S(2)}) collective-permute-start(bf16[64,1024]{1,0:T(8,128)(2,1)S(1)} %get-tuple-element.68), channel_id=1, source_target_pairs={{0,4},{2,6},{4,0},{6,2},{1,5},{3,7},{5,1},{7,3},{8,12},{10,14},{12... | collective-permute-start | bytes 393224 | tf_op jit(solution)/shard_map/ppermute | solution.py:125
  454.3 16.4 %collective-permute-start.33 = (bf16[64,1024]{1,0:T(8,128)(2,1)S(1)}, bf16[64,1024]{1,0:T(8,128)(2,1)S(1)}, u32[]{:S(2)}, u32[]{:S(2)}) collective-permute-start(bf16[64,1024]{1,0:T(8,128)(2,1)S(1)} %get-tuple-element.67), channel_id=1, source_target_pairs={{0,6},{2,0},{4,2},{6,4},{1,7},{3,1},{5,3},{7,5},{8,14},{10,8},{12,... | collective-permute-start | bytes 393224 | tf_op jit(solution)/shard_map/ppermute | solution.py:125
  470.7 41.8 %collective-permute-start.34 = (bf16[64,1024]{1,0:T(8,128)(2,1)S(1)}, bf16[64,1024]{1,0:T(8,128)(2,1)S(1)}, u32[]{:S(2)}, u32[]{:S(2)}) collective-permute-start(bf16[64,1024]{1,0:T(8,128)(2,1)S(1)} %add_convert_fusion.9), channel_id=1, source_target_pairs={{0,2},{2,4},{4,6},{6,0},{1,3},{3,5},{5,7},{7,1},{8,10},{10,12},{12... | collective-permute-start | bytes 393224 | tf_op jit(solution)/shard_map/ppermute | solution.py:129
  478.8 33.7 %collective-permute-start.35 = (bf16[64,1024]{1,0:T(8,128)(2,1)S(1)}, bf16[64,1024]{1,0:T(8,128)(2,1)S(1)}, u32[]{:S(2)}, u32[]{:S(2)}) collective-permute-start(bf16[64,1024]{1,0:T(8,128)(2,1)S(1)} %add_convert_fusion.9), channel_id=1, source_target_pairs={{0,4},{2,6},{4,0},{6,2},{1,5},{3,7},{5,1},{7,3},{8,12},{10,14},{12... | collective-permute-start | bytes 393224 | tf_op jit(solution)/shard_map/ppermute | solution.py:129
  480.2 32.3 %collective-permute-start.36 = (bf16[64,1024]{1,0:T(8,128)(2,1)S(1)}, bf16[64,1024]{1,0:T(8,128)(2,1)S(1)}, u32[]{:S(2)}, u32[]{:S(2)}) collective-permute-start(bf16[64,1024]{1,0:T(8,128)(2,1)S(1)} %add_convert_fusion.9), channel_id=1, source_target_pairs={{0,6},{2,0},{4,2},{6,4},{1,7},{3,1},{5,3},{7,5},{8,14},{10,8},{12,... | collective-permute-start | bytes 393224 | tf_op jit(solution)/shard_map/ppermute | solution.py:129
  (70 other events, 627.2 us)
Sparse Core Ops, SparseCore 0:
  54.6 47.4 all-gather.1
  244.0 56.2 all-reduce.7
  303.3 55.4 all-reduce.9
  361.7 51.6 reduce-scatter.1
  440.9 68.6 all-reduce.11

commit v3 on v2

--- a/solution.py
+++ b/solution.py
@@ -60,9 +60,8 @@
     return total.astype(jnp.float32)
 
 
-def gather(shard, axis):
+def fetch(shard):
     count = lax.axis_size("fsdp")
-    mine = lax.axis_index("fsdp")
     pieces = {0: shard}
     step = count // 2
     while step >= 1:
@@ -72,9 +71,15 @@
         }
         pieces.update(moved)
         step //= 2
+    return pieces
+
+
+def whole(pieces, axis):
+    mine = lax.axis_index("fsdp")
+    shard = pieces[0]
     extent = shard.shape[axis]
     reps = [1, 1]
-    reps[axis] = count
+    reps[axis] = len(pieces)
     full = jnp.tile(shard, reps)
     for p, piece in pieces.items():
         if p:
@@ -104,10 +109,6 @@
     return held[0]
 
 
-def summed(block):
-    return lax.psum(block.astype(jnp.bfloat16), "ctx").astype(jnp.float32)
-
-
 def over_ctx(block):
     count = lax.axis_size("ctx")
     place = lax.axis_index("ctx")
@@ -129,6 +130,37 @@
         piece = lax.ppermute(held, "ctx", away(shift)) if shift else held
         full = lax.dynamic_update_slice_in_dim(
             full, piece.astype(jnp.float32), ((place + count - shift) % count) * rows, 0
+        )
+    return full
+
+
+def ring_reduce(block):
+    count = lax.axis_size("ctx")
+    place = lax.axis_index("ctx")
+    rows = block.shape[0] // count
+    ring = [(i, (i + 1) % count) for i in range(count)]
+
+    def chunk(index):
+        return lax.dynamic_slice_in_dim(block, (index % count) * rows, rows, 0)
+
+    running = chunk(place)
+    for step in range(1, count):
+        arrived = lax.ppermute(running.astype(jnp.bfloat16), "ctx", ring)
+        running = arrived.astype(jnp.float32) + chunk(place + count - step)
+    return keep_low(running)
+
+
+def ring_spread(held):
+    count = lax.axis_size("ctx")
+    place = lax.axis_index("ctx")
+    rows = held.shape[0]
+    ring = [(i, (i + 1) % count) for i in range(count)]
+    full = jnp.zeros((rows * count, held.shape[1]), jnp.float32)
+    for step in range(count):
+        if step:
+            held = lax.ppermute(held, "ctx", ring)
+        full = lax.dynamic_update_slice_in_dim(
+            full, held.astype(jnp.float32), ((place + 1 + count - step) % count) * rows, 0
         )
     return full
 
@@ -326,11 +358,11 @@
     groups = k_width // HD
     heads = q_width // HD
     qkv_shard = jnp.concatenate([query_weight, key_weight, value_weight], axis=1)
-    full_qkv = gather(qkv_shard, 0)
-    full_out = gather(out_weight, 1)
-    full_gate = gather(gate_weight, 0)
-    full_up = gather(up_weight, 0)
-    full_down = gather(down_weight, 1)
+    full_qkv = whole(fetch(qkv_shard), 0)
+    full_out = whole(fetch(out_weight), 1)
+    full_gate = whole(fetch(gate_weight), 0)
+    up_pieces = fetch(up_weight)
+    down_pieces = fetch(down_weight)
 
     local_place = offset + jnp.arange(tok_rows, dtype=jnp.int32)
     seq_ends = jnp.cumsum(lengths, axis=1)
@@ -360,6 +392,11 @@
     )
     query_rows = (queries * HD ** (-0.5)).astype(jnp.bfloat16).reshape(pack_count, tok_rows, q_width)
     attended_rows, log_total = attend(start_rows, place_rows, query_rows, all_kv, groups)
+    attended_rows, up_pieces, down_pieces = lax.optimization_barrier(
+        (attended_rows, up_pieces, down_pieces)
+    )
+    full_up = whole(up_pieces, 0)
+    full_down = whole(down_pieces, 1)
     attended = attended_rows.reshape(total_rows, q_width)
     attn_part = jnp.dot(attended, full_out, preferred_element_type=jnp.float32)
     after_attn = inputs + both(attn_part)
@@ -386,7 +423,7 @@
     unused_ffn, ffn_pull = jax.vjp(rms_norm, after_attn, ffn_gain)
     grad_after_part, grad_ffn_gain = ffn_pull(grad_normed_ffn)
     grad_after_sum, held_down = lax.optimization_barrier((both(grad_after_part), held_down))
-    share_down = summed(held_down)
+    sum_down = ring_reduce(held_down)
     grad_after = cotangent.astype(jnp.float32) + grad_after_sum
     grad_after_low = grad_after.astype(jnp.bfloat16)
     ffn_part = jnp.dot(hidden, full_down, preferred_element_type=jnp.float32)
@@ -399,9 +436,6 @@
     held_up = reduce_blocks(lambda b: dot_tn(columns(normed_ffn, b, row_extent), grad_up_proj))
     held_up = held_up.astype(jnp.bfloat16)
     grad_attended = dot_nt(grad_after_low, full_out).astype(jnp.bfloat16)
-    grad_attended, held_gate = lax.optimization_barrier((grad_attended, held_gate))
-    held_gate, share_down = lax.optimization_barrier((held_gate, share_down))
-    share_gate = summed(held_gate)
     share_out = over_ctx(
         reduce_blocks(lambda b: dot_tn(attended, columns(grad_after_low, b, down_extent)))
     )
@@ -415,10 +449,13 @@
         groups,
     )
     grad_kv = jnp.concatenate([grad_k_rows, grad_v_rows], axis=-1)
-    grad_kv, share_gate = lax.optimization_barrier((grad_kv, share_gate))
     own_kv = lax.psum_scatter(grad_kv, "ctx", scatter_dimension=1, tiled=True)
-    own_kv, held_up = lax.optimization_barrier((own_kv.astype(jnp.bfloat16), held_up))
-    share_up = summed(held_up)
+    own_kv, sum_down, held_gate, held_up = lax.optimization_barrier(
+        (own_kv.astype(jnp.bfloat16), sum_down, held_gate, held_up)
+    )
+    share_down = ring_spread(sum_down)
+    share_gate = ring_spread(ring_reduce(held_gate))
+    share_up = ring_spread(ring_reduce(held_up))
     grad_keys = own_kv[..., :k_width].reshape(pack_count, tok_rows, groups, HD)
     grad_value_low = own_kv[..., k_width:].reshape(total_rows, k_width)
     grad_queries = grad_q_rows.reshape(pack_count, tok_rows, heads, HD)

time: 530 us -> 527 us (level)
  starting transfers between devices: 60.8 us -> 93.4 us
  waiting for transfers between devices: 228 us -> 207 us
  other arithmetic: 39 us -> 28 us
    ppermute x15 -> x33, waiting for transfers between devices: 53.6 us -> 135 us  [the longest x15 72 us: fetch(): lax.ppermute(piece, 'fsdp', pairs('fsdp', step))]
    psum x3 -> x0, waiting for transfers between devices: 74.1 us -> none  [summed(): return lax.psum(block.astype(jnp.bfloat16), 'ctx').astype(jnp.float32)]
    ppermute x15, waiting for transfers between devices: 41.5 us -> 9.38 us  [reduce_blocks(): lax.ppermute(block.astype(jnp.bfloat16), 'fsdp', pairs('fsdp', step))]
    ppermute x15 -> x33, starting transfers between devices: 9.17 us -> 33.2 us  [the longest x9 12.7 us: ring_reduce(): arrived = lax.ppermute(running.astype(jnp.bfloat16), 'ctx', ring)]
    ppermute x5, waiting for transfers between devices: 3.12 us -> 17.6 us  [everywhere(): values = values + lax.ppermute(values, axis, pairs(axis, step))]
    ppermute x6, starting transfers between devices: 17.9 us -> 32 us  [over_ctx(): piece = lax.ppermute(held, 'ctx', away(shift)) if shift else held]
    ppermute x6, waiting for transfers between devices: 8.38 us -> 16.4 us  [over_ctx(): piece = lax.ppermute(held, 'ctx', away(shift)) if shift else held]
    convert_element_type x3 -> x6, other arithmetic: 8.51 us -> 0.46 us  [ring_reduce(): arrived = lax.ppermute(running.astype(jnp.bfloat16), 'ctx', ring)]
  transfers between devices with their start and end apart: 56 -> 71, of which waited for: 21 -> 30; matrix products, arithmetic and copies ran while one was open for 22% -> 18% of each run, Pallas kernels for 10% -> 10%
where the time goes in v3:
time: 527 us; the launch traced here: 521 us
  waiting for transfers between devices  207 us (39%)
  starting transfers between devices  93.4 us (18%)
  matrix products  66.5 us (13%)
  local copies, waits for them, and re-layouts  54.7 us (10%)
  Pallas kernels  54.3 us (10%)
  other arithmetic  28 us (5%)
  between operations  16.4 us (3%)
    ppermute x15, waiting for transfers between devices, fetch(): lax.ppermute(piece, 'fsdp', pairs('fsdp', step))  72 us
    pallas_call x1, Pallas kernels, attend_back(): pl.pallas_call(back_kernel, grid=(packs * halves, rows // tile), in_specs...  32.3 us
    ppermute x6, starting transfers between devices, over_ctx(): piece = lax.ppermute(held, 'ctx', away(shift)) if shift else held  32 us
    ppermute x9, waiting for transfers between devices, ring_reduce(): arrived = lax.ppermute(running.astype(jnp.bfloat16), 'ctx', ring)  31.5 us
    ppermute x9, waiting for transfers between devices, ring_spread(): held = lax.ppermute(held, 'ctx', ring)  31.4 us
    dot_general x20, matrix products, dot_tn(): lax.dot_general(left, right, (((0,), (0,)), ((), ())), preferred_element_...  28.1 us
    pallas_call x1, Pallas kernels, attend(): pl.pallas_call(attend_kernel, grid=(packs * halves, rows // tile), in_spe...  22 us
    dynamic_update_slice x15, local copies, waits for them, and re-layouts, whole(): lax.dynamic_update_slice_in_dim(full, piece, (mine ^ p) * extent, axis)  19.9 us
  transfers between devices with their start and end apart: 71, of which 30 were waited for; matrix products, arithmetic and copies ran while one was open for 18% of the time, Pallas kernels for 10%

profile of v3, /device:TPU:0, one launch (start us, length us, event | category | flops | bytes accessed | tf_op | source)
XLA Modules:
  0.0 520.7 jit_solution(16996383247409671829)
XLA Ops:
  10.2 3.0 collective-permute-start
  15.4 9.7 %collective-permute-done = bf16[256,1024]{1,0:T(8,128)(2,1)S(1)} collective-permute-done((bf16[256,1024]{1,0:T(8,128)(2,1)S(1)}, bf16[256,1024]{1,0:T(8,128)(2,1)S(1)}, u32[]{:S(2)}, u32[]{:S(2)}) %collective-permute-start) | collective-permute-done | bytes 524320 | tf_op jit(solution)/shard_map/ppermute | solution.py:69
  38.7 30.7 %collective-permute-done.9 = bf16[512,256]{1,0:T(8,128)(2,1)} collective-permute-done((bf16[512,256]{1,0:T(8,128)(2,1)S(1)}, bf16[512,256]{1,0:T(8,128)(2,1)}, u32[]{:S(2)}, u32[]{:S(2)}) %collective-permute-start.9) | collective-permute-done | bytes 262176 | tf_op jit(solution)/shard_map/ppermute | solution.py:69
  81.9 3.7 tile.24
  88.0 6.7 %collective-permute-done.4 = bf16[256,2304]{1,0:T(8,128)(2,1)} collective-permute-done((bf16[256,2304]{1,0:T(8,128)(2,1)}, bf16[256,2304]{1,0:T(8,128)(2,1)}, u32[]{:S(2)}, u32[]{:S(2)}) %collective-permute-start.4) | collective-permute-done | bytes 1179680 | tf_op jit(solution)/shard_map/ppermute | solution.py:69
  94.7 24.7 %collective-permute-done.7 = bf16[2304,256]{1,0:T(8,128)(2,1)} collective-permute-done((bf16[2304,256]{1,0:T(8,128)(2,1)}, bf16[2304,256]{1,0:T(8,128)(2,1)}, u32[]{:S(2)}, u32[]{:S(2)}) %collective-permute-start.7) | collective-permute-done | bytes 1179680 | tf_op jit(solution)/shard_map/ppermute | solution.py:69
  126.4 22.0 %shard_map.237 = (bf16[1,512,512]{2,1,0:T(8,128)(2,1)S(1)}, f32[2,4,512]{2,1,0:T(4,128)S(1)}) custom-call(s32[1,1,512]{2,1,0:T(1,128)S(1)} %bitcast.102, s32[1,1,512]{2,1,0:T(1,128)S(1)} %iota_add_fusion.place_ref, bf16[1,512,512]{2,1,0:T(8,128)(2,1)S(1)} %copy.40.query_ref, bf16[1,2048,512]{2,1,0:T(8,128)(2,1)S(1)} %copy-done.2, ...), custom_call_target="tpu_custom_call" | custom-call | flops 26843545600 | bytes 2097152 | tf_op jit(solution)/shard_map/pallas_call | solution.py:285
  150.9 2.9 tile.53
  164.4 4.3 convolution_bitcast_fusion
  168.7 5.6 %collective-permute-done.12 = bf16[512,1024]{1,0:T(8,128)(2,1)S(1)} collective-permute-done((bf16[512,1024]{1,0:T(8,128)(2,1)S(1)}, bf16[512,1024]{1,0:T(8,128)(2,1)S(1)}, u32[]{:S(2)}, u32[]{:S(2)}) %collective-permute-start.12) | collective-permute-done | bytes 1048608 | tf_op jit(solution)/shard_map/ppermute | solution.py:55
  175.2 4.2 fusion.95
  179.4 8.5 %fusion.2 = (bf16[512,2304]{1,0:T(8,128)(2,1)S(1)}, bf16[512,2304]{1,0:T(8,128)(2,1)S(1)}, bf16[512,2304]{1,0:T(8,128)(2,1)S(1)}) fusion(f32[512,2304]{1,0:T(8,128)} %convolution_bitcast_fusion, f32[512,2304]{1,0:T(8,128)} %fusion.95, bf16[512,1024]{1,0:T(8,128)(2,1)S(1)} %multiply_convert_fusion.2, bf16[1024,2304]{1,0:T(8,128)(2,1)} %constant_dynamic-update-slice_fusion.6), kind=kOutput, calls=%fused_computation.4 | convolution fusion | flops 2434793472 | bytes 22282240 | tf_op jit(solution)/shard_map/dot_general | solution.py:404
  190.4 4.0 fusion.96
  199.8 5.1 multiply_reduce_fusion
  207.1 3.6 convolution_convert_fusion.6
  218.5 12.5 %collective-permute-done.16 = bf16[512,1024]{1,0:T(8,128)(2,1)S(1)} collective-permute-done((bf16[512,1024]{1,0:T(8,128)(2,1)S(1)}, bf16[512,1024]{1,0:T(8,128)(2,1)S(1)}, u32[]{:S(2)}, u32[]{:S(2)}) %collective-permute-start.16) | collective-permute-done | bytes 1048608 | tf_op jit(solution)/shard_map/ppermute | solution.py:55
  237.7 6.2 %collective-permute-done.19 = bf16[2304,256]{1,0:T(8,128)(2,1)S(1)} collective-permute-done((bf16[2304,256]{1,0:T(8,128)(2,1)S(1)}, bf16[2304,256]{1,0:T(8,128)(2,1)S(1)}, u32[]{:S(2)}, u32[]{:S(2)}) %collective-permute-start.19) | collective-permute-done | bytes 1179680 | tf_op jit(solution)/shard_map/ppermute | solution.py:99
  247.4 32.3 %shard_map.238 = (bf16[1,512,512]{2,1,0:T(8,128)(2,1)S(1)}, bf16[1,2048,256]{2,1,0:T(8,128)(2,1)S(1)}, bf16[1,2048,256]{2,1,0:T(8,128)(2,1)S(1)}) custom-call(s32[1,1,512]{2,1,0:T(1,128)S(1)} %bitcast.103, s32[1,1,512]{2,1,0:T(1,128)S(1)} %iota_add_fusion.place_ref, bf16[1,512,512]{2,1,0:T(8,128)(2,1)S(1)} %copy.40.query_ref, ...), custom_call_target="tpu_custom_call" | custom-call | flops 42949672960 | bytes 2097152 | tf_op jit(solution)/shard_map/pallas_call | solution.py:306
  292.6 3.1 add_convert_fusion
  295.7 3.1 add_convert_fusion.2
  305.6 3.1 collective-permute-done.42
  312.3 2.6 collective-permute-start.45
  314.9 7.1 %collective-permute-done.22 = bf16[576,256]{1,0:T(8,128)(2,1)S(1)} collective-permute-done((bf16[576,256]{1,0:T(8,128)(2,1)S(1)}, bf16[576,256]{1,0:T(8,128)(2,1)S(1)}, u32[]{:S(2)}, u32[]{:S(2)}) %collective-permute-start.22) | collective-permute-done | bytes 294944 | tf_op jit(solution)/shard_map/ppermute | solution.py:148
  322.1 4.7 collective-permute-start.23
  327.7 7.3 %collective-permute-start.46 = (bf16[128,256]{1,0:T(8,128)(2,1)S(1)}, bf16[128,256]{1,0:T(8,128)(2,1)S(1)}, u32[]{:S(2)}, u32[]{:S(2)}) collective-permute-start(bf16[128,256]{1,0:T(8,128)(2,1)S(1)} %add_convert_fusion.19), channel_id=1, source_target_pairs={{0,2},{2,4},{4,6},{6,0},{1,3},{3,5},{5,7},{7,1},{8,10},{10,12},{12... | collective-permute-start | bytes 196616 | tf_op jit(solution)/shard_map/ppermute | solution.py:130
  335.0 4.3 collective-permute-start.47
  339.3 6.5 %collective-permute-done.46 = bf16[128,256]{1,0:T(8,128)(2,1)S(1)} collective-permute-done((bf16[128,256]{1,0:T(8,128)(2,1)S(1)}, bf16[128,256]{1,0:T(8,128)(2,1)S(1)}, u32[]{:S(2)}, u32[]{:S(2)}) %collective-permute-start.46) | collective-permute-done | bytes 65568 | tf_op jit(solution)/shard_map/ppermute | solution.py:130
  345.9 3.8 collective-permute-done.47
  356.5 4.6 fusion.7
  367.9 3.5 collective-permute-start.61
  372.4 2.6 collective-permute-start.49
  381.9 11.7 %collective-permute-done.67 = f32[2176]{0:T(1024)S(1)} collective-permute-done((f32[2176]{0:T(1024)S(1)}, f32[2176]{0:T(1024)S(1)}, u32[]{:S(2)}, u32[]{:S(2)}) %collective-permute-start.67) | collective-permute-done | bytes 8736 | tf_op jit(solution)/shard_map/ppermute | solution.py:172
  394.4 3.8 collective-permute-done.68
  404.8 7.1 %collective-permute-done.56 = bf16[64,2304]{1,0:T(8,128)(2,1)S(1)} collective-permute-done((bf16[64,2304]{1,0:T(8,128)(2,1)S(1)}, bf16[64,2304]{1,0:T(8,128)(2,1)S(1)}, u32[]{:S(2)}, u32[]{:S(2)}) %collective-permute-start.56) | collective-permute-done | bytes 294944 | tf_op jit(solution)/shard_map/ppermute | solution.py:148
  413.1 5.0 collective-permute-done.50
  418.2 6.2 %collective-permute-done.62 = bf16[576,256]{1,0:T(8,128)(2,1)S(1)} collective-permute-done((bf16[576,256]{1,0:T(8,128)(2,1)S(1)}, bf16[576,256]{1,0:T(8,128)(2,1)S(1)}, u32[]{:S(2)}, u32[]{:S(2)}) %collective-permute-start.62) | collective-permute-done | bytes 294944 | tf_op jit(solution)/shard_map/ppermute | solution.py:161
  424.5 6.3 %collective-permute-done.57 = bf16[64,2304]{1,0:T(8,128)(2,1)S(1)} collective-permute-done((bf16[64,2304]{1,0:T(8,128)(2,1)S(1)}, bf16[64,2304]{1,0:T(8,128)(2,1)S(1)}, u32[]{:S(2)}, u32[]{:S(2)}) %collective-permute-start.57) | collective-permute-done | bytes 294944 | tf_op jit(solution)/shard_map/ppermute | solution.py:148
  431.1 6.0 %collective-permute-done.51 = bf16[64,2304]{1,0:T(8,128)(2,1)S(1)} collective-permute-done((bf16[64,2304]{1,0:T(8,128)(2,1)S(1)}, bf16[64,2304]{1,0:T(8,128)(2,1)S(1)}, u32[]{:S(2)}, u32[]{:S(2)}) %collective-permute-start.51) | collective-permute-done | bytes 294944 | tf_op jit(solution)/shard_map/ppermute | solution.py:148
  437.4 6.0 %collective-permute-done.63 = bf16[576,256]{1,0:T(8,128)(2,1)S(1)} collective-permute-done((bf16[576,256]{1,0:T(8,128)(2,1)S(1)}, bf16[576,256]{1,0:T(8,128)(2,1)S(1)}, u32[]{:S(2)}, u32[]{:S(2)}) %collective-permute-start.63) | collective-permute-done | bytes 294944 | tf_op jit(solution)/shard_map/ppermute | solution.py:161
  446.0 4.4 collective-permute-start.35
  452.4 3.9 collective-permute-done.52
  456.4 2.6 collective-permute-done.34
  459.0 5.6 %collective-permute-done.35 = bf16[64,1024]{1,0:T(8,128)(2,1)S(1)} collective-permute-done((bf16[64,1024]{1,0:T(8,128)(2,1)S(1)}, bf16[64,1024]{1,0:T(8,128)(2,1)S(1)}, u32[]{:S(2)}, u32[]{:S(2)}) %collective-permute-start.35) | collective-permute-done | bytes 131104 | tf_op jit(solution)/shard_map/ppermute | solution.py:126
  464.7 18.0 %collective-permute-start.37 = (bf16[64,1024]{1,0:T(8,128)(2,1)S(1)}, bf16[64,1024]{1,0:T(8,128)(2,1)S(1)}, u32[]{:S(2)}, u32[]{:S(2)}) collective-permute-start(bf16[64,1024]{1,0:T(8,128)(2,1)S(1)} %add_convert_fusion.17), channel_id=1, source_target_pairs={{0,2},{2,4},{4,6},{6,0},{1,3},{3,5},{5,7},{7,1},{8,10},{10,12},{12... | collective-permute-start | bytes 393224 | tf_op jit(solution)/shard_map/ppermute | solution.py:130
  486.7 4.8 collective-permute-done.38
  493.2 3.2 collective-permute-start.60
  496.7 10.2 %collective-permute-done.60 = bf16[64,2304]{1,0:T(8,128)(2,1)S(1)} collective-permute-done((bf16[64,2304]{1,0:T(8,128)(2,1)S(1)}, bf16[64,2304]{1,0:T(8,128)(2,1)S(1)}, u32[]{:S(2)}, u32[]{:S(2)}) %collective-permute-start.60) | collective-permute-done | bytes 294944 | tf_op jit(solution)/shard_map/ppermute | solution.py:161
  506.9 5.0 collective-permute-done.54
  (404 shorter events, 148.1 us)
Async XLA Ops:
  7.2 117.6 %all-gather.2.cloned.1.call-start = ((), (), s32[]{:S(2)}) async-start(), calls=%async_computation.1 | async-start | bytes 2621440 | tf_op jit(solution)/shard_map/all_gather | solution.py:390
  10.2 15.0 %collective-permute-start = (bf16[256,1024]{1,0:T(8,128)(2,1)S(1)}, bf16[256,1024]{1,0:T(8,128)(2,1)S(1)}, u32[]{:S(2)}, u32[]{:S(2)}) collective-permute-start(bf16[256,1024]{1,0:T(8,128)(2,1)S(1)} %constant_dynamic-update-slice_fusion.15), channel_id=1, source_target_pairs={{0,16},{8,24},{16,0},{24,8},{1,17},{9,25},{17,1},{25,9},{2,18},{10... | collective-permute-start | bytes 1572872 | tf_op jit(solution)/shard_map/ppermute | solution.py:69
  34.6 319.3 %reduce-scatter.2.cloned.1.call-start = ((), (), s32[]{:S(2)}) async-start(), calls=%async_computation.2 | async-start | bytes 2621440 | tf_op jit(solution)/shard_map/reduce_scatter | solution.py:452
  34.6 45.8 %collective-permute-start.13 = (bf16[256,2304]{1,0:T(8,128)(2,1)}, bf16[256,2304]{1,0:T(8,128)(2,1)}, u32[]{:S(2)}, u32[]{:S(2)}) collective-permute-start(bf16[256,2304]{1,0:T(8,128)(2,1)} %param.20), channel_id=1, source_target_pairs={{0,16},{8,24},{16,0},{24,8},{1,17},{9,25},{17,1},{25,9},{2,18},{10... | collective-permute-start | bytes 3538952 | tf_op jit(solution)/shard_map/ppermute | solution.py:69
  36.4 33.0 %collective-permute-start.9 = (bf16[512,256]{1,0:T(8,128)(2,1)S(1)}, bf16[512,256]{1,0:T(8,128)(2,1)}, u32[]{:S(2)}, u32[]{:S(2)}) collective-permute-start(bf16[512,256]{1,0:T(8,128)(2,1)S(1)} %copy-done.45), channel_id=1, source_target_pairs={{0,16},{8,24},{16,0},{24,8},{1,17},{9,25},{17,1},{25,9},{2,18},{10... | collective-permute-start | bytes 786440 | tf_op jit(solution)/shard_map/ppermute | solution.py:69
  36.7 34.4 %collective-permute-start.10 = (bf16[512,256]{1,0:T(8,128)(2,1)S(1)}, bf16[512,256]{1,0:T(8,128)(2,1)}, u32[]{:S(2)}, u32[]{:S(2)}) collective-permute-start(bf16[512,256]{1,0:T(8,128)(2,1)S(1)} %copy-done.45), channel_id=1, source_target_pairs={{0,8},{8,0},{16,24},{24,16},{1,9},{9,1},{17,25},{25,17},{2,10},{10... | collective-permute-start | bytes 786440 | tf_op jit(solution)/shard_map/ppermute | solution.py:69
  36.7 58.0 %collective-permute-start.4 = (bf16[256,2304]{1,0:T(8,128)(2,1)}, bf16[256,2304]{1,0:T(8,128)(2,1)}, u32[]{:S(2)}, u32[]{:S(2)}) collective-permute-start(bf16[256,2304]{1,0:T(8,128)(2,1)} %param.21), channel_id=1, source_target_pairs={{0,16},{8,24},{16,0},{24,8},{1,17},{9,25},{17,1},{25,9},{2,18},{10... | collective-permute-start | bytes 3538952 | tf_op jit(solution)/shard_map/ppermute | solution.py:69
  38.5 109.9 %collective-permute-start.3 = (bf16[256,2304]{1,0:T(8,128)(2,1)}, bf16[256,2304]{1,0:T(8,128)(2,1)}, u32[]{:S(2)}, u32[]{:S(2)}) collective-permute-start(bf16[256,2304]{1,0:T(8,128)(2,1)} %param.21), channel_id=1, source_target_pairs={{0,8},{8,0},{16,24},{24,16},{1,9},{9,1},{17,25},{25,17},{2,10},{10... | collective-permute-start | bytes 3538952 | tf_op jit(solution)/shard_map/ppermute | solution.py:69
  71.2 48.3 %collective-permute-start.14 = (bf16[256,2304]{1,0:T(8,128)(2,1)}, bf16[256,2304]{1,0:T(8,128)(2,1)}, u32[]{:S(2)}, u32[]{:S(2)}) collective-permute-start(bf16[256,2304]{1,0:T(8,128)(2,1)} %param.20), channel_id=1, source_target_pairs={{0,8},{8,0},{16,24},{24,16},{1,9},{9,1},{17,25},{25,17},{2,10},{10... | collective-permute-start | bytes 3538952 | tf_op jit(solution)/shard_map/ppermute | solution.py:69
  72.6 46.8 %collective-permute-start.7 = (bf16[2304,256]{1,0:T(8,128)(2,1)}, bf16[2304,256]{1,0:T(8,128)(2,1)}, u32[]{:S(2)}, u32[]{:S(2)}) collective-permute-start(bf16[2304,256]{1,0:T(8,128)(2,1)} %param.22), channel_id=1, source_target_pairs={{0,16},{8,24},{16,0},{24,8},{1,17},{9,25},{17,1},{25,9},{2,18},{10... | collective-permute-start | bytes 3538952 | tf_op jit(solution)/shard_map/ppermute | solution.py:69
  81.1 41.3 %collective-permute-start.15 = (bf16[256,2304]{1,0:T(8,128)(2,1)}, bf16[256,2304]{1,0:T(8,128)(2,1)}, u32[]{:S(2)}, u32[]{:S(2)}) collective-permute-start(bf16[256,2304]{1,0:T(8,128)(2,1)} %collective-permute-done.13), channel_id=1, source_target_pairs={{0,8},{8,0},{16,24},{24,16},{1,9},{9,1},{17,25},{25,17},{2,10},{10... | collective-permute-start | bytes 3538952 | tf_op jit(solution)/shard_map/ppermute | solution.py:69
  94.7 53.7 %collective-permute-start.6 = (bf16[2304,256]{1,0:T(8,128)(2,1)}, bf16[2304,256]{1,0:T(8,128)(2,1)}, u32[]{:S(2)}, u32[]{:S(2)}) collective-permute-start(bf16[2304,256]{1,0:T(8,128)(2,1)} %param.22), channel_id=1, source_target_pairs={{0,8},{8,0},{16,24},{24,16},{1,9},{9,1},{17,25},{25,17},{2,10},{10... | collective-permute-start | bytes 3538952 | tf_op jit(solution)/shard_map/ppermute | solution.py:69
  119.4 29.0 %collective-permute-start.5 = (bf16[256,2304]{1,0:T(8,128)(2,1)}, bf16[256,2304]{1,0:T(8,128)(2,1)}, u32[]{:S(2)}, u32[]{:S(2)}) collective-permute-start(bf16[256,2304]{1,0:T(8,128)(2,1)} %collective-permute-done.4), channel_id=1, source_target_pairs={{0,8},{8,0},{16,24},{24,16},{1,9},{9,1},{17,25},{25,17},{2,10},{10... | collective-permute-start | bytes 3538952 | tf_op jit(solution)/shard_map/ppermute | solution.py:69
  119.4 29.0 %collective-permute-start.8 = (bf16[2304,256]{1,0:T(8,128)(2,1)}, bf16[2304,256]{1,0:T(8,128)(2,1)}, u32[]{:S(2)}, u32[]{:S(2)}) collective-permute-start(bf16[2304,256]{1,0:T(8,128)(2,1)} %collective-permute-done.7), channel_id=1, source_target_pairs={{0,8},{8,0},{16,24},{24,16},{1,9},{9,1},{17,25},{25,17},{2,10},{10... | collective-permute-start | bytes 3538952 | tf_op jit(solution)/shard_map/ppermute | solution.py:69
  149.2 25.1 %collective-permute-start.12 = (bf16[512,1024]{1,0:T(8,128)(2,1)S(1)}, bf16[512,1024]{1,0:T(8,128)(2,1)S(1)}, u32[]{:S(2)}, u32[]{:S(2)}) collective-permute-start(bf16[512,1024]{1,0:T(8,128)(2,1)S(1)} %convolution_convert_fusion.7), channel_id=1, source_target_pairs={{0,1},{1,0},{2,3},{3,2},{4,5},{5,4},{6,7},{7,6},{8,9},{9,8},{10,11... | collective-permute-start | bytes 3145736 | tf_op jit(solution)/shard_map/ppermute | solution.py:55
  197.4 16.8 %collective-permute-start.18 = (bf16[2304,256]{1,0:T(8,128)(2,1)S(1)}, bf16[2304,256]{1,0:T(8,128)(2,1)S(1)}, u32[]{:S(2)}, u32[]{:S(2)}) collective-permute-start(bf16[2304,256]{1,0:T(8,128)(2,1)S(1)} %convolution_convert_fusion.4), channel_id=1, source_target_pairs={{0,8},{8,0},{16,24},{24,16},{1,9},{9,1},{17,25},{25,17},{2,10},{10... | collective-permute-start | bytes 3538952 | tf_op jit(solution)/shard_map/ppermute | solution.py:99
  205.4 25.6 %collective-permute-start.16 = (bf16[512,1024]{1,0:T(8,128)(2,1)S(1)}, bf16[512,1024]{1,0:T(8,128)(2,1)S(1)}, u32[]{:S(2)}, u32[]{:S(2)}) collective-permute-start(bf16[512,1024]{1,0:T(8,128)(2,1)S(1)} %fusion.8), channel_id=1, source_target_pairs={{0,1},{1,0},{2,3},{3,2},{4,5},{5,4},{6,7},{7,6},{8,9},{9,8},{10,11... | collective-permute-start | bytes 3145736 | tf_op jit(solution)/shard_map/ppermute | solution.py:55
  211.6 25.9 %collective-permute-start.17 = (bf16[2304,256]{1,0:T(8,128)(2,1)S(1)}, bf16[2304,256]{1,0:T(8,128)(2,1)S(1)}, u32[]{:S(2)}, u32[]{:S(2)}) collective-permute-start(bf16[2304,256]{1,0:T(8,128)(2,1)S(1)} %convolution_convert_fusion.5), channel_id=1, source_target_pairs={{0,8},{8,0},{16,24},{24,16},{1,9},{9,1},{17,25},{25,17},{2,10},{10... | collective-permute-start | bytes 3538952 | tf_op jit(solution)/shard_map/ppermute | solution.py:99
  211.9 19.5 %collective-permute-start.28 = (bf16[256,2304]{1,0:T(8,128)(2,1)S(1)}, bf16[256,2304]{1,0:T(8,128)(2,1)S(1)}, u32[]{:S(2)}, u32[]{:S(2)}) collective-permute-start(bf16[256,2304]{1,0:T(8,128)(2,1)S(1)} %convolution_convert_fusion), channel_id=1, source_target_pairs={{0,8},{8,0},{16,24},{24,16},{1,9},{9,1},{17,25},{25,17},{2,10},{10... | collective-permute-start | bytes 3538952 | tf_op jit(solution)/shard_map/ppermute | solution.py:99
  212.2 21.7 %collective-permute-start.25 = (bf16[256,2304]{1,0:T(8,128)(2,1)S(1)}, bf16[256,2304]{1,0:T(8,128)(2,1)S(1)}, u32[]{:S(2)}, u32[]{:S(2)}) collective-permute-start(bf16[256,2304]{1,0:T(8,128)(2,1)S(1)} %convolution_convert_fusion.2), channel_id=1, source_target_pairs={{0,8},{8,0},{16,24},{24,16},{1,9},{9,1},{17,25},{25,17},{2,10},{10... | collective-permute-start | bytes 3538952 | tf_op jit(solution)/shard_map/ppermute | solution.py:99
  215.1 28.9 %collective-permute-start.19 = (bf16[2304,256]{1,0:T(8,128)(2,1)S(1)}, bf16[2304,256]{1,0:T(8,128)(2,1)S(1)}, u32[]{:S(2)}, u32[]{:S(2)}) collective-permute-start(bf16[2304,256]{1,0:T(8,128)(2,1)S(1)} %add_convert_fusion.5), channel_id=1, source_target_pairs={{0,16},{8,24},{16,0},{24,8},{1,17},{9,25},{17,1},{25,9},{2,18},{10... | collective-permute-start | bytes 3538952 | tf_op jit(solution)/shard_map/ppermute | solution.py:99
  231.0 61.0 %collective-permute-start.27 = (bf16[256,2304]{1,0:T(8,128)(2,1)}, bf16[256,2304]{1,0:T(8,128)(2,1)}, u32[]{:S(2)}, u32[]{:S(2)}) collective-permute-start(bf16[256,2304]{1,0:T(8,128)(2,1)} %convolution_convert_fusion.1), channel_id=1, source_target_pairs={{0,8},{8,0},{16,24},{24,16},{1,9},{9,1},{17,25},{25,17},{2,10},{10... | collective-permute-start | bytes 3538952 | tf_op jit(solution)/shard_map/ppermute | solution.py:99
  231.4 64.3 %collective-permute-start.24 = (bf16[256,2304]{1,0:T(8,128)(2,1)}, bf16[256,2304]{1,0:T(8,128)(2,1)}, u32[]{:S(2)}, u32[]{:S(2)}) collective-permute-start(bf16[256,2304]{1,0:T(8,128)(2,1)} %convolution_convert_fusion.3), channel_id=1, source_target_pairs={{0,8},{8,0},{16,24},{24,16},{1,9},{9,1},{17,25},{25,17},{2,10},{10... | collective-permute-start | bytes 3538952 | tf_op jit(solution)/shard_map/ppermute | solution.py:99
  233.8 58.2 %collective-permute-start.29 = (bf16[256,2304]{1,0:T(8,128)(2,1)}, bf16[256,2304]{1,0:T(8,128)(2,1)}, u32[]{:S(2)}, u32[]{:S(2)}) collective-permute-start(bf16[256,2304]{1,0:T(8,128)(2,1)} %add_convert_fusion.1), channel_id=1, source_target_pairs={{0,16},{8,24},{16,0},{24,8},{1,17},{9,25},{17,1},{25,9},{2,18},{10... | collective-permute-start | bytes 3538952 | tf_op jit(solution)/shard_map/ppermute | solution.py:99
  237.4 58.2 %collective-permute-start.26 = (bf16[256,2304]{1,0:T(8,128)(2,1)}, bf16[256,2304]{1,0:T(8,128)(2,1)}, u32[]{:S(2)}, u32[]{:S(2)}) collective-permute-start(bf16[256,2304]{1,0:T(8,128)(2,1)} %add_convert_fusion.3), channel_id=1, source_target_pairs={{0,16},{8,24},{16,0},{24,8},{1,17},{9,25},{17,1},{25,9},{2,18},{10... | collective-permute-start | bytes 3538952 | tf_op jit(solution)/shard_map/ppermute | solution.py:99
  282.6 21.3 %collective-permute-start.21 = (bf16[576,256]{1,0:T(8,128)(2,1)}, bf16[576,256]{1,0:T(8,128)(2,1)S(1)}, u32[]{:S(2)}, u32[]{:S(2)}) collective-permute-start(bf16[576,256]{1,0:T(8,128)(2,1)} %constant_dynamic-slice_fusion.2), channel_id=1, source_target_pairs={{0,2},{2,4},{4,6},{6,0},{1,3},{3,5},{5,7},{7,1},{8,10},{10,12},{12... | collective-permute-start | bytes 884744 | tf_op jit(solution)/shard_map/ppermute | solution.py:148
  303.1 47.5 %collective-permute-start.20 = (bf16[512,1024]{1,0:T(8,128)(2,1)S(1)}, bf16[512,1024]{1,0:T(8,128)(2,1)S(1)}, u32[]{:S(2)}, u32[]{:S(2)}) collective-permute-start(bf16[512,1024]{1,0:T(8,128)(2,1)S(1)} %copy-done.32), channel_id=1, source_target_pairs={{0,1},{1,0},{2,3},{3,2},{4,5},{5,4},{6,7},{7,6},{8,9},{9,8},{10,11... | collective-permute-start | bytes 3145736 | tf_op jit(solution)/shard_map/ppermute | solution.py:55
  304.0 18.0 %collective-permute-start.22 = (bf16[576,256]{1,0:T(8,128)(2,1)S(1)}, bf16[576,256]{1,0:T(8,128)(2,1)S(1)}, u32[]{:S(2)}, u32[]{:S(2)}) collective-permute-start(bf16[576,256]{1,0:T(8,128)(2,1)S(1)} %add_convert_fusion.16), channel_id=1, source_target_pairs={{0,2},{2,4},{4,6},{6,0},{1,3},{3,5},{5,7},{7,1},{8,10},{10,12},{12... | collective-permute-start | bytes 884744 | tf_op jit(solution)/shard_map/ppermute | solution.py:148
  309.1 17.6 %collective-permute-start.43 = (bf16[128,256]{1,0:T(8,128)(2,1)S(1)}, bf16[128,256]{1,0:T(8,128)(2,1)S(1)}, u32[]{:S(2)}, u32[]{:S(2)}) collective-permute-start(bf16[128,256]{1,0:T(8,128)(2,1)S(1)} %get-tuple-element.83), channel_id=1, source_target_pairs={{0,2},{2,4},{4,6},{6,0},{1,3},{3,5},{5,7},{7,1},{8,10},{10,12},{12... | collective-permute-start | bytes 196616 | tf_op jit(solution)/shard_map/ppermute | solution.py:126
  310.8 16.0 %collective-permute-start.44 = (bf16[128,256]{1,0:T(8,128)(2,1)S(1)}, bf16[128,256]{1,0:T(8,128)(2,1)S(1)}, u32[]{:S(2)}, u32[]{:S(2)}) collective-permute-start(bf16[128,256]{1,0:T(8,128)(2,1)S(1)} %get-tuple-element.85), channel_id=1, source_target_pairs={{0,4},{2,6},{4,0},{6,2},{1,5},{3,7},{5,1},{7,3},{8,12},{10,14},{12... | collective-permute-start | bytes 196616 | tf_op jit(solution)/shard_map/ppermute | solution.py:126
  312.3 15.4 %collective-permute-start.45 = (bf16[128,256]{1,0:T(8,128)(2,1)S(1)}, bf16[128,256]{1,0:T(8,128)(2,1)S(1)}, u32[]{:S(2)}, u32[]{:S(2)}) collective-permute-start(bf16[128,256]{1,0:T(8,128)(2,1)S(1)} %get-tuple-element.84), channel_id=1, source_target_pairs={{0,6},{2,0},{4,2},{6,4},{1,7},{3,1},{5,3},{7,5},{8,14},{10,8},{12,... | collective-permute-start | bytes 196616 | tf_op jit(solution)/shard_map/ppermute | solution.py:126
  322.1 27.7 %collective-permute-start.23 = (bf16[576,256]{1,0:T(8,128)(2,1)S(1)}, bf16[576,256]{1,0:T(8,128)(2,1)S(1)}, u32[]{:S(2)}, u32[]{:S(2)}) collective-permute-start(bf16[576,256]{1,0:T(8,128)(2,1)S(1)} %add_convert_fusion.15), channel_id=1, source_target_pairs={{0,2},{2,4},{4,6},{6,0},{1,3},{3,5},{5,7},{7,1},{8,10},{10,12},{12... | collective-permute-start | bytes 884744 | tf_op jit(solution)/shard_map/ppermute | solution.py:148
  327.7 18.1 %collective-permute-start.46 = (bf16[128,256]{1,0:T(8,128)(2,1)S(1)}, bf16[128,256]{1,0:T(8,128)(2,1)S(1)}, u32[]{:S(2)}, u32[]{:S(2)}) collective-permute-start(bf16[128,256]{1,0:T(8,128)(2,1)S(1)} %add_convert_fusion.19), channel_id=1, source_target_pairs={{0,2},{2,4},{4,6},{6,0},{1,3},{3,5},{5,7},{7,1},{8,10},{10,12},{12... | collective-permute-start | bytes 196616 | tf_op jit(solution)/shard_map/ppermute | solution.py:130
  335.0 14.7 %collective-permute-start.47 = (bf16[128,256]{1,0:T(8,128)(2,1)S(1)}, bf16[128,256]{1,0:T(8,128)(2,1)S(1)}, u32[]{:S(2)}, u32[]{:S(2)}) collective-permute-start(bf16[128,256]{1,0:T(8,128)(2,1)S(1)} %add_convert_fusion.19), channel_id=1, source_target_pairs={{0,4},{2,6},{4,0},{6,2},{1,5},{3,7},{5,1},{7,3},{8,12},{10,14},{12... | collective-permute-start | bytes 196616 | tf_op jit(solution)/shard_map/ppermute | solution.py:130
  367.9 32.4 %collective-permute-start.61 = (bf16[576,256]{1,0:T(8,128)(2,1)}, bf16[576,256]{1,0:T(8,128)(2,1)S(1)}, u32[]{:S(2)}, u32[]{:S(2)}) collective-permute-start(bf16[576,256]{1,0:T(8,128)(2,1)} %add_convert_fusion.14), channel_id=1, source_target_pairs={{0,2},{2,4},{4,6},{6,0},{1,3},{3,5},{5,7},{7,1},{8,10},{10,12},{12... | collective-permute-start | bytes 884744 | tf_op jit(solution)/shard_map/ppermute | solution.py:161
  371.4 28.0 %collective-permute-start.55 = (bf16[64,2304]{1,0:T(8,128)(2,1)S(1)}, bf16[64,2304]{1,0:T(8,128)(2,1)S(1)}, u32[]{:S(2)}, u32[]{:S(2)}) collective-permute-start(bf16[64,2304]{1,0:T(8,128)(2,1)S(1)} %constant_dynamic-slice_fusion), channel_id=1, source_target_pairs={{0,2},{2,4},{4,6},{6,0},{1,3},{3,5},{5,7},{7,1},{8,10},{10,12},{12... | collective-permute-start | bytes 884744 | tf_op jit(solution)/shard_map/ppermute | solution.py:148
  372.4 27.7 %collective-permute-start.49 = (bf16[64,2304]{1,0:T(8,128)(2,1)S(1)}, bf16[64,2304]{1,0:T(8,128)(2,1)S(1)}, u32[]{:S(2)}, u32[]{:S(2)}) collective-permute-start(bf16[64,2304]{1,0:T(8,128)(2,1)S(1)} %constant_dynamic-slice_fusion.1), channel_id=1, source_target_pairs={{0,2},{2,4},{4,6},{6,0},{1,3},{3,5},{5,7},{7,1},{8,10},{10,12},{12... | collective-permute-start | bytes 884744 | tf_op jit(solution)/shard_map/ppermute | solution.py:148
  375.0 70.6 %collective-permute-start.31 = (bf16[256,1024]{1,0:T(8,128)(2,1)}, bf16[256,1024]{1,0:T(8,128)(2,1)S(1)}, u32[]{:S(2)}, u32[]{:S(2)}) collective-permute-start(bf16[256,1024]{1,0:T(8,128)(2,1)} %convolution_convert_fusion.9), channel_id=1, source_target_pairs={{0,8},{8,0},{16,24},{24,16},{1,9},{9,1},{17,25},{25,17},{2,10},{10... | collective-permute-start | bytes 1572872 | tf_op jit(solution)/shard_map/ppermute | solution.py:99
  378.9 14.6 %collective-permute-start.67 = (f32[2176]{0:T(1024)S(1)}, f32[2176]{0:T(1024)S(1)}, u32[]{:S(2)}, u32[]{:S(2)}) collective-permute-start(f32[2176]{0:T(1024)S(1)} %add.552), channel_id=1, source_target_pairs={{0,2},{2,0},{4,6},{6,4},{1,3},{3,1},{5,7},{7,5},{8,10},{10,8},{12,... | collective-permute-start | bytes 26120 | tf_op jit(solution)/shard_map/ppermute | solution.py:172
  399.4 44.1 %collective-permute-start.30 = (bf16[512,1024]{1,0:T(8,128)(2,1)S(1)}, bf16[512,1024]{1,0:T(8,128)(2,1)S(1)}, u32[]{:S(2)}, u32[]{:S(2)}) collective-permute-start(bf16[512,1024]{1,0:T(8,128)(2,1)S(1)} %fusion.9), channel_id=1, source_target_pairs={{0,1},{1,0},{2,3},{3,2},{4,5},{5,4},{6,7},{7,6},{8,9},{9,8},{10,11... | collective-permute-start | bytes 3145736 | tf_op jit(solution)/shard_map/ppermute | solution.py:55
  400.3 17.9 %collective-permute-start.50 = (bf16[64,2304]{1,0:T(8,128)(2,1)S(1)}, bf16[64,2304]{1,0:T(8,128)(2,1)S(1)}, u32[]{:S(2)}, u32[]{:S(2)}) collective-permute-start(bf16[64,2304]{1,0:T(8,128)(2,1)S(1)} %add_convert_fusion.13), channel_id=1, source_target_pairs={{0,2},{2,4},{4,6},{6,0},{1,3},{3,5},{5,7},{7,1},{8,10},{10,12},{12... | collective-permute-start | bytes 884744 | tf_op jit(solution)/shard_map/ppermute | solution.py:148
  401.5 23.0 %collective-permute-start.62 = (bf16[576,256]{1,0:T(8,128)(2,1)S(1)}, bf16[576,256]{1,0:T(8,128)(2,1)S(1)}, u32[]{:S(2)}, u32[]{:S(2)}) collective-permute-start(bf16[576,256]{1,0:T(8,128)(2,1)S(1)} %collective-permute-done.61), channel_id=1, source_target_pairs={{0,2},{2,4},{4,6},{6,0},{1,3},{3,5},{5,7},{7,1},{8,10},{10,12},{12... | collective-permute-start | bytes 884744 | tf_op jit(solution)/shard_map/ppermute | solution.py:161
  411.8 33.8 %collective-permute-start.33 = (bf16[256,1024]{1,0:T(8,128)(2,1)S(1)}, bf16[256,1024]{1,0:T(8,128)(2,1)S(1)}, u32[]{:S(2)}, u32[]{:S(2)}) collective-permute-start(bf16[256,1024]{1,0:T(8,128)(2,1)S(1)} %add_convert_fusion.7), channel_id=1, source_target_pairs={{0,16},{8,24},{16,0},{24,8},{1,17},{9,25},{17,1},{25,9},{2,18},{10... | collective-permute-start | bytes 1572872 | tf_op jit(solution)/shard_map/ppermute | solution.py:99
  446.0 18.7 %collective-permute-start.35 = (bf16[64,1024]{1,0:T(8,128)(2,1)S(1)}, bf16[64,1024]{1,0:T(8,128)(2,1)S(1)}, u32[]{:S(2)}, u32[]{:S(2)}) collective-permute-start(bf16[64,1024]{1,0:T(8,128)(2,1)S(1)} %get-tuple-element.78), channel_id=1, source_target_pairs={{0,4},{2,6},{4,0},{6,2},{1,5},{3,7},{5,1},{7,3},{8,12},{10,14},{12... | collective-permute-start | bytes 393224 | tf_op jit(solution)/shard_map/ppermute | solution.py:126
  450.3 42.9 %collective-permute-start.59 = (bf16[64,2304]{1,0:T(8,128)(2,1)S(1)}, bf16[64,2304]{1,0:T(8,128)(2,1)S(1)}, u32[]{:S(2)}, u32[]{:S(2)}) collective-permute-start(bf16[64,2304]{1,0:T(8,128)(2,1)S(1)} %collective-permute-done.58), channel_id=1, source_target_pairs={{0,2},{2,4},{4,6},{6,0},{1,3},{3,5},{5,7},{7,1},{8,10},{10,12},{12... | collective-permute-start | bytes 884744 | tf_op jit(solution)/shard_map/ppermute | solution.py:161
  456.3 40.2 %collective-permute-start.53 = (bf16[64,2304]{1,0:T(8,128)(2,1)S(1)}, bf16[64,2304]{1,0:T(8,128)(2,1)S(1)}, u32[]{:S(2)}, u32[]{:S(2)}) collective-permute-start(bf16[64,2304]{1,0:T(8,128)(2,1)S(1)} %collective-permute-done.52), channel_id=1, source_target_pairs={{0,2},{2,4},{4,6},{6,0},{1,3},{3,5},{5,7},{7,1},{8,10},{10,12},{12... | collective-permute-start | bytes 884744 | tf_op jit(solution)/shard_map/ppermute | solution.py:161
  464.7 21.9 %collective-permute-start.37 = (bf16[64,1024]{1,0:T(8,128)(2,1)S(1)}, bf16[64,1024]{1,0:T(8,128)(2,1)S(1)}, u32[]{:S(2)}, u32[]{:S(2)}) collective-permute-start(bf16[64,1024]{1,0:T(8,128)(2,1)S(1)} %add_convert_fusion.17), channel_id=1, source_target_pairs={{0,2},{2,4},{4,6},{6,0},{1,3},{3,5},{5,7},{7,1},{8,10},{10,12},{12... | collective-permute-start | bytes 393224 | tf_op jit(solution)/shard_map/ppermute | solution.py:130
  496.5 15.4 %collective-permute-start.54 = (bf16[64,2304]{1,0:T(8,128)(2,1)S(1)}, bf16[64,2304]{1,0:T(8,128)(2,1)S(1)}, u32[]{:S(2)}, u32[]{:S(2)}) collective-permute-start(bf16[64,2304]{1,0:T(8,128)(2,1)S(1)} %collective-permute-done.53), channel_id=1, source_target_pairs={{0,2},{2,4},{4,6},{6,0},{1,3},{3,5},{5,7},{7,1},{8,10},{10,12},{12... | collective-permute-start | bytes 884744 | tf_op jit(solution)/shard_map/ppermute | solution.py:161
  (95 other events, 776.5 us)
Sparse Core Ops, SparseCore 0:
  34.7 47.4 all-gather.1
  289.8 63.9 reduce-scatter.1
